TPU v7x, 256 devices: a whole 4x4x8 slice. The times are simulated.
256 devices in a mesh: pair: 8 (over z_hi, core), vcol: 32 (over x, y, z_lo).
Axes of the slice: x: 4, y: 4, z: 8 (z_hi: 4, z_lo: 2; z = z_hi * 2 + z_lo), core: 2. Of those that a mesh axis runs over, the one named last changes fastest.
Arguments:
- amplitudes: bfloat16 [5120, 8192], P('pair', 'vcol'), may hold values from -6 to 6
- tile_owner: int32 [64], replicated, may hold values from 0 to 63, each once
- integrals: bfloat16 [8192, 8192], P('pair', 'vcol'), may hold values from -0.125 to 0.125
- screening: int32 [80, 64, 64], P('pair'), may hold values 0 or 1
- occ_energy: float32 [5120], P('pair'), may hold values from -1 to -0.2
- virt_energy: float32 [8192], replicated, may hold values from 0.2 to 1
Outputs:
- residual: bfloat16 [5120, 8192], P('pair', 'vcol')
Inputs may be any that keep to these rules, and one draw needn't show every extreme that they name: `tile_owner`: each of the 64 tiles appears exactly once.
All inputs are finite; a program needn't handle non-finite values. No bound on the sum of `screening` on one device may be relied on, other than what follows from the above.
Results may differ from a plain program's by a relative error of at most 0.0036.
Values may be sent and summed in bfloat16 or wider, within the bound.
No kernel may reach another device: no remote copies, remote signals or barrier semaphores. Data moves between devices by JAX's collectives and lax.ppermute only.
A program may use at most 64 MiB of HBM per device.

v0:
```python
import jax
import jax.numpy as jnp
from jax import lax
from jax.sharding import PartitionSpec as P

TILE = 128
PBLK = 64
KT_DEV = 2


def one_hot(indices, length):
    return (indices[:, None] == jnp.arange(length, dtype=jnp.int32)[None, :]).astype(jnp.float32)


def gather_rows(panel):
    return lax.all_gather(panel, "pair", axis=0, tiled=True)


def local(amplitudes, tile_owner, integrals, screening, occ_energy, virt_energy):
    pair_local = amplitudes.shape[0]
    tile_count = tile_owner.shape[0]
    width = KT_DEV * TILE
    block_count = pair_local // PBLK
    column = lax.axis_index("vcol")
    first_slot = column * KT_DEV
    owned_tiles = lax.dynamic_slice_in_dim(tile_owner, first_slot, KT_DEV, 0)
    screen_float = screening.astype(jnp.float32)
    piece_in = lax.all_gather(integrals, "vcol", axis=1, tiled=True)
    tiles_in = piece_in.shape[1] // TILE
    chooser = one_hot(owned_tiles, tiles_in).astype(jnp.bfloat16)
    shaped = piece_in.reshape(piece_in.shape[0], tiles_in, TILE)
    columns = jnp.einsum("pmk,jm->pjk", shaped, chooser, preferred_element_type=jnp.float32)
    panel = gather_rows(columns.reshape(integrals.shape[0], width).astype(jnp.bfloat16))
    picked = jnp.einsum("bct,jt->bcj", screen_float, one_hot(owned_tiles, tile_count))
    marks_slot = jnp.take(picked, tile_owner, axis=1).astype(jnp.bfloat16)
    panel_slot = jnp.take(panel.reshape(tile_count, TILE, width), tile_owner, axis=0)
    piece_in = lax.all_gather(amplitudes, "vcol", axis=1, tiled=True)
    tiles_in = piece_in.shape[1] // TILE
    left_all = piece_in.reshape(block_count, PBLK, tiles_in * TILE)

    def one_block(operands):
        left_rows, marks = operands
        masked = (
            panel_slot.reshape(tiles_in, TILE, KT_DEV, TILE) * marks[:, None, :, None]
        ).reshape(tiles_in * TILE, width)
        return jnp.dot(left_rows, masked, preferred_element_type=jnp.float32)

    summed = lax.map(one_block, (left_all, marks_slot))
    ladder_owned = summed.reshape(pair_local, width).astype(jnp.bfloat16).astype(jnp.float32)
    virt_owned = jnp.dot(
        one_hot(owned_tiles, tile_count),
        virt_energy.reshape(tile_count, TILE),
        precision=lax.Precision.HIGHEST,
    ).reshape(width)
    residual = ladder_owned + (virt_owned[None, :] - occ_energy[:, None]) * amplitudes.astype(
        jnp.float32
    )
    return residual.astype(jnp.bfloat16)


def solution(mesh):
    return jax.shard_map(
        local,
        mesh=mesh,
        in_specs=(P("pair", "vcol"), P(), P("pair", "vcol"), P("pair", None, None), P("pair"), P()),
        out_specs=P("pair", "vcol"),
        check_vma=False,
    )
```

profile of v0, /device:TPU:64, one launch (start us, length us, event | category | flops | bytes accessed | tf_op | source)
XLA Modules:
  0.0 730.7 jit_solution(13781370392742419483)
XLA Ops:
  6.5 0.7 all-gather.6.cloned.1.call-update
  7.3 0.7 dynamic_slice.11
  8.0 365.3 %all-gather.6.cloned.1.call-done = bf16[1024,8192]{1,0:T(8,128)(2,1)} async-done(((bf16[1024,256]{1,0:T(8,128)(2,1)}), bf16[1024,8192]{1,0:T(8,128)(2,1)}) %all-gather.6.cloned.1.call-update) | async-done | bytes 16777232 | tf_op jit(solution)/shard_map/all_gather | solution.py:28
  373.3 9.7 %copy.12 = bf16[128,8,64,128]{3,2,1,0:T(8,128)(2,1)S(1)} copy(bf16[128,8,64,128]{3,1,2,0:T(8,128)(2,1)} %bitcast.59) | data formatting | bytes 33554432
  383.0 2.5 convolution_convert_fusion
  385.5 0.9 copy.17
  388.7 51.6 %all-gather.8.cloned.1.call-done = bf16[8192,256]{1,0:T(8,128)(2,1)} async-done(((bf16[1024,256]{1,0:T(8,128)(2,1)}), bf16[8192,256]{1,0:T(8,128)(2,1)}) %all-gather.8.cloned.1.call-update) | async-done | bytes 4194320 | tf_op jit(solution)/shard_map/all_gather | solution.py:16
  440.3 5.0 gather_fusion.1
  445.2 4.6 broadcast_select_fusion
  449.8 225.2 %all-gather.4.cloned.1.call-done = bf16[640,8192]{1,0:T(8,128)(2,1)} async-done(((bf16[640,256]{1,0:T(8,128)(2,1)}), bf16[640,8192]{1,0:T(8,128)(2,1)}) %all-gather.4.cloned.1.call-update) | async-done | bytes 10485776 | tf_op jit(solution)/shard_map/all_gather | solution.py:37
  675.1 48.1 %while.10 = (s32[]{:T(128)}, bf16[10,64,256]{2,1,0:T(8,128)(2,1)S(1)}, bf16[10,64,8192]{2,1,0:T(8,128)(2,1)}, bf16[10,64,2]{1,2,0:T(2,128)(2,1)S(1)}, bf16[64,128,256]{2,1,0:T(8,128)(2,1)}, /*index=5*/s32[]{:T(128)}) while((s32[]{:T(128)}, bf16[10,64,256]{2,1,0:T(8,128)(2,1)S(1)}, bf16[10,64,8192]{2,1,0:T(8,128)(2,1)}, ...), condition=%wide.region_1.2_spmd, body=%wide.region_0.1_spmd.sunk | while | flops 270532608 | bytes 13830481 | solution.py:48
  675.3 2.5 broadcast_multiply_fusion.2
  677.8 2.0 fusion.24
  680.2 2.5 broadcast_multiply_fusion.2
  682.6 2.0 fusion.24
  685.0 2.5 broadcast_multiply_fusion.2
  687.5 2.0 fusion.24
  689.8 2.5 broadcast_multiply_fusion.2
  692.3 2.0 fusion.24
  694.6 2.5 broadcast_multiply_fusion.2
  697.1 2.0 fusion.24
  699.4 2.5 broadcast_multiply_fusion.2
  701.9 2.0 fusion.24
  704.2 2.5 broadcast_multiply_fusion.2
  706.7 2.0 fusion.24
  709.1 2.5 broadcast_multiply_fusion.2
  711.5 2.0 fusion.24
  713.9 2.5 broadcast_multiply_fusion.2
  716.4 2.0 fusion.24
  718.7 2.5 broadcast_multiply_fusion.2
  721.2 2.0 fusion.24
  723.2 1.0 fusion.5
  (65 shorter events, 4.9 us)
Async XLA Ops:
  6.5 382.0 %copy-start = (f32[8192]{0:T(1024)S(1)}, f32[8192]{0:T(1024)}, u32[]{:S(2)}) copy-start(f32[8192]{0:T(1024)} %param.13) | copy-start | bytes 98308
  6.5 366.8 %all-gather.6.cloned.1.call-start = ((), (), s32[]{:S(2)}) async-start(), calls=%async_computation.1 | async-start | bytes 17301504 | tf_op jit(solution)/shard_map/all_gather | solution.py:28
  7.3 433.0 %all-gather.8.cloned.1.call-start = ((), (), s32[]{:S(2)}) async-start(), calls=%async_computation.2 | async-start | bytes 4718592 | tf_op jit(solution)/shard_map/all_gather | solution.py:16
  383.0 4.2 copy-start.2
  383.0 4.6 copy-start.4
  386.4 288.6 %all-gather.4.cloned.1.call-start = ((), (), s32[]{:S(2)}) async-start(), calls=%async_computation | async-start | bytes 10813440 | tf_op jit(solution)/shard_map/all_gather | solution.py:37
  675.1 48.2 %copy-start.1 = (bf16[640,256]{1,0:T(8,128)(2,1)S(1)}, bf16[640,256]{1,0:T(8,128)(2,1)}, u32[]{:S(2)}) copy-start(bf16[640,256]{1,0:T(8,128)(2,1)} %param.8) | copy-start | bytes 983044
  675.1 48.2 %copy-start.3 = (f32[640]{0:T(1024)S(1)}, f32[640]{0:T(1024)}, u32[]{:S(2)}) copy-start(f32[640]{0:T(1024)} %param.12) | copy-start | bytes 7684
Sparse Core Ops, SparseCore 0:
  9.1 364.1 all-gather.5
  386.5 53.6 all-gather.7
  442.0 233.0 all-gather.3
where the time goes:
time: 733 us; the launch traced here: 731 us
  waiting for transfers between devices  643 us (88%)
  other arithmetic  30.5 us (4%)
  matrix products  23.3 us (3%)
  local copies, waits for them, and re-layouts  19.7 us (3%)
  between operations  13.2 us (2%)
    all_gather x1, waiting for transfers between devices, local(): piece_in = lax.all_gather(integrals, 'vcol', axis=1, tiled=True)  365 us
    all_gather x1, waiting for transfers between devices, local(): piece_in = lax.all_gather(amplitudes, 'vcol', axis=1, tiled=True)  225 us
    all_gather x1, waiting for transfers between devices, gather_rows(): return lax.all_gather(panel, 'pair', axis=0, tiled=True)  51.6 us
    mul x10, other arithmetic, one_block(): panel_slot.reshape(tiles_in, TILE, KT_DEV, TILE) * marks[:, None, :, None]  24.7 us
    dot_general x10, matrix products, one_block(): return jnp.dot(left_rows, masked, preferred_element_type=jnp.float32)  20.4 us
  transfers between devices with their start and end apart: 3, of which 3 were waited for; matrix products, arithmetic and copies ran while one was open for 2% of the time, Pallas kernels for 0%

commit v1 on v0

v1 whole, which is shorter than its diff:
```python
import functools

import jax
import jax.numpy as jnp
from jax import lax
from jax.experimental import pallas as pl
from jax.experimental.pallas import tpu as pltpu
from jax.sharding import Mesh
from jax.sharding import PartitionSpec as P

TILE = 128
PBLK = 64
ZH, CORE, NX, NY, ZL = 4, 2, 4, 4, 2
AXES = ("zh", "core", "x", "y", "zl")


def shift(value, axis, size, by):
    return lax.ppermute(value, axis, [((i + by) % size, i) for i in range(size)])


def reorder_kernel(owner_ref, src_ref, dst_ref):
    slots = owner_ref.shape[0]
    for s in range(slots):
        t = owner_ref[s]
        src = lax.rem(t // 2, 2) * (slots // 4) + t // 4
        both = src_ref[src]
        tile = jnp.where(lax.rem(t, 2) == 0, both[:, :TILE], both[:, TILE:])
        dst_ref[s // 4, :, (s % 4) * TILE : (s % 4 + 1) * TILE] = tile


def reorder(owner, spread):
    n, rows, width = spread.shape
    return pl.pallas_call(
        reorder_kernel,
        out_shape=jax.ShapeDtypeStruct((n // 2, rows, 2 * width), spread.dtype),
        in_specs=[
            pl.BlockSpec(memory_space=pltpu.SMEM),
            pl.BlockSpec(memory_space=pltpu.VMEM),
        ],
        out_specs=pl.BlockSpec(memory_space=pltpu.VMEM),
        compiler_params=pltpu.CompilerParams(vmem_limit_bytes=8 << 20),
        cost_estimate=pl.CostEstimate(flops=0, bytes_accessed=1 << 20, transcendentals=0),
        name="reorder",
    )(owner, spread)


def line_sources():
    first, second = [], []
    for d in (0, 1, 3):
        first.append([(0, d, e) for e in range(4)])
        second.append([(1, e, d) for e in range(4)])
    first += [[(0, 2, 0), (0, 2, 1)], [(0, 2, 2), (0, 2, 3)]]
    second += [[(1, 0, 2), (1, 1, 2)], [(1, 2, 2), (1, 3, 2)]]
    return first + second


def ladder_kernel(pos_ref, owner_ref, screen_ref, panel_ref, *refs):
    sources = line_sources()
    blocks = refs[: len(sources)]
    out_ref, held, sems = refs[len(sources) :]
    x, y, zl, target = pos_ref[0], pos_ref[1], pos_ref[2], pos_ref[3]
    rows = out_ref.shape[0]
    nb = rows // PBLK
    tiles = owner_ref.shape[0]
    column = pl.multiple_of(target * 2 * TILE, 2 * TILE)
    line = (x * NY + y) * ZL + target
    wanted = [owner_ref[2 * line + i] for i in range(2)]
    pieces = [piece for block in sources for piece in block]

    def tile_of(piece, j):
        partner, dy, dx = piece
        device = (((x + dx) & 3) * NY + ((y + dy) & 3)) * ZL + (zl ^ partner)
        return owner_ref[2 * device + j]

    def copy(k, j):
        t = tile_of(pieces[k], j)
        place = ((t // 16) * 4 + lax.rem(t // 4, 2) * 2 + lax.rem(t // 8, 2)) * 4 + lax.rem(t, 4)
        return pltpu.make_async_copy(
            panel_ref.at[place, :, pl.ds(column, 2 * TILE)],
            held.at[k, pl.ds(j * TILE, TILE), :],
            sems.at[k, j],
        )

    for k in range(len(pieces)):
        for j in range(2):
            copy(k, j).start()
    totals = [None, None]
    k = 0
    for ref, block in zip(blocks, sources):
        for n in range(len(block)):
            for j in range(2):
                copy(k + n, j).wait()
        right = held[k : k + len(block)].reshape(len(block) * 2 * TILE, 2 * TILE)
        for i in range(2):
            left = []
            for n, piece in enumerate(block):
                for j in range(2):
                    t = tile_of(piece, j)
                    strips = []
                    for b in range(nb):
                        mark = screen_ref[(b * tiles + t) * tiles + wanted[i]]
                        strip = ref[n, b * PBLK : (b + 1) * PBLK, j * TILE : (j + 1) * TILE]
                        strips.append(strip * jnp.full((PBLK, TILE), mark, jnp.float32).astype(strip.dtype))
                    left.append(jnp.concatenate(strips, axis=0))
            part = jnp.dot(
                jnp.concatenate(left, axis=1),
                right[:, i * TILE : (i + 1) * TILE],
                preferred_element_type=jnp.float32,
            )
            totals[i] = part if totals[i] is None else totals[i] + part
        k += len(block)
    for i in range(2):
        out_ref[:, i * TILE : (i + 1) * TILE] = totals[i].astype(out_ref.dtype)


def ladder(pos, owner, screen, panel, blocks):
    rows, width = blocks[0].shape[1:]
    pieces = sum(b.shape[0] for b in blocks)
    smem, vmem = (pl.BlockSpec(memory_space=m) for m in (pltpu.SMEM, pltpu.VMEM))
    return pl.pallas_call(
        ladder_kernel,
        out_shape=jax.ShapeDtypeStruct((rows, width), jnp.bfloat16),
        in_specs=[smem, smem, smem, pl.BlockSpec(memory_space=pl.ANY)] + [vmem] * len(blocks),
        out_specs=vmem,
        scratch_shapes=[
            pltpu.VMEM((pieces, 2 * TILE, width), jnp.bfloat16),
            pltpu.SemaphoreType.DMA((pieces, 2)),
        ],
        compiler_params=pltpu.CompilerParams(vmem_limit_bytes=24 << 20),
        cost_estimate=pl.CostEstimate(
            flops=2 * rows * width * pieces * width,
            bytes_accessed=(rows + width) * pieces * width * 2,
            transcendentals=0,
        ),
        name="ladder",
    )(pos, owner, screen, panel, *blocks)


def gather_amplitudes(own, other):
    blocks = []
    for mine, (a, na), (b, nb) in ((own, ("x", NX), ("y", NY)), (other, ("y", NY), ("x", NX))):
        near = [shift(mine, a, na, d) for d in (1, 2, 3)]
        blocks.append(jnp.stack([mine] + near))
    for i, (b, nb) in enumerate((("y", NY), ("x", NX))):
        ahead, behind = shift(blocks[i], b, nb, 1), shift(blocks[i], b, nb, 3)
        far = [shift(ahead[:2], b, nb, 1), shift(behind[2:], b, nb, 3)]
        blocks[i] = [blocks[i], ahead, behind] + far
    return blocks[0] + blocks[1]


def local(amplitudes, tile_owner, integrals, screening, occ_energy, virt_energy):
    pairs, width = amplitudes.shape
    half = pairs // ZL
    tiles = tile_owner.shape[0]
    x, y, zl = (lax.axis_index(a) for a in ("x", "y", "zl"))
    device = (x * NY + y) * ZL + zl
    rows = integrals.shape[0] // (NX * NY * ZL)

    mine = lax.dynamic_slice_in_dim(amplitudes, zl * half, half, 0)
    other = lax.dynamic_slice_in_dim(amplitudes, (1 - zl) * half, half, 0)
    other = shift(other, "zl", ZL, 1)

    spread = lax.all_to_all(integrals.reshape(-1, rows, width), ("zl", "x", "y"), 0, 0, tiled=True)
    slots = reorder(tile_owner, spread)
    strip = lax.all_to_all(slots, ("x", "y"), 0, 0, tiled=True)
    strip, mine, other = lax.optimization_barrier((strip, mine, other))
    panel = lax.all_gather(strip.reshape(-1, ZL * width), ("zh", "zl", "core"), axis=0, tiled=True)
    panel = panel.reshape(tiles, TILE, ZL * width)
    blocks = gather_amplitudes(mine, other)

    screen = lax.dynamic_slice_in_dim(screening, zl * (half // PBLK), half // PBLK, 0)
    screen = screen.astype(jnp.float32).reshape(-1)
    place = [jnp.stack([x, y, zl, t]).astype(jnp.int32) for t in (1 - zl, zl)]
    sent = ladder(place[0], tile_owner, screen, panel, blocks)
    got = shift(sent, "zl", ZL, 1)
    kept = ladder(place[1], tile_owner, screen, panel, blocks)

    total = jnp.concatenate(
        [jnp.where(zl == 0, kept, got), jnp.where(zl == 0, got, kept)], axis=0
    ).astype(jnp.float32)
    virt_owned = jnp.concatenate(
        [
            lax.dynamic_slice_in_dim(virt_energy, tile_owner[2 * device + i] * TILE, TILE, 0)
            for i in range(2)
        ]
    )
    residual = total + (virt_owned[None, :] - occ_energy[:, None]) * amplitudes.astype(jnp.float32)
    return residual.astype(jnp.bfloat16)


def solution(mesh):
    fine = Mesh(mesh.devices.reshape(ZH, CORE, NX, NY, ZL), AXES)
    pair, vcol = ("zh", "core"), ("x", "y", "zl")
    return jax.shard_map(
        local,
        mesh=fine,
        in_specs=(P(pair, vcol), P(), P(pair, vcol), P(pair, None, None), P(pair), P()),
        out_specs=P(pair, vcol),
        check_vma=False,
    )
```

time: 733 us -> 140 us (0.19)
  waiting for transfers between devices: 643 us -> 30 us
  starting transfers between devices: 0.08 us -> 29.1 us
  other arithmetic: 30.5 us -> 3.17 us
  matrix products: 23.3 us -> 0 us
  blocking collectives: 0 us -> 20.3 us
  Pallas kernels: 0 us -> 17.8 us
    all_gather x3 -> x1, waiting for transfers between devices: 642 us -> 12.6 us  [local(): lax.all_gather(strip.reshape(-1, ZL * width), ('zh', 'zl', 'core'), axis=...]
    ppermute x0 -> x16, starting transfers between devices: none -> 25.3 us  [shift(): lax.ppermute(value, axis, [((i + by) % size, i) for i in range(size)])]
    mul x10 -> x0, other arithmetic: 24.7 us -> none  [one_block(): panel_slot.reshape(tiles_in, TILE, KT_DEV, TILE) * marks[:, None, :, None]]
    dot_general x13 -> x0, matrix products: 23.3 us -> none  [the longest x10 20.4 us: one_block(): return jnp.dot(left_rows, masked, preferred_element_type=jnp.float32)]
    all_to_all x0 -> x1, blocking collectives: none -> 20.3 us  [local(): lax.all_to_all(integrals.reshape(-1, rows, width), ('zl', 'x', 'y'), 0, 0...]
    pallas_call x0 -> x3, Pallas kernels: none -> 17.8 us  [the longest x2 15.8 us: ladder(): pl.pallas_call(ladder_kernel, out_shape=jax.ShapeDtypeStruct((rows, width...]
    ppermute x0 -> x16, waiting for transfers between devices: none -> 13.7 us  [shift(): lax.ppermute(value, axis, [((i + by) % size, i) for i in range(size)])]
    unnamed x12 -> x38, local copies, waits for them, and re-layouts: 10.6 us -> 18.9 us
  transfers between devices with their start and end apart: 3 -> 18, of which waited for: 3 -> 10; matrix products, arithmetic and copies ran while one was open for 2% -> 4% of each run, Pallas kernels for 0% -> 6%
where the time goes in v1:
time: 140 us; the launch traced here: 138 us
  waiting for transfers between devices  30 us (21%)
  starting transfers between devices  29.1 us (21%)
  local copies, waits for them, and re-layouts  23.3 us (17%)
  blocking collectives  20.3 us (14%)
  Pallas kernels  17.8 us (13%)
  between operations  14.8 us (11%)
  other arithmetic  3.17 us (2%)
    ppermute x16, starting transfers between devices, shift(): lax.ppermute(value, axis, [((i + by) % size, i) for i in range(size)])  25.3 us
    all_to_all x1, blocking collectives, local(): lax.all_to_all(integrals.reshape(-1, rows, width), ('zl', 'x', 'y'), 0, 0...  20.3 us
    unnamed x38, local copies, waits for them, and re-layouts  18.9 us
    pallas_call x2, Pallas kernels, ladder(): pl.pallas_call(ladder_kernel, out_shape=jax.ShapeDtypeStruct((rows, width...  15.8 us
    ppermute x16, waiting for transfers between devices, shift(): lax.ppermute(value, axis, [((i + by) % size, i) for i in range(size)])  13.7 us
    all_gather x1, waiting for transfers between devices, local(): lax.all_gather(strip.reshape(-1, ZL * width), ('zh', 'zl', 'core'), axis=...  12.6 us
    all_to_all x1, starting transfers between devices, local(): strip = lax.all_to_all(slots, ('x', 'y'), 0, 0, tiled=True)  3.76 us
    all_to_all x1, waiting for transfers between devices, local(): strip = lax.all_to_all(slots, ('x', 'y'), 0, 0, tiled=True)  3.61 us
  transfers between devices with their start and end apart: 18, of which 10 were waited for; matrix products, arithmetic and copies ran while one was open for 4% of the time, Pallas kernels for 6%

profile of v1, /device:TPU:64, one launch (start us, length us, event | category | flops | bytes accessed | tf_op | source)
XLA Modules:
  0.0 138.4 jit_solution(4977962990084574348)
XLA Ops:
  6.5 20.3 %all_to_all.10.src_ref = bf16[32,32,256]{2,1,0:T(8,128)(2,1)S(1)} all-to-all(bf16[32,32,256]{2,1,0:T(8,128)(2,1)} %bitcast.21), channel_id=1, replica_groups=mesh['zh'=4,'core'=2,'x'=4,'y'=4,'zl'=2] {'zl','x','y'}, dimensions={0} | all-to-all | bytes 1048576 | tf_op jit(solution)/shard_map/all_to_all | solution.py:163
  27.5 2.0 %reorder.1 = bf16[16,32,512]{2,1,0:T(8,128)(2,1)} custom-call(s32[64]{0:T(128)S(1)} %copy-done.14, bf16[32,32,256]{2,1,0:T(8,128)(2,1)S(1)} %all_to_all.10.src_ref), custom_call_target="tpu_custom_call" | custom-call | bytes 1048576 | tf_op jit(solution)/shard_map/reorder/pallas_call | solution.py:33
  29.5 3.8 %all-to-all-start.1 = ((bf16[16,32,512]{2,1,0:T(8,128)(2,1)}), bf16[16,32,512]{2,1,0:T(8,128)(2,1)S(1)}, u32[]{:S(2)}, u32[]{:S(2)}) async-start(bf16[16,32,512]{2,1,0:T(8,128)(2,1)} %reorder.1), calls=%async_computation.1 | async-start | bytes 1048576 | tf_op jit(solution)/shard_map/all_to_all | solution.py:165
  33.3 1.0 constant_dynamic-slice_fusion
  34.4 1.0 collective-permute-start
  35.4 4.4 %collective-permute-done = bf16[320,256]{1,0:T(8,128)(2,1)S(1)} collective-permute-done((bf16[320,256]{1,0:T(8,128)(2,1)S(1)}, bf16[320,256]{1,0:T(8,128)(2,1)S(1)}, u32[]{:S(2)}, u32[]{:S(2)}) %collective-permute-start) | collective-permute-done | bytes 163872 | tf_op jit(solution)/shard_map/ppermute | solution.py:18
  39.8 3.6 %all-to-all-done.1 = bf16[16,32,512]{2,1,0:T(8,128)(2,1)S(1)} async-done(((bf16[16,32,512]{2,1,0:T(8,128)(2,1)}), bf16[16,32,512]{2,1,0:T(8,128)(2,1)S(1)}, u32[]{:S(2)}, u32[]{:S(2)}) %all-to-all-start.1) | async-done | bytes 524320 | tf_op jit(solution)/shard_map/all_to_all | solution.py:165
  44.8 1.5 %collective-permute-start.9 = (bf16[320,256]{1,0:T(8,128)(2,1)S(1)}, bf16[320,256]{1,0:T(8,128)(2,1)S(1)}, u32[]{:S(2)}, u32[]{:S(2)}) collective-permute-start(bf16[320,256]{1,0:T(8,128)(2,1)S(1)} %collective-permute-done), channel_id=1, source_target_pairs={{4,0},{6,2},{0,4},{2,6},{5,1},{7,3},{1,5},{3,7},{12,8},{14,10},{8,... | collective-permute-start | bytes 491528 | tf_op jit(solution)/shard_map/ppermute | solution.py:18
  46.3 1.7 %collective-permute-start.8 = (bf16[320,256]{1,0:T(8,128)(2,1)S(1)}, bf16[320,256]{1,0:T(8,128)(2,1)S(1)}, u32[]{:S(2)}, u32[]{:S(2)}) collective-permute-start(bf16[320,256]{1,0:T(8,128)(2,1)S(1)} %collective-permute-done), channel_id=1, source_target_pairs={{2,0},{4,2},{6,4},{0,6},{3,1},{5,3},{7,5},{1,7},{10,8},{12,10},{14... | collective-permute-start | bytes 491528 | tf_op jit(solution)/shard_map/ppermute | solution.py:18
  48.3 2.5 %collective-permute-start.2 = (bf16[320,256]{1,0:T(8,128)(2,1)S(1)}, bf16[320,256]{1,0:T(8,128)(2,1)S(1)}, u32[]{:S(2)}, u32[]{:S(2)}) collective-permute-start(bf16[320,256]{1,0:T(8,128)(2,1)S(1)} %get-tuple-element.9), channel_id=1, source_target_pairs={{16,0},{24,8},{0,16},{8,24},{17,1},{25,9},{1,17},{9,25},{18,2},{26... | collective-permute-start | bytes 491528 | tf_op jit(solution)/shard_map/ppermute | solution.py:18
  50.9 1.7 %collective-permute-done.10 = bf16[320,256]{1,0:T(8,128)(2,1)S(1)} collective-permute-done((bf16[320,256]{1,0:T(8,128)(2,1)S(1)}, bf16[320,256]{1,0:T(8,128)(2,1)S(1)}, u32[]{:S(2)}, u32[]{:S(2)}) %collective-permute-start.10) | collective-permute-done | bytes 163872 | tf_op jit(solution)/shard_map/ppermute | solution.py:18
  52.6 1.1 collective-permute-start.1
  53.8 1.0 collective-permute-start.12
  54.8 2.3 %collective-permute-start.11 = (bf16[4,320,256]{2,1,0:T(8,128)(2,1)S(1)}, bf16[4,320,256]{2,1,0:T(8,128)(2,1)S(1)}, u32[]{:S(2)}, u32[]{:S(2)}) collective-permute-start(bf16[4,320,256]{2,1,0:T(8,128)(2,1)S(1)} %pad_maximum_fusion.1.refs_5_), channel_id=1, source_target_pairs={{8,0},{16,8},{24,16},{0,24},{9,1},{17,9},{25,17},{1,25},{10,2},{18... | collective-permute-start | bytes 1966088 | tf_op jit(solution)/shard_map/ppermute | solution.py:18
  57.1 2.3 %collective-permute-done.2 = bf16[320,256]{1,0:T(8,128)(2,1)S(1)} collective-permute-done((bf16[320,256]{1,0:T(8,128)(2,1)S(1)}, bf16[320,256]{1,0:T(8,128)(2,1)S(1)}, u32[]{:S(2)}, u32[]{:S(2)}) %collective-permute-start.2) | collective-permute-done | bytes 163872 | tf_op jit(solution)/shard_map/ppermute | solution.py:18
  59.4 1.3 collective-permute-done.1
  61.3 2.9 %collective-permute-start.4 = (bf16[4,320,256]{2,1,0:T(8,128)(2,1)S(1)}, bf16[4,320,256]{2,1,0:T(8,128)(2,1)}, u32[]{:S(2)}, u32[]{:S(2)}) collective-permute-start(bf16[4,320,256]{2,1,0:T(8,128)(2,1)S(1)} %pad_maximum_fusion.refs_0_), channel_id=1, source_target_pairs={{2,0},{4,2},{6,4},{0,6},{3,1},{5,3},{7,5},{1,7},{10,8},{12,10},{14... | collective-permute-start | bytes 1966088 | tf_op jit(solution)/shard_map/ppermute | solution.py:18
  64.1 1.3 fusion.1
  68.6 1.8 %collective-permute-done.12.refs_7_ = bf16[4,320,256]{2,1,0:T(8,128)(2,1)S(1)} collective-permute-done((bf16[4,320,256]{2,1,0:T(8,128)(2,1)S(1)}, bf16[4,320,256]{2,1,0:T(8,128)(2,1)S(1)}, u32[]{:S(2)}, u32[]{:S(2)}) %collective-permute-start.12) | collective-permute-done | bytes 655392 | tf_op jit(solution)/shard_map/ppermute | solution.py:18
  70.5 3.4 %collective-permute-start.13 = (bf16[2,320,256]{2,1,0:T(8,128)(2,1)S(1)}, bf16[2,320,256]{2,1,0:T(8,128)(2,1)S(1)}, u32[]{:S(2)}, u32[]{:S(2)}) collective-permute-start(bf16[2,320,256]{2,1,0:T(8,128)(2,1)S(1)} %slice.18), channel_id=1, source_target_pairs={{8,0},{16,8},{24,16},{0,24},{9,1},{17,9},{25,17},{1,25},{10,2},{18... | collective-permute-start | bytes 983048 | tf_op jit(solution)/shard_map/ppermute | solution.py:18
  74.4 1.0 slice.16
  75.4 3.1 %collective-permute-start.6 = (bf16[2,320,256]{2,1,0:T(8,128)(2,1)S(1)}, bf16[2,320,256]{2,1,0:T(8,128)(2,1)S(1)}, u32[]{:S(2)}, u32[]{:S(2)}) collective-permute-start(bf16[2,320,256]{2,1,0:T(8,128)(2,1)S(1)} %slice.16), channel_id=1, source_target_pairs={{2,0},{4,2},{6,4},{0,6},{3,1},{5,3},{7,5},{1,7},{10,8},{12,10},{14... | collective-permute-start | bytes 983048 | tf_op jit(solution)/shard_map/ppermute | solution.py:18
  80.2 2.1 %collective-permute-done.7.refs_4_ = bf16[2,320,256]{2,1,0:T(8,128)(2,1)S(1)} collective-permute-done((bf16[2,320,256]{2,1,0:T(8,128)(2,1)S(1)}, bf16[2,320,256]{2,1,0:T(8,128)(2,1)S(1)}, u32[]{:S(2)}, u32[]{:S(2)}) %collective-permute-start.7) | collective-permute-done | bytes 327712 | tf_op jit(solution)/shard_map/ppermute | solution.py:18
  83.8 12.6 %all-gather.2.cloned.1.call-done = bf16[8192,512]{1,0:T(8,128)(2,1)} async-done(((bf16[512,512]{1,0:T(8,128)(2,1)}), bf16[8192,512]{1,0:T(8,128)(2,1)}) %all-gather.2.cloned.1.call-update) | async-done | bytes 8388624 | tf_op jit(solution)/shard_map/all_gather | solution.py:167
  96.4 3.4 %copy-done = bf16[8192,512]{1,0:T(8,128)(2,1)S(1)} copy-done((bf16[8192,512]{1,0:T(8,128)(2,1)S(1)}, bf16[8192,512]{1,0:T(8,128)(2,1)}, u32[]{:S(2)}) %copy-start) | copy-done | bytes 8388632
  99.8 1.0 copy-done.3
  100.8 1.0 copy-done.6
  101.7 1.0 copy-done.9
  103.7 7.9 %ladder.3 = bf16[320,256]{1,0:T(8,128)(2,1)S(1)} custom-call(s32[4]{0:T(128)S(1)} %pad_add_fusion.2.pos_ref, s32[64]{0:T(128)S(1)} %copy-done.15, f32[20480]{0:T(1024)S(1)} %reshape.18.screen_ref, bf16[64,128,512]{2,1,0:T(8,128)(2,1)S(1)} %bitcast.17, bf16[4,320,256]{2,1,0:T(8,128)(2,1)S(1)} %pad_maximum_fusion.refs_0_, ...), custom_call_target="tpu_custom_call" | custom-call | flops 1342177280 | bytes 9437184 | tf_op jit(solution)/shard_map/ladder/pallas_call | solution.py:120
  111.6 2.8 %collective-permute-start.15 = (bf16[320,256]{1,0:T(8,128)(2,1)S(1)}, bf16[320,256]{1,0:T(8,128)(2,1)}, u32[]{:S(2)}, u32[]{:S(2)}) collective-permute-start(bf16[320,256]{1,0:T(8,128)(2,1)S(1)} %ladder.3), channel_id=1, source_target_pairs={{1,0},{0,1},{3,2},{2,3},{5,4},{4,5},{7,6},{6,7},{9,8},{8,9},{11,10... | collective-permute-start | bytes 491528 | tf_op jit(solution)/shard_map/ppermute | solution.py:18
  114.4 3.4 %copy-done.1 = bf16[8192,512]{1,0:T(8,128)(2,1)S(1)} copy-done((bf16[8192,512]{1,0:T(8,128)(2,1)S(1)}, bf16[8192,512]{1,0:T(8,128)(2,1)}, u32[]{:S(2)}) %copy-start.1) | copy-done | bytes 8388632
  121.7 7.9 %ladder.2 = bf16[320,256]{1,0:T(8,128)(2,1)S(1)} custom-call(s32[4]{0:T(128)S(1)} %get-tuple-element.11.pos_ref, s32[64]{0:T(128)S(1)} %copy-done.15, f32[20480]{0:T(1024)S(1)} %reshape.18.screen_ref, bf16[64,128,512]{2,1,0:T(8,128)(2,1)S(1)} %bitcast.18, bf16[4,320,256]{2,1,0:T(8,128)(2,1)S(1)} %pad_maximum_fusion.refs_0_, ...), custom_call_target="tpu_custom_call" | custom-call | flops 1342177280 | bytes 9437184 | tf_op jit(solution)/shard_map/ladder/pallas_call | solution.py:120
  (63 shorter events, 15.6 us)
Async XLA Ops:
  6.5 89.9 %copy-start.15 = (s32[64]{0:T(128)S(1)}, s32[64]{0:T(128)}, u32[]{:S(2)}) copy-start(s32[64]{0:T(128)} %owner_ref.5) | copy-start | bytes 772
  29.5 13.9 %all-to-all-start.1 = ((bf16[16,32,512]{2,1,0:T(8,128)(2,1)}), bf16[16,32,512]{2,1,0:T(8,128)(2,1)S(1)}, u32[]{:S(2)}, u32[]{:S(2)}) async-start(bf16[16,32,512]{2,1,0:T(8,128)(2,1)} %reorder.1), calls=%async_computation.1 | async-start | bytes 1048576 | tf_op jit(solution)/shard_map/all_to_all | solution.py:165
  33.3 63.1 %all-gather.2.cloned.1.call-start = ((), (), s32[]{:S(2)}) async-start(), calls=%async_computation.2 | async-start | bytes 8912896 | tf_op jit(solution)/shard_map/all_gather | solution.py:167
  34.4 5.4 %collective-permute-start = (bf16[320,256]{1,0:T(8,128)(2,1)S(1)}, bf16[320,256]{1,0:T(8,128)(2,1)S(1)}, u32[]{:S(2)}, u32[]{:S(2)}) collective-permute-start(bf16[320,256]{1,0:T(8,128)(2,1)S(1)} %get-tuple-element.15), channel_id=1, source_target_pairs={{1,0},{0,1},{3,2},{2,3},{5,4},{4,5},{7,6},{6,7},{9,8},{8,9},{11,10... | collective-permute-start | bytes 491528 | tf_op jit(solution)/shard_map/ppermute | solution.py:18
  43.4 0.8 copy-start.16
  44.2 8.4 %collective-permute-start.10 = (bf16[320,256]{1,0:T(8,128)(2,1)S(1)}, bf16[320,256]{1,0:T(8,128)(2,1)S(1)}, u32[]{:S(2)}, u32[]{:S(2)}) collective-permute-start(bf16[320,256]{1,0:T(8,128)(2,1)S(1)} %collective-permute-done), channel_id=1, source_target_pairs={{6,0},{0,2},{2,4},{4,6},{7,1},{1,3},{3,5},{5,7},{14,8},{8,10},{10,... | collective-permute-start | bytes 491528 | tf_op jit(solution)/shard_map/ppermute | solution.py:18
  44.8 8.8 %collective-permute-start.9 = (bf16[320,256]{1,0:T(8,128)(2,1)S(1)}, bf16[320,256]{1,0:T(8,128)(2,1)S(1)}, u32[]{:S(2)}, u32[]{:S(2)}) collective-permute-start(bf16[320,256]{1,0:T(8,128)(2,1)S(1)} %collective-permute-done), channel_id=1, source_target_pairs={{4,0},{6,2},{0,4},{2,6},{5,1},{7,3},{1,5},{3,7},{12,8},{14,10},{8,... | collective-permute-start | bytes 491528 | tf_op jit(solution)/shard_map/ppermute | solution.py:18
  46.3 7.4 %collective-permute-start.8 = (bf16[320,256]{1,0:T(8,128)(2,1)S(1)}, bf16[320,256]{1,0:T(8,128)(2,1)S(1)}, u32[]{:S(2)}, u32[]{:S(2)}) collective-permute-start(bf16[320,256]{1,0:T(8,128)(2,1)S(1)} %collective-permute-done), channel_id=1, source_target_pairs={{2,0},{4,2},{6,4},{0,6},{3,1},{5,3},{7,5},{1,7},{10,8},{12,10},{14... | collective-permute-start | bytes 491528 | tf_op jit(solution)/shard_map/ppermute | solution.py:18
  48.0 9.1 %collective-permute-start.3 = (bf16[320,256]{1,0:T(8,128)(2,1)S(1)}, bf16[320,256]{1,0:T(8,128)(2,1)S(1)}, u32[]{:S(2)}, u32[]{:S(2)}) collective-permute-start(bf16[320,256]{1,0:T(8,128)(2,1)S(1)} %get-tuple-element.9), channel_id=1, source_target_pairs={{24,0},{0,8},{8,16},{16,24},{25,1},{1,9},{9,17},{17,25},{26,2},{2,... | collective-permute-start | bytes 491528 | tf_op jit(solution)/shard_map/ppermute | solution.py:18
  48.3 11.1 %collective-permute-start.2 = (bf16[320,256]{1,0:T(8,128)(2,1)S(1)}, bf16[320,256]{1,0:T(8,128)(2,1)S(1)}, u32[]{:S(2)}, u32[]{:S(2)}) collective-permute-start(bf16[320,256]{1,0:T(8,128)(2,1)S(1)} %get-tuple-element.9), channel_id=1, source_target_pairs={{16,0},{24,8},{0,16},{8,24},{17,1},{25,9},{1,17},{9,25},{18,2},{26... | collective-permute-start | bytes 491528 | tf_op jit(solution)/shard_map/ppermute | solution.py:18
  52.6 8.2 %collective-permute-start.1 = (bf16[320,256]{1,0:T(8,128)(2,1)S(1)}, bf16[320,256]{1,0:T(8,128)(2,1)S(1)}, u32[]{:S(2)}, u32[]{:S(2)}) collective-permute-start(bf16[320,256]{1,0:T(8,128)(2,1)S(1)} %get-tuple-element.9), channel_id=1, source_target_pairs={{8,0},{16,8},{24,16},{0,24},{9,1},{17,9},{25,17},{1,25},{10,2},{18... | collective-permute-start | bytes 491528 | tf_op jit(solution)/shard_map/ppermute | solution.py:18
  53.8 16.6 %collective-permute-start.12 = (bf16[4,320,256]{2,1,0:T(8,128)(2,1)S(1)}, bf16[4,320,256]{2,1,0:T(8,128)(2,1)S(1)}, u32[]{:S(2)}, u32[]{:S(2)}) collective-permute-start(bf16[4,320,256]{2,1,0:T(8,128)(2,1)S(1)} %pad_maximum_fusion.1.refs_5_), channel_id=1, source_target_pairs={{24,0},{0,8},{8,16},{16,24},{25,1},{1,9},{9,17},{17,25},{26,2},{2,... | collective-permute-start | bytes 1966088 | tf_op jit(solution)/shard_map/ppermute | solution.py:18
  54.8 15.7 %collective-permute-start.11 = (bf16[4,320,256]{2,1,0:T(8,128)(2,1)S(1)}, bf16[4,320,256]{2,1,0:T(8,128)(2,1)S(1)}, u32[]{:S(2)}, u32[]{:S(2)}) collective-permute-start(bf16[4,320,256]{2,1,0:T(8,128)(2,1)S(1)} %pad_maximum_fusion.1.refs_5_), channel_id=1, source_target_pairs={{8,0},{16,8},{24,16},{0,24},{9,1},{17,9},{25,17},{1,25},{10,2},{18... | collective-permute-start | bytes 1966088 | tf_op jit(solution)/shard_map/ppermute | solution.py:18
  60.8 13.1 %collective-permute-start.5 = (bf16[4,320,256]{2,1,0:T(8,128)(2,1)S(1)}, bf16[4,320,256]{2,1,0:T(8,128)(2,1)S(1)}, u32[]{:S(2)}, u32[]{:S(2)}) collective-permute-start(bf16[4,320,256]{2,1,0:T(8,128)(2,1)S(1)} %pad_maximum_fusion.refs_0_), channel_id=1, source_target_pairs={{6,0},{0,2},{2,4},{4,6},{7,1},{1,3},{3,5},{5,7},{14,8},{8,10},{10,... | collective-permute-start | bytes 1966088 | tf_op jit(solution)/shard_map/ppermute | solution.py:18
  61.3 13.2 %collective-permute-start.4 = (bf16[4,320,256]{2,1,0:T(8,128)(2,1)S(1)}, bf16[4,320,256]{2,1,0:T(8,128)(2,1)}, u32[]{:S(2)}, u32[]{:S(2)}) collective-permute-start(bf16[4,320,256]{2,1,0:T(8,128)(2,1)S(1)} %pad_maximum_fusion.refs_0_), channel_id=1, source_target_pairs={{2,0},{4,2},{6,4},{0,6},{3,1},{5,3},{7,5},{1,7},{10,8},{12,10},{14... | collective-permute-start | bytes 1966088 | tf_op jit(solution)/shard_map/ppermute | solution.py:18
  70.4 8.4 %collective-permute-start.14 = (bf16[2,320,256]{2,1,0:T(8,128)(2,1)S(1)}, bf16[2,320,256]{2,1,0:T(8,128)(2,1)S(1)}, u32[]{:S(2)}, u32[]{:S(2)}) collective-permute-start(bf16[2,320,256]{2,1,0:T(8,128)(2,1)S(1)} %slice.19), channel_id=1, source_target_pairs={{24,0},{0,8},{8,16},{16,24},{25,1},{1,9},{9,17},{17,25},{26,2},{2,... | collective-permute-start | bytes 983048 | tf_op jit(solution)/shard_map/ppermute | solution.py:18
  70.5 9.0 %collective-permute-start.13 = (bf16[2,320,256]{2,1,0:T(8,128)(2,1)S(1)}, bf16[2,320,256]{2,1,0:T(8,128)(2,1)S(1)}, u32[]{:S(2)}, u32[]{:S(2)}) collective-permute-start(bf16[2,320,256]{2,1,0:T(8,128)(2,1)S(1)} %slice.18), channel_id=1, source_target_pairs={{8,0},{16,8},{24,16},{0,24},{9,1},{17,9},{25,17},{1,25},{10,2},{18... | collective-permute-start | bytes 983048 | tf_op jit(solution)/shard_map/ppermute | solution.py:18
  73.9 8.4 %collective-permute-start.7 = (bf16[2,320,256]{2,1,0:T(8,128)(2,1)S(1)}, bf16[2,320,256]{2,1,0:T(8,128)(2,1)S(1)}, u32[]{:S(2)}, u32[]{:S(2)}) collective-permute-start(bf16[2,320,256]{2,1,0:T(8,128)(2,1)S(1)} %slice.17), channel_id=1, source_target_pairs={{6,0},{0,2},{2,4},{4,6},{7,1},{1,3},{3,5},{5,7},{14,8},{8,10},{10,... | collective-permute-start | bytes 983048 | tf_op jit(solution)/shard_map/ppermute | solution.py:18
  75.4 7.7 %collective-permute-start.6 = (bf16[2,320,256]{2,1,0:T(8,128)(2,1)S(1)}, bf16[2,320,256]{2,1,0:T(8,128)(2,1)S(1)}, u32[]{:S(2)}, u32[]{:S(2)}) collective-permute-start(bf16[2,320,256]{2,1,0:T(8,128)(2,1)S(1)} %slice.16), channel_id=1, source_target_pairs={{2,0},{4,2},{6,4},{0,6},{3,1},{5,3},{7,5},{1,7},{10,8},{12,10},{14... | collective-permute-start | bytes 983048 | tf_op jit(solution)/shard_map/ppermute | solution.py:18
  96.4 3.4 %copy-start = (bf16[8192,512]{1,0:T(8,128)(2,1)S(1)}, bf16[8192,512]{1,0:T(8,128)(2,1)}, u32[]{:S(2)}) copy-start(bf16[8192,512]{1,0:T(8,128)(2,1)} %all-gather.2.cloned.1.call-done) | copy-start | bytes 25165828
  99.8 1.0 copy-start.3
  100.8 1.0 copy-start.6
  101.7 1.0 copy-start.9
  102.7 1.0 copy-start.12
  111.6 19.0 %copy-start.18 = (f32[640]{0:T(1024)S(1)}, f32[640]{0:T(1024)}, u32[]{:S(2)}) copy-start(f32[640]{0:T(1024)} %param.10) | copy-start | bytes 7684
  111.6 18.0 %collective-permute-start.15 = (bf16[320,256]{1,0:T(8,128)(2,1)S(1)}, bf16[320,256]{1,0:T(8,128)(2,1)}, u32[]{:S(2)}, u32[]{:S(2)}) collective-permute-start(bf16[320,256]{1,0:T(8,128)(2,1)S(1)} %ladder.3), channel_id=1, source_target_pairs={{1,0},{0,1},{3,2},{2,3},{5,4},{4,5},{7,6},{6,7},{9,8},{8,9},{11,10... | collective-permute-start | bytes 491528 | tf_op jit(solution)/shard_map/ppermute | solution.py:18
  114.4 3.4 %copy-start.1 = (bf16[8192,512]{1,0:T(8,128)(2,1)S(1)}, bf16[8192,512]{1,0:T(8,128)(2,1)}, u32[]{:S(2)}) copy-start(bf16[8192,512]{1,0:T(8,128)(2,1)} %all-gather.2.cloned.1.call-done) | copy-start | bytes 25165828
  117.8 1.0 copy-start.4
  118.8 1.0 copy-start.7
  119.8 1.0 copy-start.10
  120.7 1.0 copy-start.13
  121.7 8.9 %copy-start.17 = (bf16[640,256]{1,0:T(8,128)(2,1)S(1)}, bf16[640,256]{1,0:T(8,128)(2,1)}, u32[]{:S(2)}) copy-start(bf16[640,256]{1,0:T(8,128)(2,1)} %param.6) | copy-start | bytes 983044
  (5 other events, 3.6 us)
Sparse Core Ops, SparseCore 0:
  44.3 52.0 all-gather.1

commit v2 on v0

v2 whole, which is shorter than its diff:
```python
import jax
import jax.numpy as jnp
from jax import lax
from jax.experimental import pallas as pl
from jax.experimental.pallas import tpu as pltpu
from jax.sharding import Mesh
from jax.sharding import PartitionSpec as P

TILE = 128
PBLK = 64
ZH, CORE, NX, NY, ZL = 4, 2, 4, 4, 2
AXES = ("zh", "core", "x", "y", "zl")
SMEM, VMEM, HBM = (
    pl.BlockSpec(memory_space=m) for m in (pltpu.SMEM, pltpu.VMEM, pltpu.HBM)
)


def shift(value, axis, size, by):
    return lax.ppermute(value, axis, [((i + by) % size, i) for i in range(size)])


def gather_amplitudes(own, other):
    blocks = []
    for mine, a, na in ((own, "x", NX), (other, "y", NY)):
        blocks.append(jnp.stack([mine] + [shift(mine, a, na, d) for d in (1, 2, 3)]))
    parts = []
    for block, b, nb in ((blocks[0], "y", NY), (blocks[1], "x", NX)):
        ahead, behind = shift(block, b, nb, 1), shift(block, b, nb, 3)
        far = [shift(ahead[:2], b, nb, 1), shift(behind[2:], b, nb, 3)]
        parts += [block, ahead, behind] + far
    order = [(0, d, e) for d in (0, 1, 3, 2) for e in range(4)]
    order += [(1, e, d) for d in (0, 1, 3, 2) for e in range(4)]
    return jnp.concatenate(parts), order


def ladder_kernel(pos_ref, place_ref, screen_ref, left_hbm, panel_ref, out_ref, left_ref, held, total, left_sem, sems):
    groups, depth, width = held.shape
    rows = left_ref.shape[1]
    tiles = place_ref.shape[0]
    line, per = pos_ref[0], depth // TILE

    def fetch(g):
        return pltpu.make_async_copy(panel_ref.at[g], held.at[g], sems.at[g])

    left_copy = pltpu.make_async_copy(left_hbm, left_ref, left_sem)
    left_copy.start()

    @pl.loop(0, groups)
    def _(g):
        fetch(g).start()

    total[...] = jnp.zeros_like(total)
    left_copy.wait()

    @pl.loop(0, groups)
    def _(g):
        fetch(g).wait()
        part = lax.rem(g // CORE, ZL)
        first = (g // (CORE * ZL) * CORE + lax.rem(g, CORE)) * per
        for j in range(width // TILE):
            wanted = (line * ZL + part) * 2 + j
            left = []
            for r in range(per):
                at = place_ref[first + r]
                column = pl.ds(pl.multiple_of(lax.rem(at, 2) * TILE, TILE), TILE)
                strips = []
                for b in range(rows // PBLK):
                    mark = screen_ref[(b * tiles + first + r) * tiles + wanted]
                    strip = left_ref[at // 2, b * PBLK : (b + 1) * PBLK, column]
                    strips.append(strip * jnp.full((PBLK, TILE), mark, jnp.float32).astype(strip.dtype))
                left.append(jnp.concatenate(strips, axis=0))
            total[part, j] += jnp.dot(
                jnp.concatenate(left, axis=1),
                held[g, :, j * TILE : (j + 1) * TILE],
                preferred_element_type=jnp.float32,
            )

    count, piece, _ = out_ref.shape
    for i in range(total.shape[0] * total.shape[1]):
        for c in range(count):
            strip = total[i // 2, i % 2, c * piece : (c + 1) * piece, :]
            out_ref[c, :, i * TILE : (i + 1) * TILE] = strip.astype(out_ref.dtype)


def ladder(pos, place, screen, left, panel):
    groups, depth, width = panel.shape
    rows = left.shape[1]
    chunks = NX * NY
    return pl.pallas_call(
        ladder_kernel,
        out_shape=jax.ShapeDtypeStruct((chunks, rows // chunks, ZL * width), jnp.bfloat16),
        in_specs=[SMEM, SMEM, SMEM, HBM, HBM],
        out_specs=VMEM,
        scratch_shapes=[
            pltpu.VMEM(left.shape, left.dtype),
            pltpu.VMEM(panel.shape, panel.dtype),
            pltpu.VMEM((ZL, width // TILE, rows, TILE), jnp.float32),
            pltpu.SemaphoreType.DMA,
            pltpu.SemaphoreType.DMA((groups,)),
        ],
        compiler_params=pltpu.CompilerParams(vmem_limit_bytes=58 << 20),
        cost_estimate=pl.CostEstimate(
            flops=2 * rows * width * groups * depth,
            bytes_accessed=(rows + width) * groups * depth * 2,
            transcendentals=0,
        ),
        name="ladder",
    )(pos, place, screen, left, panel)


def reorder_kernel(owner_ref, src_ref, dst_ref):
    for s in range(owner_ref.shape[0]):
        t = owner_ref[s]
        tile = src_ref[t // 4, :, pl.ds(pl.multiple_of(lax.rem(t, 4) * TILE, TILE), TILE)]
        device, j = s // 2, s % 2
        target = device % ZL * NX * NY + device // ZL
        dst_ref[target, :, j * TILE : (j + 1) * TILE] = tile


def reorder(owner, spread):
    n, rows, width = spread.shape
    return pl.pallas_call(
        reorder_kernel,
        out_shape=jax.ShapeDtypeStruct((n * ZL, rows, width // ZL), spread.dtype),
        in_specs=[SMEM, VMEM],
        out_specs=VMEM,
        compiler_params=pltpu.CompilerParams(vmem_limit_bytes=8 << 20),
        cost_estimate=pl.CostEstimate(flops=0, bytes_accessed=1 << 20, transcendentals=0),
        name="reorder",
    )(owner, spread)


def local(amplitudes, tile_owner, integrals, screening, occ_energy, virt_energy):
    pairs, width = amplitudes.shape
    half = pairs // ZL
    tiles = tile_owner.shape[0]
    x, y, zl = (lax.axis_index(a) for a in ("x", "y", "zl"))
    line = x * NY + y

    panel = lax.all_gather(integrals, ("zh", "zl", "core"), axis=0, tiled=False)

    mine = lax.dynamic_slice_in_dim(amplitudes, zl * half, half, 0)
    other = lax.dynamic_slice_in_dim(amplitudes, (1 - zl) * half, half, 0)
    other = shift(other, "zl", ZL, 1)
    left, order = gather_amplitudes(mine, other)

    partner, dy, dx = (jnp.array(v, jnp.int32) for v in zip(*order))
    device = (((x + dx) % NX) * NY + (y + dy) % NY) * ZL + (zl ^ partner)
    slots = (2 * device[:, None] + jnp.arange(2, dtype=jnp.int32)).reshape(-1)
    steps = jnp.arange(tiles, dtype=jnp.int32)
    held = jnp.sum(jnp.where(slots[:, None] == steps[None, :], tile_owner[None, :], 0), axis=1)
    place = jnp.sum(jnp.where(held[:, None] == steps[None, :], steps[:, None], 0), axis=0)

    screen = lax.dynamic_slice_in_dim(screening, zl * (half // PBLK), half // PBLK, 0)
    screen = screen.astype(jnp.float32).reshape(-1)
    found = ladder(jnp.stack([line]).astype(jnp.int32), place, screen, left, panel)
    spread = lax.all_to_all(found, ("x", "y"), 0, 0, tiled=True)
    sent = reorder(tile_owner, spread)
    total = lax.all_to_all(sent, ("zl", "x", "y"), 0, 0, tiled=True)
    total = total.reshape(pairs, width).astype(jnp.float32)

    own = 2 * (line * ZL + zl)
    virt_owned = jnp.concatenate(
        [lax.dynamic_slice_in_dim(virt_energy, tile_owner[own + i] * TILE, TILE, 0) for i in range(2)]
    )
    residual = total + (virt_owned[None, :] - occ_energy[:, None]) * amplitudes.astype(jnp.float32)
    return residual.astype(jnp.bfloat16)


def solution(mesh):
    fine = Mesh(mesh.devices.reshape(ZH, CORE, NX, NY, ZL), AXES)
    pair, vcol = ("zh", "core"), ("x", "y", "zl")
    return jax.shard_map(
        local,
        mesh=fine,
        in_specs=(P(pair, vcol), P(), P(pair, vcol), P(pair, None, None), P(pair), P()),
        out_specs=P(pair, vcol),
        check_vma=False,
    )
```

time: 733 us -> 130 us (0.18)
  waiting for transfers between devices: 643 us -> 39.6 us
  other arithmetic: 30.5 us -> 4.23 us
  starting transfers between devices: 0.08 us -> 26 us
  matrix products: 23.3 us -> 0 us
  Pallas kernels: 0 us -> 15.8 us
  blocking collectives: 0 us -> 12.6 us
    all_gather x3 -> x1, waiting for transfers between devices: 642 us -> 0.01 us  [local(): panel = lax.all_gather(integrals, ('zh', 'zl', 'core'), axis=0, tiled=False)]
    ppermute x0 -> x15, waiting for transfers between devices: none -> 32 us  [shift(): lax.ppermute(value, axis, [((i + by) % size, i) for i in range(size)])]
    mul x10 -> x1, other arithmetic: 24.7 us -> 0.7 us  [local(): slots = (2 * device[:, None] + jnp.arange(2, dtype=jnp.int32)).reshape(-1)]
    dot_general x13 -> x0, matrix products: 23.3 us -> none  [the longest x10 20.4 us: one_block(): return jnp.dot(left_rows, masked, preferred_element_type=jnp.float32)]
    ppermute x0 -> x15, starting transfers between devices: none -> 20.3 us  [shift(): lax.ppermute(value, axis, [((i + by) % size, i) for i in range(size)])]
    pallas_call x0 -> x2, Pallas kernels: none -> 15.8 us  [the longest x1 14.1 us: ladder(): pl.pallas_call(ladder_kernel, out_shape=jax.ShapeDtypeStruct((chunks, row...]
    all_to_all x0 -> x1, blocking collectives: none -> 12.6 us  [local(): spread = lax.all_to_all(found, ('x', 'y'), 0, 0, tiled=True)]
  transfers between devices with their start and end apart: 3 -> 17, of which waited for: 3 -> 8; matrix products, arithmetic and copies ran while one was open for 2% -> 15% of each run, Pallas kernels for 0% -> 0%
where the time goes in v2:
time: 130 us; the launch traced here: 129 us
  waiting for transfers between devices  39.6 us (30%)
  starting transfers between devices  26 us (20%)
  local copies, waits for them, and re-layouts  16.2 us (12%)
  Pallas kernels  15.8 us (12%)
  between operations  14.8 us (11%)
  blocking collectives  12.6 us (10%)
  other arithmetic  4.23 us (3%)
    ppermute x15, waiting for transfers between devices, shift(): lax.ppermute(value, axis, [((i + by) % size, i) for i in range(size)])  32 us
    ppermute x15, starting transfers between devices, shift(): lax.ppermute(value, axis, [((i + by) % size, i) for i in range(size)])  20.3 us
    pallas_call x1, Pallas kernels, ladder(): pl.pallas_call(ladder_kernel, out_shape=jax.ShapeDtypeStruct((chunks, row...  14.1 us
    all_to_all x1, blocking collectives, local(): spread = lax.all_to_all(found, ('x', 'y'), 0, 0, tiled=True)  12.6 us
    unnamed x21, local copies, waits for them, and re-layouts  12.2 us
    all_to_all x1, waiting for transfers between devices, local(): total = lax.all_to_all(sent, ('zl', 'x', 'y'), 0, 0, tiled=True)  6.9 us
    all_to_all x1, starting transfers between devices, local(): total = lax.all_to_all(sent, ('zl', 'x', 'y'), 0, 0, tiled=True)  5.68 us
  transfers between devices with their start and end apart: 17, of which 8 were waited for; matrix products, arithmetic and copies ran while one was open for 15% of the time, Pallas kernels for 0%

profile of v2, /device:TPU:64, one launch (start us, length us, event | category | flops | bytes accessed | tf_op | source)
XLA Modules:
  0.0 129.3 jit_solution(9339568432544961141)
XLA Ops:
  7.3 1.6 %constant_dynamic-update-slice_fusion.15 = (bf16[32,320,256]{2,1,0:T(8,128)(2,1)}, bf16[320,256]{1,0:T(8,128)(2,1)S(1)}) fusion(bf16[640,256]{1,0:T(8,128)(2,1)} %param.9, s32[]{:T(128)S(6)} %select_n.45), kind=kLoop, calls=%fused_computation.19 | loop fusion | bytes 491524
  8.9 2.8 %collective-permute-start = (bf16[320,256]{1,0:T(8,128)(2,1)S(1)}, bf16[320,256]{1,0:T(8,128)(2,1)S(1)}, u32[]{:S(2)}, u32[]{:S(2)}) collective-permute-start(bf16[320,256]{1,0:T(8,128)(2,1)S(1)} %get-tuple-element.6), channel_id=1, source_target_pairs={{8,0},{16,8},{24,16},{0,24},{9,1},{17,9},{25,17},{1,25},{10,2},{18... | collective-permute-start | bytes 491528 | tf_op jit(solution)/shard_map/ppermute | solution.py:19
  11.6 0.8 collective-permute-start.1
  12.4 0.9 collective-permute-start.2
  13.3 0.9 constant_dynamic-slice_fusion
  14.2 2.0 %collective-permute-start.7 = (bf16[320,256]{1,0:T(8,128)(2,1)S(1)}, bf16[320,256]{1,0:T(8,128)(2,1)S(1)}, u32[]{:S(2)}, u32[]{:S(2)}) collective-permute-start(bf16[320,256]{1,0:T(8,128)(2,1)S(1)} %constant_dynamic-slice_fusion), channel_id=1, source_target_pairs={{1,0},{0,1},{3,2},{2,3},{5,4},{4,5},{7,6},{6,7},{9,8},{8,9},{11,10... | collective-permute-start | bytes 491528 | tf_op jit(solution)/shard_map/ppermute | solution.py:19
  17.0 0.9 dynamic-slice_convert_fusion
  18.8 0.8 select_reduce_fusion.1
  20.3 2.0 %collective-permute-done.2 = bf16[320,256]{1,0:T(8,128)(2,1)S(1)} collective-permute-done((bf16[320,256]{1,0:T(8,128)(2,1)S(1)}, bf16[320,256]{1,0:T(8,128)(2,1)S(1)}, u32[]{:S(2)}, u32[]{:S(2)}) %collective-permute-start.2) | collective-permute-done | bytes 163872 | tf_op jit(solution)/shard_map/ppermute | solution.py:19
  22.4 3.1 %collective-permute-start.3 = (bf16[4,320,256]{2,1,0:T(8,128)(2,1)S(1)}, bf16[4,320,256]{2,1,0:T(8,128)(2,1)S(1)}, u32[]{:S(2)}, u32[]{:S(2)}) collective-permute-start(bf16[4,320,256]{2,1,0:T(8,128)(2,1)S(1)} %pad_maximum_fusion), channel_id=1, source_target_pairs={{2,0},{4,2},{6,4},{0,6},{3,1},{5,3},{7,5},{1,7},{10,8},{12,10},{14... | collective-permute-start | bytes 1966088 | tf_op jit(solution)/shard_map/ppermute | solution.py:19
  26.1 3.2 %collective-permute-start.8 = (bf16[320,256]{1,0:T(8,128)(2,1)S(1)}, bf16[320,256]{1,0:T(8,128)(2,1)S(1)}, u32[]{:S(2)}, u32[]{:S(2)}) collective-permute-start(bf16[320,256]{1,0:T(8,128)(2,1)S(1)} %collective-permute-done.7), channel_id=1, source_target_pairs={{2,0},{4,2},{6,4},{0,6},{3,1},{5,3},{7,5},{1,7},{10,8},{12,10},{14... | collective-permute-start | bytes 491528 | tf_op jit(solution)/shard_map/ppermute | solution.py:19
  29.3 0.9 collective-permute-start.10
  30.9 15.8 %collective-permute-done.8 = bf16[320,256]{1,0:T(8,128)(2,1)S(1)} collective-permute-done((bf16[320,256]{1,0:T(8,128)(2,1)S(1)}, bf16[320,256]{1,0:T(8,128)(2,1)S(1)}, u32[]{:S(2)}, u32[]{:S(2)}) %collective-permute-start.8) | collective-permute-done | bytes 163872 | tf_op jit(solution)/shard_map/ppermute | solution.py:19
  46.7 0.8 collective-permute-done.9
  47.5 3.2 %collective-permute-done.10 = bf16[320,256]{1,0:T(8,128)(2,1)S(1)} collective-permute-done((bf16[320,256]{1,0:T(8,128)(2,1)S(1)}, bf16[320,256]{1,0:T(8,128)(2,1)S(1)}, u32[]{:S(2)}, u32[]{:S(2)}) %collective-permute-start.10) | collective-permute-done | bytes 163872 | tf_op jit(solution)/shard_map/ppermute | solution.py:19
  50.9 2.0 %collective-permute-start.12 = (bf16[4,320,256]{2,1,0:T(8,128)(2,1)S(1)}, bf16[4,320,256]{2,1,0:T(8,128)(2,1)S(1)}, u32[]{:S(2)}, u32[]{:S(2)}) collective-permute-start(bf16[4,320,256]{2,1,0:T(8,128)(2,1)S(1)} %pad_maximum_fusion.1), channel_id=1, source_target_pairs={{24,0},{0,8},{8,16},{16,24},{25,1},{1,9},{9,17},{17,25},{26,2},{2,... | collective-permute-start | bytes 1966088 | tf_op jit(solution)/shard_map/ppermute | solution.py:19
  54.4 2.1 %collective-permute-start.6 = (bf16[2,320,256]{2,1,0:T(8,128)(2,1)S(1)}, bf16[2,320,256]{2,1,0:T(8,128)(2,1)S(1)}, u32[]{:S(2)}, u32[]{:S(2)}) collective-permute-start(bf16[2,320,256]{2,1,0:T(8,128)(2,1)S(1)} %slice.17), channel_id=1, source_target_pairs={{6,0},{0,2},{2,4},{4,6},{7,1},{1,3},{3,5},{5,7},{14,8},{8,10},{10,... | collective-permute-start | bytes 983048 | tf_op jit(solution)/shard_map/ppermute | solution.py:19
  56.5 0.9 constant_dynamic-update-slice_fusion.11
  57.4 0.9 constant_dynamic-update-slice_fusion.10
  58.3 8.1 %collective-permute-done.11 = bf16[4,320,256]{2,1,0:T(8,128)(2,1)S(1)} collective-permute-done((bf16[4,320,256]{2,1,0:T(8,128)(2,1)S(1)}, bf16[4,320,256]{2,1,0:T(8,128)(2,1)S(1)}, u32[]{:S(2)}, u32[]{:S(2)}) %collective-permute-start.11) | collective-permute-done | bytes 655392 | tf_op jit(solution)/shard_map/ppermute | solution.py:19
  66.4 1.6 %collective-permute-start.13 = (bf16[2,320,256]{2,1,0:T(8,128)(2,1)S(1)}, bf16[2,320,256]{2,1,0:T(8,128)(2,1)S(1)}, u32[]{:S(2)}, u32[]{:S(2)}) collective-permute-start(bf16[2,320,256]{2,1,0:T(8,128)(2,1)S(1)} %slice.18), channel_id=1, source_target_pairs={{8,0},{16,8},{24,16},{0,24},{9,1},{17,9},{25,17},{1,25},{10,2},{18... | collective-permute-start | bytes 983048 | tf_op jit(solution)/shard_map/ppermute | solution.py:19
  68.0 0.8 collective-permute-start.14
  73.0 0.9 constant_dynamic-update-slice_fusion.3
  73.9 0.9 constant_dynamic-update-slice_fusion.2
  75.5 1.4 %collective-permute-done.14 = bf16[2,320,256]{2,1,0:T(8,128)(2,1)S(1)} collective-permute-done((bf16[2,320,256]{2,1,0:T(8,128)(2,1)S(1)}, bf16[2,320,256]{2,1,0:T(8,128)(2,1)S(1)}, u32[]{:S(2)}, u32[]{:S(2)}) %collective-permute-start.14) | collective-permute-done | bytes 327712 | tf_op jit(solution)/shard_map/ppermute | solution.py:19
  77.7 14.1 %ladder.1 = bf16[16,20,512]{2,1,0:T(8,128)(2,1)} custom-call(s32[1]{0:T(128)} %bitcast.pos_ref, s32[64]{0:T(128)} %select_reduce_fusion.place_ref, f32[20480]{0:T(1024)} %reshape.30.screen_ref, bf16[32,320,256]{2,1,0:T(8,128)(2,1)} %constant_dynamic-update-slice_fusion.left_hbm, bf16[16,1024,256]{2,1,0:T(8,128)(2,1)} %bitcast.20), custom_call_target="tpu_custom_call" | custom-call | flops 2684354560 | bytes 18874368 | tf_op jit(solution)/shard_map/ladder/pallas_call | solution.py:89
  91.9 12.6 %all_to_all.10.src_ref = bf16[16,20,512]{2,1,0:T(8,128)(2,1)S(1)} all-to-all(bf16[16,20,512]{2,1,0:T(8,128)(2,1)} %ladder.1), channel_id=1, replica_groups=mesh['zh'=4,'core'=2,'x'=4,'y'=4,'zl'=2] {'x','y'}, dimensions={0} | all-to-all | bytes 655360 | tf_op jit(solution)/shard_map/all_to_all | solution.py:157
  104.5 1.7 %reorder.1 = bf16[32,20,256]{2,1,0:T(8,128)(2,1)} custom-call(s32[64]{0:T(128)S(1)} %copy-done, bf16[16,20,512]{2,1,0:T(8,128)(2,1)S(1)} %all_to_all.10.src_ref), custom_call_target="tpu_custom_call" | custom-call | bytes 1048576 | tf_op jit(solution)/shard_map/reorder/pallas_call | solution.py:122
  106.2 5.7 %all-to-all-start.1 = ((bf16[32,20,256]{2,1,0:T(8,128)(2,1)}), bf16[32,20,256]{2,1,0:T(8,128)(2,1)S(1)}, u32[]{:S(2)}, u32[]{:S(2)}) async-start(bf16[32,20,256]{2,1,0:T(8,128)(2,1)} %reorder.1), calls=%async_computation.1 | async-start | bytes 786432 | tf_op jit(solution)/shard_map/all_to_all | solution.py:159
  113.8 0.8 fusion.7
  114.6 6.9 %all-to-all-done.1 = bf16[32,20,256]{2,1,0:T(8,128)(2,1)S(1)} async-done(((bf16[32,20,256]{2,1,0:T(8,128)(2,1)}), bf16[32,20,256]{2,1,0:T(8,128)(2,1)S(1)}, u32[]{:S(2)}, u32[]{:S(2)}) %all-to-all-start.1) | async-done | bytes 327712 | tf_op jit(solution)/shard_map/all_to_all | solution.py:159
  121.6 0.9 add_convert_fusion
  (47 shorter events, 12.5 us)
Async XLA Ops:
  6.5 71.2 %all-gather.3.cloned.1.call-start = ((), (), s32[]{:S(2)}) async-start(), calls=%async_computation.2 | async-start | bytes 8912896 | tf_op jit(solution)/shard_map/all_gather | solution.py:140
  8.9 10.8 %collective-permute-start = (bf16[320,256]{1,0:T(8,128)(2,1)S(1)}, bf16[320,256]{1,0:T(8,128)(2,1)S(1)}, u32[]{:S(2)}, u32[]{:S(2)}) collective-permute-start(bf16[320,256]{1,0:T(8,128)(2,1)S(1)} %get-tuple-element.6), channel_id=1, source_target_pairs={{8,0},{16,8},{24,16},{0,24},{9,1},{17,9},{25,17},{1,25},{10,2},{18... | collective-permute-start | bytes 491528 | tf_op jit(solution)/shard_map/ppermute | solution.py:19
  11.6 8.7 %collective-permute-start.1 = (bf16[320,256]{1,0:T(8,128)(2,1)S(1)}, bf16[320,256]{1,0:T(8,128)(2,1)S(1)}, u32[]{:S(2)}, u32[]{:S(2)}) collective-permute-start(bf16[320,256]{1,0:T(8,128)(2,1)S(1)} %get-tuple-element.6), channel_id=1, source_target_pairs={{16,0},{24,8},{0,16},{8,24},{17,1},{25,9},{1,17},{9,25},{18,2},{26... | collective-permute-start | bytes 491528 | tf_op jit(solution)/shard_map/ppermute | solution.py:19
  12.4 9.9 %collective-permute-start.2 = (bf16[320,256]{1,0:T(8,128)(2,1)S(1)}, bf16[320,256]{1,0:T(8,128)(2,1)S(1)}, u32[]{:S(2)}, u32[]{:S(2)}) collective-permute-start(bf16[320,256]{1,0:T(8,128)(2,1)S(1)} %get-tuple-element.6), channel_id=1, source_target_pairs={{24,0},{0,8},{8,16},{16,24},{25,1},{1,9},{9,17},{17,25},{26,2},{2,... | collective-permute-start | bytes 491528 | tf_op jit(solution)/shard_map/ppermute | solution.py:19
  14.2 11.9 %collective-permute-start.7 = (bf16[320,256]{1,0:T(8,128)(2,1)S(1)}, bf16[320,256]{1,0:T(8,128)(2,1)S(1)}, u32[]{:S(2)}, u32[]{:S(2)}) collective-permute-start(bf16[320,256]{1,0:T(8,128)(2,1)S(1)} %constant_dynamic-slice_fusion), channel_id=1, source_target_pairs={{1,0},{0,1},{3,2},{2,3},{5,4},{4,5},{7,6},{6,7},{9,8},{8,9},{11,10... | collective-permute-start | bytes 491528 | tf_op jit(solution)/shard_map/ppermute | solution.py:19
  22.4 31.2 %collective-permute-start.3 = (bf16[4,320,256]{2,1,0:T(8,128)(2,1)S(1)}, bf16[4,320,256]{2,1,0:T(8,128)(2,1)S(1)}, u32[]{:S(2)}, u32[]{:S(2)}) collective-permute-start(bf16[4,320,256]{2,1,0:T(8,128)(2,1)S(1)} %pad_maximum_fusion), channel_id=1, source_target_pairs={{2,0},{4,2},{6,4},{0,6},{3,1},{5,3},{7,5},{1,7},{10,8},{12,10},{14... | collective-permute-start | bytes 1966088 | tf_op jit(solution)/shard_map/ppermute | solution.py:19
  26.1 28.3 %collective-permute-start.4 = (bf16[4,320,256]{2,1,0:T(8,128)(2,1)S(1)}, bf16[4,320,256]{2,1,0:T(8,128)(2,1)S(1)}, u32[]{:S(2)}, u32[]{:S(2)}) collective-permute-start(bf16[4,320,256]{2,1,0:T(8,128)(2,1)S(1)} %pad_maximum_fusion), channel_id=1, source_target_pairs={{6,0},{0,2},{2,4},{4,6},{7,1},{1,3},{3,5},{5,7},{14,8},{8,10},{10,... | collective-permute-start | bytes 1966088 | tf_op jit(solution)/shard_map/ppermute | solution.py:19
  26.1 20.6 %collective-permute-start.8 = (bf16[320,256]{1,0:T(8,128)(2,1)S(1)}, bf16[320,256]{1,0:T(8,128)(2,1)S(1)}, u32[]{:S(2)}, u32[]{:S(2)}) collective-permute-start(bf16[320,256]{1,0:T(8,128)(2,1)S(1)} %collective-permute-done.7), channel_id=1, source_target_pairs={{2,0},{4,2},{6,4},{0,6},{3,1},{5,3},{7,5},{1,7},{10,8},{12,10},{14... | collective-permute-start | bytes 491528 | tf_op jit(solution)/shard_map/ppermute | solution.py:19
  29.3 18.1 %collective-permute-start.9 = (bf16[320,256]{1,0:T(8,128)(2,1)S(1)}, bf16[320,256]{1,0:T(8,128)(2,1)S(1)}, u32[]{:S(2)}, u32[]{:S(2)}) collective-permute-start(bf16[320,256]{1,0:T(8,128)(2,1)S(1)} %collective-permute-done.7), channel_id=1, source_target_pairs={{4,0},{6,2},{0,4},{2,6},{5,1},{7,3},{1,5},{3,7},{12,8},{14,10},{8,... | collective-permute-start | bytes 491528 | tf_op jit(solution)/shard_map/ppermute | solution.py:19
  29.3 21.4 %collective-permute-start.10 = (bf16[320,256]{1,0:T(8,128)(2,1)S(1)}, bf16[320,256]{1,0:T(8,128)(2,1)S(1)}, u32[]{:S(2)}, u32[]{:S(2)}) collective-permute-start(bf16[320,256]{1,0:T(8,128)(2,1)S(1)} %collective-permute-done.7), channel_id=1, source_target_pairs={{6,0},{0,2},{2,4},{4,6},{7,1},{1,3},{3,5},{5,7},{14,8},{8,10},{10,... | collective-permute-start | bytes 491528 | tf_op jit(solution)/shard_map/ppermute | solution.py:19
  50.8 15.6 %collective-permute-start.11 = (bf16[4,320,256]{2,1,0:T(8,128)(2,1)S(1)}, bf16[4,320,256]{2,1,0:T(8,128)(2,1)S(1)}, u32[]{:S(2)}, u32[]{:S(2)}) collective-permute-start(bf16[4,320,256]{2,1,0:T(8,128)(2,1)S(1)} %pad_maximum_fusion.1), channel_id=1, source_target_pairs={{8,0},{16,8},{24,16},{0,24},{9,1},{17,9},{25,17},{1,25},{10,2},{18... | collective-permute-start | bytes 1966088 | tf_op jit(solution)/shard_map/ppermute | solution.py:19
  50.9 17.1 %collective-permute-start.12 = (bf16[4,320,256]{2,1,0:T(8,128)(2,1)S(1)}, bf16[4,320,256]{2,1,0:T(8,128)(2,1)S(1)}, u32[]{:S(2)}, u32[]{:S(2)}) collective-permute-start(bf16[4,320,256]{2,1,0:T(8,128)(2,1)S(1)} %pad_maximum_fusion.1), channel_id=1, source_target_pairs={{24,0},{0,8},{8,16},{16,24},{25,1},{1,9},{9,17},{17,25},{26,2},{2,... | collective-permute-start | bytes 1966088 | tf_op jit(solution)/shard_map/ppermute | solution.py:19
  53.6 15.2 %collective-permute-start.5 = (bf16[2,320,256]{2,1,0:T(8,128)(2,1)S(1)}, bf16[2,320,256]{2,1,0:T(8,128)(2,1)S(1)}, u32[]{:S(2)}, u32[]{:S(2)}) collective-permute-start(bf16[2,320,256]{2,1,0:T(8,128)(2,1)S(1)} %slice.16), channel_id=1, source_target_pairs={{2,0},{4,2},{6,4},{0,6},{3,1},{5,3},{7,5},{1,7},{10,8},{12,10},{14... | collective-permute-start | bytes 983048 | tf_op jit(solution)/shard_map/ppermute | solution.py:19
  54.4 15.1 %collective-permute-start.6 = (bf16[2,320,256]{2,1,0:T(8,128)(2,1)S(1)}, bf16[2,320,256]{2,1,0:T(8,128)(2,1)S(1)}, u32[]{:S(2)}, u32[]{:S(2)}) collective-permute-start(bf16[2,320,256]{2,1,0:T(8,128)(2,1)S(1)} %slice.17), channel_id=1, source_target_pairs={{6,0},{0,2},{2,4},{4,6},{7,1},{1,3},{3,5},{5,7},{14,8},{8,10},{10,... | collective-permute-start | bytes 983048 | tf_op jit(solution)/shard_map/ppermute | solution.py:19
  66.4 8.4 %collective-permute-start.13 = (bf16[2,320,256]{2,1,0:T(8,128)(2,1)S(1)}, bf16[2,320,256]{2,1,0:T(8,128)(2,1)S(1)}, u32[]{:S(2)}, u32[]{:S(2)}) collective-permute-start(bf16[2,320,256]{2,1,0:T(8,128)(2,1)S(1)} %slice.18), channel_id=1, source_target_pairs={{8,0},{16,8},{24,16},{0,24},{9,1},{17,9},{25,17},{1,25},{10,2},{18... | collective-permute-start | bytes 983048 | tf_op jit(solution)/shard_map/ppermute | solution.py:19
  68.0 9.0 %collective-permute-start.14 = (bf16[2,320,256]{2,1,0:T(8,128)(2,1)S(1)}, bf16[2,320,256]{2,1,0:T(8,128)(2,1)S(1)}, u32[]{:S(2)}, u32[]{:S(2)}) collective-permute-start(bf16[2,320,256]{2,1,0:T(8,128)(2,1)S(1)} %slice.19), channel_id=1, source_target_pairs={{24,0},{0,8},{8,16},{16,24},{25,1},{1,9},{9,17},{17,25},{26,2},{2,... | collective-permute-start | bytes 983048 | tf_op jit(solution)/shard_map/ppermute | solution.py:19
  77.7 26.8 %copy-start = (s32[64]{0:T(128)S(1)}, s32[64]{0:T(128)}, u32[]{:S(2)}) copy-start(s32[64]{0:T(128)} %owner_ref.1) | copy-start | bytes 772
  77.7 43.8 %copy-start.1 = (bf16[640,256]{1,0:T(8,128)(2,1)S(1)}, bf16[640,256]{1,0:T(8,128)(2,1)}, u32[]{:S(2)}) copy-start(bf16[640,256]{1,0:T(8,128)(2,1)} %param.9) | copy-start | bytes 983044
  77.7 43.8 %copy-start.2 = (f32[640]{0:T(1024)S(1)}, f32[640]{0:T(1024)}, u32[]{:S(2)}) copy-start(f32[640]{0:T(1024)} %param.13) | copy-start | bytes 7684
  106.2 15.3 %all-to-all-start.1 = ((bf16[32,20,256]{2,1,0:T(8,128)(2,1)}), bf16[32,20,256]{2,1,0:T(8,128)(2,1)S(1)}, u32[]{:S(2)}, u32[]{:S(2)}) async-start(bf16[32,20,256]{2,1,0:T(8,128)(2,1)} %reorder.1), calls=%async_computation.1 | async-start | bytes 786432 | tf_op jit(solution)/shard_map/all_to_all | solution.py:159
Sparse Core Ops, SparseCore 0:
  9.2 56.3 all-gather.2

commit v3 on v2

v3 whole, which is shorter than its diff:
```python
import functools
import itertools

import jax
import jax.numpy as jnp
from jax import lax
from jax.experimental import pallas as pl
from jax.experimental.pallas import tpu as pltpu
from jax.sharding import Mesh
from jax.sharding import PartitionSpec as P

TILE = 128
PBLK = 64
ZH, CORE, NX, NY, ZL = 4, 2, 4, 4, 2
AXES = ("zh", "core", "x", "y", "zl")
SMEM, VMEM, HBM = (
    pl.BlockSpec(memory_space=m) for m in (pltpu.SMEM, pltpu.VMEM, pltpu.HBM)
)


def send(value, route):
    sizes = (ZH, CORE, NX, NY, ZL)
    pairs = []
    for at in itertools.product(*(range(n) for n in sizes)):
        source = [i % n for i, n in zip(route(*at), sizes)]
        pairs.append(tuple(functools.reduce(lambda u, v: u * v[1] + v[0], zip(p, sizes), 0) for p in (source, at)))
    return lax.ppermute(value, AXES, pairs)


def ring(value):
    def route(zh, core, x, y, zl):
        z = zh * ZL + zl + 2 * core - 1
        return z // ZL, core, x, y, z % ZL

    return send(value, route)


def swap(value):
    return send(value, lambda zh, core, x, y, zl: (zh, 1 - core, x, y, zl))


def minor(value, by):
    return send(value, lambda zh, core, x, y, zl: (zh, core, x + by * (1 - core), y + by * core, zl))


def major(value, by):
    return send(value, lambda zh, core, x, y, zl: (zh, core, x + by * core, y + by * (1 - core), zl))


def gather_amplitudes(own):
    block = jnp.stack([own] + [minor(own, d) for d in (1, 2, 3)])
    ahead, behind = major(block, 1), major(block, 3)
    far = [major(ahead[:2], 1), major(behind[2:], 3)]
    return [block, ahead, behind] + far, [(d, e) for d in (0, 1, 3, 2) for e in range(4)]


def gather_panel(own):
    near, late = [(own, (0, 0))], []
    other = swap(own)
    near.append((other, (0, 1)))
    first, second = own, other
    for d in (1, 2, 3, 4):
        out = near if d < 3 else late
        first = ring(first)
        out += [(first, (d, 0)), (swap(first), (-d, 1))]
        if d < 4:
            second = ring(second)
            out += [(second, (d, 1)), (swap(second), (-d, 0))]
    return near, late


def ladder_kernel(more, last, count, *refs):
    line_ref, first_ref, part_ref, place_ref, screen_ref = refs[:5]
    blocks, refs = refs[5:10], refs[10:]
    panels, refs = refs[:count], refs[count:]
    if more:
        before, refs = refs[0], refs[1:]
    out_ref, left_ref, held, left_sem, sems = refs[:5]
    total = refs[5] if last else out_ref
    depth, width = held.shape[1:]
    rows = left_ref.shape[1]
    tiles = place_ref.shape[0]
    line, per, wide = line_ref[0], depth // TILE, left_ref.shape[2] // TILE

    copies, at = [], 0
    for i, block in enumerate(blocks):
        n = block.shape[0]
        copies.append(pltpu.make_async_copy(block, left_ref.at[at : at + n], left_sem.at[i]))
        at += n
    fetch = [pltpu.make_async_copy(panel, held.at[g], sems.at[g]) for g, panel in enumerate(panels)]
    for c in copies + fetch:
        c.start()
    if more:
        total[...] = before[...]
    else:
        total[...] = jnp.zeros_like(total)
    for c in copies:
        c.wait()

    @pl.loop(0, count)
    def _(g):
        pltpu.make_async_copy(panels[0], held.at[g], sems.at[g]).wait()
        part, first = part_ref[g], first_ref[g]
        for j in range(width // TILE):
            wanted = (line * ZL + part) * 2 + j
            left = []
            for r in range(per):
                at = place_ref[first + r]
                column = pl.ds(pl.multiple_of(lax.rem(at, wide) * TILE, TILE), TILE)
                strips = []
                for b in range(rows // PBLK):
                    mark = screen_ref[(b * tiles + first + r) * tiles + wanted]
                    strip = left_ref[at // wide, b * PBLK : (b + 1) * PBLK, column]
                    strips.append(strip * jnp.full((PBLK, TILE), mark, jnp.float32).astype(strip.dtype))
                left.append(jnp.concatenate(strips, axis=0))
            total[part, j] += jnp.dot(
                jnp.concatenate(left, axis=1),
                held[g, :, j * TILE : (j + 1) * TILE],
                preferred_element_type=jnp.float32,
            )

    if last:
        chunks, piece, _ = out_ref.shape
        for i in range(total.shape[0] * total.shape[1]):
            for c in range(chunks):
                strip = total[i // 2, i % 2, c * piece : (c + 1) * piece, :]
                out_ref[c, :, i * TILE : (i + 1) * TILE] = strip.astype(out_ref.dtype)


def ladder(line, where, place, screen, blocks, panels, before, last):
    depth, width = panels[0].shape
    rows = blocks[0].shape[1]
    count, pieces = len(panels), sum(b.shape[0] for b in blocks)
    sums = (ZL, width // TILE, rows, TILE)
    chunks = NX * NY
    more = before is not None
    return pl.pallas_call(
        functools.partial(ladder_kernel, more, last, count),
        out_shape=jax.ShapeDtypeStruct((chunks, rows // chunks, ZL * width), jnp.bfloat16)
        if last
        else jax.ShapeDtypeStruct(sums, jnp.float32),
        in_specs=[SMEM] * 5 + [HBM] * (len(blocks) + count) + [VMEM] * more,
        out_specs=VMEM,
        scratch_shapes=[
            pltpu.VMEM((pieces,) + blocks[0].shape[1:], jnp.bfloat16),
            pltpu.VMEM((count, depth, width), jnp.bfloat16),
            pltpu.SemaphoreType.DMA((len(blocks),)),
            pltpu.SemaphoreType.DMA((count,)),
        ]
        + [pltpu.VMEM(sums, jnp.float32)] * last,
        compiler_params=pltpu.CompilerParams(vmem_limit_bytes=50 << 20),
        cost_estimate=pl.CostEstimate(
            flops=4 * rows * width * count * depth,
            bytes_accessed=(2 * rows + width) * count * depth * 2,
            transcendentals=0,
        ),
        name="ladder",
    )(line, *where, place, screen, *blocks, *panels, *([before] if more else []))


def reorder_kernel(owner_ref, src_ref, dst_ref):
    for s in range(owner_ref.shape[0]):
        t = owner_ref[s]
        tile = src_ref[t // 4, :, pl.ds(pl.multiple_of(lax.rem(t, 4) * TILE, TILE), TILE)]
        device, j = s // 2, s % 2
        target = device % ZL * NX * NY + device // ZL
        dst_ref[target, :, j * TILE : (j + 1) * TILE] = tile


def reorder(owner, spread):
    n, rows, width = spread.shape
    return pl.pallas_call(
        reorder_kernel,
        out_shape=jax.ShapeDtypeStruct((n * ZL, rows, width // ZL), spread.dtype),
        in_specs=[SMEM, VMEM],
        out_specs=VMEM,
        compiler_params=pltpu.CompilerParams(vmem_limit_bytes=8 << 20),
        cost_estimate=pl.CostEstimate(flops=0, bytes_accessed=1 << 20, transcendentals=0),
        name="reorder",
    )(owner, spread)


def local(amplitudes, tile_owner, integrals, screening, occ_energy, virt_energy):
    pairs, width = amplitudes.shape
    half = pairs // ZL
    tiles = tile_owner.shape[0]
    zh, core, x, y, zl = (lax.axis_index(a) for a in AXES)
    line = x * NY + y
    steps = jnp.arange(tiles, dtype=jnp.int32)

    mine = lax.dynamic_slice_in_dim(amplitudes, zl * half, half, 0)
    other = lax.dynamic_slice_in_dim(amplitudes, (1 - zl) * half, half, 0)
    other = send(other, lambda zh, core, x, y, zl: (zh, core, x, y, 1 - zl))
    blocks, order = gather_amplitudes(jnp.concatenate([mine, other], axis=1))
    near, late = gather_panel(integrals)

    far, close = (jnp.array(v, jnp.int32) for v in zip(*order))
    dx, dy = jnp.where(core == 0, close, far), jnp.where(core == 0, far, close)
    device = (((x + dx) % NX) * NY + (y + dy) % NY)[:, None] * ZL + (zl ^ jnp.arange(ZL, dtype=jnp.int32))
    slots = (2 * device[:, :, None] + jnp.arange(2, dtype=jnp.int32)).reshape(-1)
    held = jnp.sum(jnp.where(slots[:, None] == steps[None, :], tile_owner[None, :], 0), axis=1)
    place = jnp.sum(jnp.where(held[:, None] == steps[None, :], steps[:, None], 0), axis=0)

    screen = lax.dynamic_slice_in_dim(screening, zl * (half // PBLK), half // PBLK, 0)
    screen = screen.astype(jnp.float32).reshape(-1)
    found = None
    for last, group in ((False, near), (True, late)):
        panels, marks = zip(*group)
        step, flip = (jnp.array(v, jnp.int32) for v in zip(*marks))
        chip = (zh * ZL + zl + step * (2 * core - 1)) % (ZH * ZL)
        first = (chip // ZL * CORE + (core ^ flip)) * (integrals.shape[0] // TILE)
        where = (first.astype(jnp.int32), (chip % ZL).astype(jnp.int32))
        found = ladder(jnp.stack([line]).astype(jnp.int32), where, place, screen, blocks, panels, found, last)
    spread = lax.all_to_all(found, ("x", "y"), 0, 0, tiled=True)
    sent = reorder(tile_owner, spread)
    total = lax.all_to_all(sent, ("zl", "x", "y"), 0, 0, tiled=True)
    total = total.reshape(pairs, width).astype(jnp.float32)

    own = 2 * (line * ZL + zl)
    virt_owned = jnp.concatenate(
        [lax.dynamic_slice_in_dim(virt_energy, tile_owner[own + i] * TILE, TILE, 0) for i in range(2)]
    )
    residual = total + (virt_owned[None, :] - occ_energy[:, None]) * amplitudes.astype(jnp.float32)
    return residual.astype(jnp.bfloat16)


def solution(mesh):
    fine = Mesh(mesh.devices.reshape(ZH, CORE, NX, NY, ZL), AXES)
    pair, vcol = ("zh", "core"), ("x", "y", "zl")
    return jax.shard_map(
        local,
        mesh=fine,
        in_specs=(P(pair, vcol), P(), P(pair, vcol), P(pair, None, None), P(pair), P()),
        out_specs=P(pair, vcol),
        check_vma=False,
    )
```

time: 130 us -> 118 us (0.908)
  between operations: 14.8 us -> 1.64 us
  local copies, waits for them, and re-layouts: 16.2 us -> 5.96 us
  starting transfers between devices: 26 us -> 36 us
  Pallas kernels: 15.8 us -> 20 us
    ppermute x15 -> x23, starting transfers between devices: 20.3 us -> 31.9 us  [send(): return lax.ppermute(value, AXES, pairs)]
    unnamed x21 -> x26, local copies, waits for them, and re-layouts: 12.2 us -> 0.9 us
    pallas_call x1 -> x2, Pallas kernels: 14.1 us -> 18.2 us  [ladder(): pl.pallas_call(functools.partial(ladder_kernel, more, last, count), out_s...]
    slice x4 -> x2, local copies, waits for them, and re-layouts: 0.09 us -> 2.28 us  [gather_amplitudes(): far = [major(ahead[:2], 1), major(behind[2:], 3)]]
    all_to_all x1, starting transfers between devices: 5.68 us -> 4.03 us  [local(): total = lax.all_to_all(sent, ('zl', 'x', 'y'), 0, 0, tiled=True)]
    ppermute x15 -> x23, waiting for transfers between devices: 32 us -> 32.1 us  [send(): return lax.ppermute(value, AXES, pairs)]
  transfers between devices with their start and end apart: 17 -> 24, of which waited for: 8 -> 11; matrix products, arithmetic and copies ran while one was open for 15% -> 6% of each run, Pallas kernels for 0% -> 9%
where the time goes in v3:
time: 118 us
  waiting for transfers between devices  38.9 us (33%)
  starting transfers between devices  36 us (31%)
  Pallas kernels  20 us (17%)
  blocking collectives  11.7 us (10%)
  local copies, waits for them, and re-layouts  5.96 us (5%)
  other arithmetic  3.63 us (3%)
  between operations  1.64 us (1%)
    ppermute x23, waiting for transfers between devices, send(): return lax.ppermute(value, AXES, pairs)  32.1 us
    ppermute x23, starting transfers between devices, send(): return lax.ppermute(value, AXES, pairs)  31.9 us
    pallas_call x2, Pallas kernels, ladder(): pl.pallas_call(functools.partial(ladder_kernel, more, last, count), out_s...  18.2 us
    all_to_all x1, blocking collectives, local(): spread = lax.all_to_all(found, ('x', 'y'), 0, 0, tiled=True)  11.7 us
    all_to_all x1, waiting for transfers between devices, local(): total = lax.all_to_all(sent, ('zl', 'x', 'y'), 0, 0, tiled=True)  6.76 us
    all_to_all x1, starting transfers between devices, local(): total = lax.all_to_all(sent, ('zl', 'x', 'y'), 0, 0, tiled=True)  4.03 us
  transfers between devices with their start and end apart: 24, of which 11 were waited for; matrix products, arithmetic and copies ran while one was open for 6% of the time, Pallas kernels for 9%

profile of v3, /device:TPU:64, one launch (start us, length us, event | category | flops | bytes accessed | tf_op | source)
XLA Modules:
  0.0 117.8 jit_solution(14200576463107815160)
XLA Ops:
  0.0 1.1 constant_dynamic-slice_fusion.1
  1.1 2.0 %collective-permute-start = (bf16[320,256]{1,0:T(8,128)(2,1)S(1)}, bf16[320,256]{1,0:T(8,128)(2,1)S(1)}, u32[]{:S(2)}, u32[]{:S(2)}) collective-permute-start(bf16[320,256]{1,0:T(8,128)(2,1)S(1)} %get-tuple-element.12), channel_id=1, source_target_pairs={{1,0},{0,1},{3,2},{2,3},{5,4},{4,5},{7,6},{6,7},{9,8},{8,9},{11,10... | collective-permute-start | bytes 491528 | tf_op jit(solution)/shard_map/ppermute | solution.py:27
  3.1 4.2 %collective-permute-done = bf16[320,256]{1,0:T(8,128)(2,1)S(1)} collective-permute-done((bf16[320,256]{1,0:T(8,128)(2,1)S(1)}, bf16[320,256]{1,0:T(8,128)(2,1)S(1)}, u32[]{:S(2)}, u32[]{:S(2)}) %collective-permute-start) | collective-permute-done | bytes 163872 | tf_op jit(solution)/shard_map/ppermute | solution.py:27
  7.3 2.8 %collective-permute-start.1 = (bf16[320,512]{1,0:T(8,128)(2,1)S(1)}, bf16[320,512]{1,0:T(8,128)(2,1)S(1)}, u32[]{:S(2)}, u32[]{:S(2)}) collective-permute-start(bf16[320,512]{1,0:T(8,128)(2,1)S(1)} %get-tuple-element.10), channel_id=1, source_target_pairs={{8,0},{9,1},{10,2},{11,3},{12,4},{13,5},{14,6},{15,7},{16,8},{17,9... | collective-permute-start | bytes 983048 | tf_op jit(solution)/shard_map/ppermute | solution.py:27
  11.9 1.7 %collective-permute-start.8 = (bf16[1024,256]{1,0:T(8,128)(2,1)S(1)}, bf16[1024,256]{1,0:T(8,128)(2,1)S(1)}, u32[]{:S(2)}, u32[]{:S(2)}) collective-permute-start(bf16[1024,256]{1,0:T(8,128)(2,1)S(1)} %copy-done.1), channel_id=1, source_target_pairs={{193,0},{0,1},{195,2},{2,3},{197,4},{4,5},{199,6},{6,7},{201,8},{8... | collective-permute-start | bytes 1572872 | tf_op jit(solution)/shard_map/ppermute | solution.py:27
  13.6 3.1 %collective-permute-start.13 = (bf16[1024,256]{1,0:T(8,128)(2,1)S(1)}, bf16[1024,256]{1,0:T(8,128)(2,1)S(1)}, u32[]{:S(2)}, u32[]{:S(2)}) collective-permute-start(bf16[1024,256]{1,0:T(8,128)(2,1)S(1)} %collective-permute-done.12.refs_11_), channel_id=1, source_target_pairs={{193,0},{0,1},{195,2},{2,3},{197,4},{4,5},{199,6},{6,7},{201,8},{8... | collective-permute-start | bytes 1572872 | tf_op jit(solution)/shard_map/ppermute | solution.py:27
  16.7 1.6 %collective-permute-done.1 = bf16[320,512]{1,0:T(8,128)(2,1)S(1)} collective-permute-done((bf16[320,512]{1,0:T(8,128)(2,1)S(1)}, bf16[320,512]{1,0:T(8,128)(2,1)S(1)}, u32[]{:S(2)}, u32[]{:S(2)}) %collective-permute-start.1) | collective-permute-done | bytes 327712 | tf_op jit(solution)/shard_map/ppermute | solution.py:27
  18.9 3.4 %collective-permute-done.3 = bf16[320,512]{1,0:T(8,128)(2,1)S(1)} collective-permute-done((bf16[320,512]{1,0:T(8,128)(2,1)S(1)}, bf16[320,512]{1,0:T(8,128)(2,1)S(1)}, u32[]{:S(2)}, u32[]{:S(2)}) %collective-permute-start.3) | collective-permute-done | bytes 327712 | tf_op jit(solution)/shard_map/ppermute | solution.py:27
  22.3 1.2 %pad_maximum_fusion.refs_5_ = bf16[4,320,512]{2,1,0:T(8,128)(2,1)} fusion(bf16[1,320,512]{2,1,0:T(8,128)(2,1)S(1)} %bitcast.10, bf16[1,320,512]{2,1,0:T(8,128)(2,1)S(1)} %bitcast.9, bf16[1,320,512]{2,1,0:T(8,128)(2,1)S(1)} %bitcast.8, bf16[1,320,512]{2,1,0:T(8,128)(2,1)S(1)} %get-tuple-element.9), kind=kLoop, calls=%fused_computation | loop fusion | flops 1966080 | bytes 2621440 | tf_op jit(solution)/shard_map/stack | solution.py:51
  23.5 3.0 %collective-permute-start.4 = (bf16[4,320,512]{2,1,0:T(8,128)(2,1)}, bf16[4,320,512]{2,1,0:T(8,128)(2,1)}, u32[]{:S(2)}, u32[]{:S(2)}) collective-permute-start(bf16[4,320,512]{2,1,0:T(8,128)(2,1)} %pad_maximum_fusion.refs_5_), channel_id=1, source_target_pairs={{2,0},{3,1},{4,2},{5,3},{6,4},{7,5},{0,6},{1,7},{10,8},{11,9},{12,... | collective-permute-start | bytes 3932168 | tf_op jit(solution)/shard_map/ppermute | solution.py:27
  26.5 1.7 %collective-permute-start.9 = (bf16[1024,256]{1,0:T(8,128)(2,1)S(1)}, bf16[1024,256]{1,0:T(8,128)(2,1)S(1)}, u32[]{:S(2)}, u32[]{:S(2)}) collective-permute-start(bf16[1024,256]{1,0:T(8,128)(2,1)S(1)} %collective-permute-done.8.refs_12_), channel_id=1, source_target_pairs={{193,0},{0,1},{195,2},{2,3},{197,4},{4,5},{199,6},{6,7},{201,8},{8... | collective-permute-start | bytes 1572872 | tf_op jit(solution)/shard_map/ppermute | solution.py:27
  28.4 3.2 %collective-permute-start.14 = (bf16[1024,256]{1,0:T(8,128)(2,1)S(1)}, bf16[1024,256]{1,0:T(8,128)(2,1)}, u32[]{:S(2)}, u32[]{:S(2)}) collective-permute-start(bf16[1024,256]{1,0:T(8,128)(2,1)S(1)} %collective-permute-done.13.refs_14_), channel_id=1, source_target_pairs={{193,0},{0,1},{195,2},{2,3},{197,4},{4,5},{199,6},{6,7},{201,8},{8... | collective-permute-start | bytes 1572872 | tf_op jit(solution)/shard_map/ppermute | solution.py:27
  31.7 4.0 %collective-permute-done.9.refs_16_ = bf16[1024,256]{1,0:T(8,128)(2,1)S(1)} collective-permute-done((bf16[1024,256]{1,0:T(8,128)(2,1)S(1)}, bf16[1024,256]{1,0:T(8,128)(2,1)S(1)}, u32[]{:S(2)}, u32[]{:S(2)}) %collective-permute-start.9) | collective-permute-done | bytes 524320 | tf_op jit(solution)/shard_map/ppermute | solution.py:27
  35.7 2.4 %collective-permute-start.10 = (bf16[1024,256]{1,0:T(8,128)(2,1)S(1)}, bf16[1024,256]{1,0:T(8,128)(2,1)S(1)}, u32[]{:S(2)}, u32[]{:S(2)}) collective-permute-start(bf16[1024,256]{1,0:T(8,128)(2,1)S(1)} %collective-permute-done.9.refs_16_), channel_id=1, source_target_pairs={{193,0},{0,1},{195,2},{2,3},{197,4},{4,5},{199,6},{6,7},{201,8},{8... | collective-permute-start | bytes 1572872 | tf_op jit(solution)/shard_map/ppermute | solution.py:27
  38.3 3.1 %collective-permute-done.14.refs_18_ = bf16[1024,256]{1,0:T(8,128)(2,1)} collective-permute-done((bf16[1024,256]{1,0:T(8,128)(2,1)S(1)}, bf16[1024,256]{1,0:T(8,128)(2,1)}, u32[]{:S(2)}, u32[]{:S(2)}) %collective-permute-start.14) | collective-permute-done | bytes 524320 | tf_op jit(solution)/shard_map/ppermute | solution.py:27
  41.4 0.9 dynamic-slice_convert_fusion
  42.8 4.1 %collective-permute-done.10.refs_10_ = bf16[1024,256]{1,0:T(8,128)(2,1)S(1)} collective-permute-done((bf16[1024,256]{1,0:T(8,128)(2,1)S(1)}, bf16[1024,256]{1,0:T(8,128)(2,1)S(1)}, u32[]{:S(2)}, u32[]{:S(2)}) %collective-permute-start.10) | collective-permute-done | bytes 524320 | tf_op jit(solution)/shard_map/ppermute | solution.py:27
  46.9 2.4 %collective-permute-start.15 = (bf16[1024,256]{1,0:T(8,128)(2,1)}, bf16[1024,256]{1,0:T(8,128)(2,1)S(1)}, u32[]{:S(2)}, u32[]{:S(2)}) collective-permute-start(bf16[1024,256]{1,0:T(8,128)(2,1)} %collective-permute-done.14.refs_18_), channel_id=1, source_target_pairs={{193,0},{0,1},{195,2},{2,3},{197,4},{4,5},{199,6},{6,7},{201,8},{8... | collective-permute-start | bytes 1572872 | tf_op jit(solution)/shard_map/ppermute | solution.py:27
  49.3 3.7 %collective-permute-start.17 = (bf16[1024,256]{1,0:T(8,128)(2,1)S(1)}, bf16[1024,256]{1,0:T(8,128)(2,1)S(1)}, u32[]{:S(2)}, u32[]{:S(2)}) collective-permute-start(bf16[1024,256]{1,0:T(8,128)(2,1)S(1)} %collective-permute-done.10.refs_10_), channel_id=1, source_target_pairs={{193,0},{0,1},{195,2},{2,3},{197,4},{4,5},{199,6},{6,7},{201,8},{8... | collective-permute-start | bytes 1572872 | tf_op jit(solution)/shard_map/ppermute | solution.py:27
  53.2 1.1 slice.8
  54.3 1.1 slice.9
  55.5 3.3 %collective-permute-start.6 = (bf16[2,320,512]{2,1,0:T(8,128)(2,1)S(1)}, bf16[2,320,512]{2,1,0:T(8,128)(2,1)S(1)}, u32[]{:S(2)}, u32[]{:S(2)}) collective-permute-start(bf16[2,320,512]{2,1,0:T(8,128)(2,1)S(1)} %slice.8), channel_id=1, source_target_pairs={{2,0},{3,1},{4,2},{5,3},{6,4},{7,5},{0,6},{1,7},{10,8},{11,9},{12,... | collective-permute-start | bytes 1966088 | tf_op jit(solution)/shard_map/ppermute | solution.py:27
  58.9 3.0 %collective-permute-done.17.refs_14_ = bf16[1024,256]{1,0:T(8,128)(2,1)S(1)} collective-permute-done((bf16[1024,256]{1,0:T(8,128)(2,1)S(1)}, bf16[1024,256]{1,0:T(8,128)(2,1)S(1)}, u32[]{:S(2)}, u32[]{:S(2)}) %collective-permute-start.17) | collective-permute-done | bytes 524320 | tf_op jit(solution)/shard_map/ppermute | solution.py:27
  62.5 4.4 %collective-permute-done.6.refs_8_ = bf16[2,320,512]{2,1,0:T(8,128)(2,1)S(1)} collective-permute-done((bf16[2,320,512]{2,1,0:T(8,128)(2,1)S(1)}, bf16[2,320,512]{2,1,0:T(8,128)(2,1)S(1)}, u32[]{:S(2)}, u32[]{:S(2)}) %collective-permute-start.6) | collective-permute-done | bytes 655392 | tf_op jit(solution)/shard_map/ppermute | solution.py:27
  66.9 3.7 %collective-permute-done.7.refs_9_ = bf16[2,320,512]{2,1,0:T(8,128)(2,1)S(1)} collective-permute-done((bf16[2,320,512]{2,1,0:T(8,128)(2,1)S(1)}, bf16[2,320,512]{2,1,0:T(8,128)(2,1)S(1)}, u32[]{:S(2)}, u32[]{:S(2)}) %collective-permute-start.7) | collective-permute-done | bytes 655392 | tf_op jit(solution)/shard_map/ppermute | solution.py:27
  71.4 10.6 %ladder.2.refs_16_ = f32[2,2,320,128]{3,2,1,0:T(8,128)} custom-call(s32[1]{0:T(128)} %bitcast.refs_0_, s32[10]{0:T(128)S(1)} %add_multiply_fusion.1.refs_1_, s32[10]{0:T(128)S(1)} %get-tuple-element.5.refs_2_, s32[64]{0:T(128)S(1)} %select_reduce_fusion.refs_3_, f32[20480]{0:T(1024)S(1)} %reshape.63.refs_4_, bf16[4,320,512]{2,1,0:T(8,128)(2,1)} %pad_maximum_fusion.refs_5_, ...), custom_call_target="tpu_custom_call" | custom-call | flops 3355443200 | bytes 18350080 | tf_op jit(solution)/shard_map/ladder/pallas_call | solution.py:137
  82.0 7.7 %ladder.3 = bf16[16,20,512]{2,1,0:T(8,128)(2,1)S(1)} custom-call(s32[1]{0:T(128)} %bitcast.refs_0_, s32[6]{0:T(128)S(1)} %add_multiply_fusion.2.refs_1_, s32[6]{0:T(128)S(1)} %get-tuple-element.7.refs_2_, s32[64]{0:T(128)S(1)} %select_reduce_fusion.refs_3_, f32[20480]{0:T(1024)S(1)} %reshape.63.refs_4_, bf16[4,320,512]{2,1,0:T(8,128)(2,1)} %pad_maximum_fusion.refs_5_, ...), custom_call_target="tpu_custom_call" | custom-call | flops 2013265920 | bytes 11010048 | tf_op jit(solution)/shard_map/ladder/pallas_call | solution.py:137
  89.7 11.7 %all_to_all.10.src_ref = bf16[16,20,512]{2,1,0:T(8,128)(2,1)S(1)} all-to-all(bf16[16,20,512]{2,1,0:T(8,128)(2,1)S(1)} %ladder.3), channel_id=1, replica_groups=mesh['zh'=4,'core'=2,'x'=4,'y'=4,'zl'=2] {'x','y'}, dimensions={0} | all-to-all | bytes 655360 | tf_op jit(solution)/shard_map/all_to_all | solution.py:214
  101.4 1.7 %reorder.1 = bf16[32,20,256]{2,1,0:T(8,128)(2,1)} custom-call(s32[64]{0:T(128)S(1)} %copy-done, bf16[16,20,512]{2,1,0:T(8,128)(2,1)S(1)} %all_to_all.10.src_ref), custom_call_target="tpu_custom_call" | custom-call | bytes 1048576 | tf_op jit(solution)/shard_map/reorder/pallas_call | solution.py:172
  103.2 4.0 %all-to-all-start.1 = ((bf16[32,20,256]{2,1,0:T(8,128)(2,1)}), bf16[32,20,256]{2,1,0:T(8,128)(2,1)S(1)}, u32[]{:S(2)}, u32[]{:S(2)}) async-start(bf16[32,20,256]{2,1,0:T(8,128)(2,1)} %reorder.1), calls=%async_computation.1 | async-start | bytes 786432 | tf_op jit(solution)/shard_map/all_to_all | solution.py:216
  110.0 6.8 %all-to-all-done.1 = bf16[32,20,256]{2,1,0:T(8,128)(2,1)S(1)} async-done(((bf16[32,20,256]{2,1,0:T(8,128)(2,1)}), bf16[32,20,256]{2,1,0:T(8,128)(2,1)S(1)}, u32[]{:S(2)}, u32[]{:S(2)}) %all-to-all-start.1) | async-done | bytes 327712 | tf_op jit(solution)/shard_map/all_to_all | solution.py:216
  116.9 0.9 add_convert_fusion
  (69 shorter events, 6.2 us)
Async XLA Ops:
  0.0 11.9 %copy-start.1 = (bf16[1024,256]{1,0:T(8,128)(2,1)S(1)}, bf16[1024,256]{1,0:T(8,128)(2,1)}, u32[]{:S(2)}) copy-start(bf16[1024,256]{1,0:T(8,128)(2,1)} %refs_10_.1) | copy-start | bytes 1572868
  1.1 6.2 %collective-permute-start = (bf16[320,256]{1,0:T(8,128)(2,1)S(1)}, bf16[320,256]{1,0:T(8,128)(2,1)S(1)}, u32[]{:S(2)}, u32[]{:S(2)}) collective-permute-start(bf16[320,256]{1,0:T(8,128)(2,1)S(1)} %get-tuple-element.12), channel_id=1, source_target_pairs={{1,0},{0,1},{3,2},{2,3},{5,4},{4,5},{7,6},{6,7},{9,8},{8,9},{11,10... | collective-permute-start | bytes 491528 | tf_op jit(solution)/shard_map/ppermute | solution.py:27
  3.1 10.5 %collective-permute-start.12 = (bf16[1024,256]{1,0:T(8,128)(2,1)}, bf16[1024,256]{1,0:T(8,128)(2,1)S(1)}, u32[]{:S(2)}, u32[]{:S(2)}) collective-permute-start(bf16[1024,256]{1,0:T(8,128)(2,1)} %refs_10_.1), channel_id=1, source_target_pairs={{32,0},{33,1},{34,2},{35,3},{36,4},{37,5},{38,6},{39,7},{40,8},{41... | collective-permute-start | bytes 1572872 | tf_op jit(solution)/shard_map/ppermute | solution.py:27
  7.3 11.0 %collective-permute-start.1 = (bf16[320,512]{1,0:T(8,128)(2,1)S(1)}, bf16[320,512]{1,0:T(8,128)(2,1)S(1)}, u32[]{:S(2)}, u32[]{:S(2)}) collective-permute-start(bf16[320,512]{1,0:T(8,128)(2,1)S(1)} %get-tuple-element.10), channel_id=1, source_target_pairs={{8,0},{9,1},{10,2},{11,3},{12,4},{13,5},{14,6},{15,7},{16,8},{17,9... | collective-permute-start | bytes 983048 | tf_op jit(solution)/shard_map/ppermute | solution.py:27
  10.2 8.7 %collective-permute-start.2 = (bf16[320,512]{1,0:T(8,128)(2,1)S(1)}, bf16[320,512]{1,0:T(8,128)(2,1)S(1)}, u32[]{:S(2)}, u32[]{:S(2)}) collective-permute-start(bf16[320,512]{1,0:T(8,128)(2,1)S(1)} %get-tuple-element.10), channel_id=1, source_target_pairs={{16,0},{17,1},{18,2},{19,3},{20,4},{21,5},{22,6},{23,7},{24,8},{25... | collective-permute-start | bytes 983048 | tf_op jit(solution)/shard_map/ppermute | solution.py:27
  11.0 11.3 %collective-permute-start.3 = (bf16[320,512]{1,0:T(8,128)(2,1)S(1)}, bf16[320,512]{1,0:T(8,128)(2,1)S(1)}, u32[]{:S(2)}, u32[]{:S(2)}) collective-permute-start(bf16[320,512]{1,0:T(8,128)(2,1)S(1)} %get-tuple-element.10), channel_id=1, source_target_pairs={{24,0},{25,1},{26,2},{27,3},{28,4},{29,5},{30,6},{31,7},{0,8},{1,9... | collective-permute-start | bytes 983048 | tf_op jit(solution)/shard_map/ppermute | solution.py:27
  11.9 14.7 %collective-permute-start.8 = (bf16[1024,256]{1,0:T(8,128)(2,1)S(1)}, bf16[1024,256]{1,0:T(8,128)(2,1)S(1)}, u32[]{:S(2)}, u32[]{:S(2)}) collective-permute-start(bf16[1024,256]{1,0:T(8,128)(2,1)S(1)} %copy-done.1), channel_id=1, source_target_pairs={{193,0},{0,1},{195,2},{2,3},{197,4},{4,5},{199,6},{6,7},{201,8},{8... | collective-permute-start | bytes 1572872 | tf_op jit(solution)/shard_map/ppermute | solution.py:27
  13.6 14.8 %collective-permute-start.13 = (bf16[1024,256]{1,0:T(8,128)(2,1)S(1)}, bf16[1024,256]{1,0:T(8,128)(2,1)S(1)}, u32[]{:S(2)}, u32[]{:S(2)}) collective-permute-start(bf16[1024,256]{1,0:T(8,128)(2,1)S(1)} %collective-permute-done.12.refs_11_), channel_id=1, source_target_pairs={{193,0},{0,1},{195,2},{2,3},{197,4},{4,5},{199,6},{6,7},{201,8},{8... | collective-permute-start | bytes 1572872 | tf_op jit(solution)/shard_map/ppermute | solution.py:27
  22.3 6.0 %copy-start.11 = (s32[16]{0:T(128)S(1)}, s32[16]{0:T(128)}, u32[]{:S(2)}) copy-start(s32[16]{0:T(128)} %constant.138.clone) | copy-start | bytes 196
  22.3 20.3 %copy-start = (s32[64]{0:T(128)S(1)}, s32[64]{0:T(128)}, u32[]{:S(2)}) copy-start(s32[64]{0:T(128)} %owner_ref.1) | copy-start | bytes 772
  22.3 20.5 %copy-start.7 = (s32[10]{0:T(128)S(1)}, s32[10]{0:T(128)}, u32[]{:S(2)}) copy-start(s32[10]{0:T(128)} %constant.139.clone) | copy-start | bytes 124
  23.5 23.4 %collective-permute-start.4 = (bf16[4,320,512]{2,1,0:T(8,128)(2,1)}, bf16[4,320,512]{2,1,0:T(8,128)(2,1)}, u32[]{:S(2)}, u32[]{:S(2)}) collective-permute-start(bf16[4,320,512]{2,1,0:T(8,128)(2,1)} %pad_maximum_fusion.refs_5_), channel_id=1, source_target_pairs={{2,0},{3,1},{4,2},{5,3},{6,4},{7,5},{0,6},{1,7},{10,8},{11,9},{12,... | collective-permute-start | bytes 3932168 | tf_op jit(solution)/shard_map/ppermute | solution.py:27
  26.5 22.8 %collective-permute-start.5 = (bf16[4,320,512]{2,1,0:T(8,128)(2,1)}, bf16[4,320,512]{2,1,0:T(8,128)(2,1)}, u32[]{:S(2)}, u32[]{:S(2)}) collective-permute-start(bf16[4,320,512]{2,1,0:T(8,128)(2,1)} %pad_maximum_fusion.refs_5_), channel_id=1, source_target_pairs={{6,0},{7,1},{0,2},{1,3},{2,4},{3,5},{4,6},{5,7},{14,8},{15,9},{8,1... | collective-permute-start | bytes 3932168 | tf_op jit(solution)/shard_map/ppermute | solution.py:27
  26.5 9.2 %collective-permute-start.9 = (bf16[1024,256]{1,0:T(8,128)(2,1)S(1)}, bf16[1024,256]{1,0:T(8,128)(2,1)S(1)}, u32[]{:S(2)}, u32[]{:S(2)}) collective-permute-start(bf16[1024,256]{1,0:T(8,128)(2,1)S(1)} %collective-permute-done.8.refs_12_), channel_id=1, source_target_pairs={{193,0},{0,1},{195,2},{2,3},{197,4},{4,5},{199,6},{6,7},{201,8},{8... | collective-permute-start | bytes 1572872 | tf_op jit(solution)/shard_map/ppermute | solution.py:27
  28.3 9.9 %collective-permute-start.19 = (bf16[1024,256]{1,0:T(8,128)(2,1)S(1)}, bf16[1024,256]{1,0:T(8,128)(2,1)}, u32[]{:S(2)}, u32[]{:S(2)}) collective-permute-start(bf16[1024,256]{1,0:T(8,128)(2,1)S(1)} %collective-permute-done.8.refs_12_), channel_id=1, source_target_pairs={{32,0},{33,1},{34,2},{35,3},{36,4},{37,5},{38,6},{39,7},{40,8},{41... | collective-permute-start | bytes 1572872 | tf_op jit(solution)/shard_map/ppermute | solution.py:27
  28.4 13.0 %collective-permute-start.14 = (bf16[1024,256]{1,0:T(8,128)(2,1)S(1)}, bf16[1024,256]{1,0:T(8,128)(2,1)}, u32[]{:S(2)}, u32[]{:S(2)}) collective-permute-start(bf16[1024,256]{1,0:T(8,128)(2,1)S(1)} %collective-permute-done.13.refs_14_), channel_id=1, source_target_pairs={{193,0},{0,1},{195,2},{2,3},{197,4},{4,5},{199,6},{6,7},{201,8},{8... | collective-permute-start | bytes 1572872 | tf_op jit(solution)/shard_map/ppermute | solution.py:27
  35.7 11.2 %collective-permute-start.10 = (bf16[1024,256]{1,0:T(8,128)(2,1)S(1)}, bf16[1024,256]{1,0:T(8,128)(2,1)S(1)}, u32[]{:S(2)}, u32[]{:S(2)}) collective-permute-start(bf16[1024,256]{1,0:T(8,128)(2,1)S(1)} %collective-permute-done.9.refs_16_), channel_id=1, source_target_pairs={{193,0},{0,1},{195,2},{2,3},{197,4},{4,5},{199,6},{6,7},{201,8},{8... | collective-permute-start | bytes 1572872 | tf_op jit(solution)/shard_map/ppermute | solution.py:27
  38.2 17.3 %collective-permute-start.21 = (bf16[1024,256]{1,0:T(8,128)(2,1)S(1)}, bf16[1024,256]{1,0:T(8,128)(2,1)}, u32[]{:S(2)}, u32[]{:S(2)}) collective-permute-start(bf16[1024,256]{1,0:T(8,128)(2,1)S(1)} %collective-permute-done.9.refs_16_), channel_id=1, source_target_pairs={{32,0},{33,1},{34,2},{35,3},{36,4},{37,5},{38,6},{39,7},{40,8},{41... | collective-permute-start | bytes 1572872 | tf_op jit(solution)/shard_map/ppermute | solution.py:27
  41.4 17.3 %collective-permute-start.20 = (bf16[1024,256]{1,0:T(8,128)(2,1)S(1)}, bf16[1024,256]{1,0:T(8,128)(2,1)}, u32[]{:S(2)}, u32[]{:S(2)}) collective-permute-start(bf16[1024,256]{1,0:T(8,128)(2,1)S(1)} %collective-permute-done.13.refs_14_), channel_id=1, source_target_pairs={{32,0},{33,1},{34,2},{35,3},{36,4},{37,5},{38,6},{39,7},{40,8},{41... | collective-permute-start | bytes 1572872 | tf_op jit(solution)/shard_map/ppermute | solution.py:27
  46.9 11.9 %collective-permute-start.22 = (bf16[1024,256]{1,0:T(8,128)(2,1)}, bf16[1024,256]{1,0:T(8,128)(2,1)S(1)}, u32[]{:S(2)}, u32[]{:S(2)}) collective-permute-start(bf16[1024,256]{1,0:T(8,128)(2,1)} %collective-permute-done.14.refs_18_), channel_id=1, source_target_pairs={{32,0},{33,1},{34,2},{35,3},{36,4},{37,5},{38,6},{39,7},{40,8},{41... | collective-permute-start | bytes 1572872 | tf_op jit(solution)/shard_map/ppermute | solution.py:27
  46.9 15.3 %collective-permute-start.15 = (bf16[1024,256]{1,0:T(8,128)(2,1)}, bf16[1024,256]{1,0:T(8,128)(2,1)S(1)}, u32[]{:S(2)}, u32[]{:S(2)}) collective-permute-start(bf16[1024,256]{1,0:T(8,128)(2,1)} %collective-permute-done.14.refs_18_), channel_id=1, source_target_pairs={{193,0},{0,1},{195,2},{2,3},{197,4},{4,5},{199,6},{6,7},{201,8},{8... | collective-permute-start | bytes 1572872 | tf_op jit(solution)/shard_map/ppermute | solution.py:27
  49.3 12.6 %collective-permute-start.17 = (bf16[1024,256]{1,0:T(8,128)(2,1)S(1)}, bf16[1024,256]{1,0:T(8,128)(2,1)S(1)}, u32[]{:S(2)}, u32[]{:S(2)}) collective-permute-start(bf16[1024,256]{1,0:T(8,128)(2,1)S(1)} %collective-permute-done.10.refs_10_), channel_id=1, source_target_pairs={{193,0},{0,1},{195,2},{2,3},{197,4},{4,5},{199,6},{6,7},{201,8},{8... | collective-permute-start | bytes 1572872 | tf_op jit(solution)/shard_map/ppermute | solution.py:27
  53.1 9.3 %copy-start.8 = (s32[6]{0:T(128)S(1)}, s32[6]{0:T(128)}, u32[]{:S(2)}) copy-start(s32[6]{0:T(128)} %constant.142.clone) | copy-start | bytes 76
  55.5 11.4 %collective-permute-start.6 = (bf16[2,320,512]{2,1,0:T(8,128)(2,1)S(1)}, bf16[2,320,512]{2,1,0:T(8,128)(2,1)S(1)}, u32[]{:S(2)}, u32[]{:S(2)}) collective-permute-start(bf16[2,320,512]{2,1,0:T(8,128)(2,1)S(1)} %slice.8), channel_id=1, source_target_pairs={{2,0},{3,1},{4,2},{5,3},{6,4},{7,5},{0,6},{1,7},{10,8},{11,9},{12,... | collective-permute-start | bytes 1966088 | tf_op jit(solution)/shard_map/ppermute | solution.py:27
  58.8 11.8 %collective-permute-start.7 = (bf16[2,320,512]{2,1,0:T(8,128)(2,1)S(1)}, bf16[2,320,512]{2,1,0:T(8,128)(2,1)S(1)}, u32[]{:S(2)}, u32[]{:S(2)}) collective-permute-start(bf16[2,320,512]{2,1,0:T(8,128)(2,1)S(1)} %slice.9), channel_id=1, source_target_pairs={{6,0},{7,1},{0,2},{1,3},{2,4},{3,5},{4,6},{5,7},{14,8},{15,9},{8,1... | collective-permute-start | bytes 1966088 | tf_op jit(solution)/shard_map/ppermute | solution.py:27
  58.8 11.7 %copy-start.12 = (bf16[1024,256]{1,0:T(8,128)(2,1)}, bf16[1024,256]{1,0:T(8,128)(2,1)S(1)}, u32[]{:S(2)}) copy-start(bf16[1024,256]{1,0:T(8,128)(2,1)S(1)} %collective-permute-done.22.refs_19_) | copy-start | bytes 1572868
  58.8 23.2 %collective-permute-start.11 = (bf16[1024,256]{1,0:T(8,128)(2,1)S(1)}, bf16[1024,256]{1,0:T(8,128)(2,1)S(1)}, u32[]{:S(2)}, u32[]{:S(2)}) collective-permute-start(bf16[1024,256]{1,0:T(8,128)(2,1)S(1)} %collective-permute-done.10.refs_10_), channel_id=1, source_target_pairs={{32,0},{33,1},{34,2},{35,3},{36,4},{37,5},{38,6},{39,7},{40,8},{41... | collective-permute-start | bytes 1572872 | tf_op jit(solution)/shard_map/ppermute | solution.py:27
  62.0 20.1 %collective-permute-start.18 = (bf16[1024,256]{1,0:T(8,128)(2,1)S(1)}, bf16[1024,256]{1,0:T(8,128)(2,1)S(1)}, u32[]{:S(2)}, u32[]{:S(2)}) collective-permute-start(bf16[1024,256]{1,0:T(8,128)(2,1)S(1)} %collective-permute-done.17.refs_14_), channel_id=1, source_target_pairs={{32,0},{33,1},{34,2},{35,3},{36,4},{37,5},{38,6},{39,7},{40,8},{41... | collective-permute-start | bytes 1572872 | tf_op jit(solution)/shard_map/ppermute | solution.py:27
  62.3 19.8 %collective-permute-start.16 = (bf16[1024,256]{1,0:T(8,128)(2,1)S(1)}, bf16[1024,256]{1,0:T(8,128)(2,1)S(1)}, u32[]{:S(2)}, u32[]{:S(2)}) collective-permute-start(bf16[1024,256]{1,0:T(8,128)(2,1)S(1)} %collective-permute-done.15.refs_12_), channel_id=1, source_target_pairs={{32,0},{33,1},{34,2},{35,3},{36,4},{37,5},{38,6},{39,7},{40,8},{41... | collective-permute-start | bytes 1572872 | tf_op jit(solution)/shard_map/ppermute | solution.py:27
  101.4 15.4 %copy-start.2 = (bf16[640,256]{1,0:T(8,128)(2,1)S(1)}, bf16[640,256]{1,0:T(8,128)(2,1)}, u32[]{:S(2)}) copy-start(bf16[640,256]{1,0:T(8,128)(2,1)} %param.12) | copy-start | bytes 983044
  101.4 15.4 %copy-start.5 = (f32[640]{0:T(1024)S(1)}, f32[640]{0:T(1024)}, u32[]{:S(2)}) copy-start(f32[640]{0:T(1024)} %param.16) | copy-start | bytes 7684
  103.2 13.6 %all-to-all-start.1 = ((bf16[32,20,256]{2,1,0:T(8,128)(2,1)}), bf16[32,20,256]{2,1,0:T(8,128)(2,1)S(1)}, u32[]{:S(2)}, u32[]{:S(2)}) async-start(bf16[32,20,256]{2,1,0:T(8,128)(2,1)} %reorder.1), calls=%async_computation.1 | async-start | bytes 786432 | tf_op jit(solution)/shard_map/all_to_all | solution.py:216
  (5 other events, 21.9 us)

commit v4 on v3

--- a/solution.py
+++ b/solution.py
@@ -47,36 +47,48 @@
     return send(value, lambda zh, core, x, y, zl: (zh, core, x + by * core, y + by * (1 - core), zl))
 
 
-def gather_amplitudes(own):
-    block = jnp.stack([own] + [minor(own, d) for d in (1, 2, 3)])
+def tie(*values):
+    return lax.optimization_barrier(values)
+
+
+def gather(left, panel):
+    other = swap(panel)
+    first, second, flips = [panel], [other], []
+
+    def advance():
+        first.append(ring(first[-1]))
+        flips.append(swap(first[-1]))
+        if len(second) < ZH:
+            second.append(ring(second[-1]))
+            flips.append(swap(second[-1]))
+
+    left, second[0] = tie(left, second[0])
+    advance()
+    block = jnp.stack([left] + [minor(left, d) for d in (1, 2, 3)])
+    block, first[1], second[1] = tie(block, first[1], second[1])
     ahead, behind = major(block, 1), major(block, 3)
+    advance()
+    advance()
+    ahead, behind, first[2], second[2] = tie(ahead, behind, first[2], second[2])
     far = [major(ahead[:2], 1), major(behind[2:], 3)]
-    return [block, ahead, behind] + far, [(d, e) for d in (0, 1, 3, 2) for e in range(4)]
-
-
-def gather_panel(own):
-    near, late = [(own, (0, 0))], []
-    other = swap(own)
-    near.append((other, (0, 1)))
-    first, second = own, other
-    for d in (1, 2, 3, 4):
-        out = near if d < 3 else late
-        first = ring(first)
-        out += [(first, (d, 0)), (swap(first), (-d, 1))]
-        if d < 4:
-            second = ring(second)
-            out += [(second, (d, 1)), (swap(second), (-d, 0))]
-    return near, late
-
-
-def ladder_kernel(more, last, count, *refs):
+    advance()
+    return [block, ahead, behind] + far, first + second + flips
+
+
+def amplitude_steps():
+    return [(d, e) for d in (0, 1, 3, 2) for e in range(4)]
+
+
+def panel_steps():
+    steps = [(d, 0) for d in range(5)] + [(d, 1) for d in range(4)]
+    return steps + [(-d, flip) for d in (1, 2, 3) for flip in (1, 0)] + [(-4, 1)]
+
+
+def ladder_kernel(count, *refs):
     line_ref, first_ref, part_ref, place_ref, screen_ref = refs[:5]
     blocks, refs = refs[5:10], refs[10:]
     panels, refs = refs[:count], refs[count:]
-    if more:
-        before, refs = refs[0], refs[1:]
-    out_ref, left_ref, held, left_sem, sems = refs[:5]
-    total = refs[5] if last else out_ref
+    out_ref, left_ref, held, total, left_sem, sems = refs
     depth, width = held.shape[1:]
     rows = left_ref.shape[1]
     tiles = place_ref.shape[0]
@@ -90,10 +102,7 @@
     fetch = [pltpu.make_async_copy(panel, held.at[g], sems.at[g]) for g, panel in enumerate(panels)]
     for c in copies + fetch:
         c.start()
-    if more:
-        total[...] = before[...]
-    else:
-        total[...] = jnp.zeros_like(total)
+    total[...] = jnp.zeros_like(total)
     for c in copies:
         c.wait()
 
@@ -119,43 +128,38 @@
                 preferred_element_type=jnp.float32,
             )
 
-    if last:
-        chunks, piece, _ = out_ref.shape
-        for i in range(total.shape[0] * total.shape[1]):
-            for c in range(chunks):
-                strip = total[i // 2, i % 2, c * piece : (c + 1) * piece, :]
-                out_ref[c, :, i * TILE : (i + 1) * TILE] = strip.astype(out_ref.dtype)
-
-
-def ladder(line, where, place, screen, blocks, panels, before, last):
+    chunks, piece, _ = out_ref.shape
+    for i in range(total.shape[0] * total.shape[1]):
+        for c in range(chunks):
+            strip = total[i // 2, i % 2, c * piece : (c + 1) * piece, :]
+            out_ref[c, :, i * TILE : (i + 1) * TILE] = strip.astype(out_ref.dtype)
+
+
+def ladder(line, where, place, screen, blocks, panels):
     depth, width = panels[0].shape
     rows = blocks[0].shape[1]
     count, pieces = len(panels), sum(b.shape[0] for b in blocks)
-    sums = (ZL, width // TILE, rows, TILE)
     chunks = NX * NY
-    more = before is not None
     return pl.pallas_call(
-        functools.partial(ladder_kernel, more, last, count),
-        out_shape=jax.ShapeDtypeStruct((chunks, rows // chunks, ZL * width), jnp.bfloat16)
-        if last
-        else jax.ShapeDtypeStruct(sums, jnp.float32),
-        in_specs=[SMEM] * 5 + [HBM] * (len(blocks) + count) + [VMEM] * more,
+        functools.partial(ladder_kernel, count),
+        out_shape=jax.ShapeDtypeStruct((chunks, rows // chunks, ZL * width), jnp.bfloat16),
+        in_specs=[SMEM] * 5 + [HBM] * (len(blocks) + count),
         out_specs=VMEM,
         scratch_shapes=[
             pltpu.VMEM((pieces,) + blocks[0].shape[1:], jnp.bfloat16),
             pltpu.VMEM((count, depth, width), jnp.bfloat16),
+            pltpu.VMEM((ZL, width // TILE, rows, TILE), jnp.float32),
             pltpu.SemaphoreType.DMA((len(blocks),)),
             pltpu.SemaphoreType.DMA((count,)),
-        ]
-        + [pltpu.VMEM(sums, jnp.float32)] * last,
-        compiler_params=pltpu.CompilerParams(vmem_limit_bytes=50 << 20),
+        ],
+        compiler_params=pltpu.CompilerParams(vmem_limit_bytes=40 << 20),
         cost_estimate=pl.CostEstimate(
-            flops=4 * rows * width * count * depth,
-            bytes_accessed=(2 * rows + width) * count * depth * 2,
+            flops=2 * rows * width * count * depth,
+            bytes_accessed=(rows + width) * count * depth * 2,
             transcendentals=0,
         ),
         name="ladder",
-    )(line, *where, place, screen, *blocks, *panels, *([before] if more else []))
+    )(line, *where, place, screen, *blocks, *panels)
 
 
 def reorder_kernel(owner_ref, src_ref, dst_ref):
@@ -191,10 +195,9 @@
     mine = lax.dynamic_slice_in_dim(amplitudes, zl * half, half, 0)
     other = lax.dynamic_slice_in_dim(amplitudes, (1 - zl) * half, half, 0)
     other = send(other, lambda zh, core, x, y, zl: (zh, core, x, y, 1 - zl))
-    blocks, order = gather_amplitudes(jnp.concatenate([mine, other], axis=1))
-    near, late = gather_panel(integrals)
-
-    far, close = (jnp.array(v, jnp.int32) for v in zip(*order))
+    blocks, panels = gather(jnp.concatenate([mine, other], axis=1), integrals)
+
+    far, close = (jnp.array(v, jnp.int32) for v in zip(*amplitude_steps()))
     dx, dy = jnp.where(core == 0, close, far), jnp.where(core == 0, far, close)
     device = (((x + dx) % NX) * NY + (y + dy) % NY)[:, None] * ZL + (zl ^ jnp.arange(ZL, dtype=jnp.int32))
     slots = (2 * device[:, :, None] + jnp.arange(2, dtype=jnp.int32)).reshape(-1)
@@ -203,14 +206,11 @@
 
     screen = lax.dynamic_slice_in_dim(screening, zl * (half // PBLK), half // PBLK, 0)
     screen = screen.astype(jnp.float32).reshape(-1)
-    found = None
-    for last, group in ((False, near), (True, late)):
-        panels, marks = zip(*group)
-        step, flip = (jnp.array(v, jnp.int32) for v in zip(*marks))
-        chip = (zh * ZL + zl + step * (2 * core - 1)) % (ZH * ZL)
-        first = (chip // ZL * CORE + (core ^ flip)) * (integrals.shape[0] // TILE)
-        where = (first.astype(jnp.int32), (chip % ZL).astype(jnp.int32))
-        found = ladder(jnp.stack([line]).astype(jnp.int32), where, place, screen, blocks, panels, found, last)
+    step, flip = (jnp.array(v, jnp.int32) for v in zip(*panel_steps()))
+    chip = (zh * ZL + zl + step * (2 * core - 1)) % (ZH * ZL)
+    first = (chip // ZL * CORE + (core ^ flip)) * (integrals.shape[0] // TILE)
+    where = (first.astype(jnp.int32), (chip % ZL).astype(jnp.int32))
+    found = ladder(jnp.stack([line]).astype(jnp.int32), where, place, screen, blocks, panels)
     spread = lax.all_to_all(found, ("x", "y"), 0, 0, tiled=True)
     sent = reorder(tile_owner, spread)
     total = lax.all_to_all(sent, ("zl", "x", "y"), 0, 0, tiled=True)

time: 118 us -> 112 us (0.949)
  Pallas kernels: 20 us -> 13.7 us
  waiting for transfers between devices: 38.9 us -> 44.9 us
  starting transfers between devices: 36 us -> 32.4 us
  local copies, waits for them, and re-layouts: 5.96 us -> 3.95 us
    pallas_call x2 -> x1, Pallas kernels: 18.2 us -> 12 us  [ladder(): pl.pallas_call(functools.partial(ladder_kernel, count), out_shape=jax.Sha...]
    ppermute x23, waiting for transfers between devices: 32.1 us -> 38 us  [send(): return lax.ppermute(value, AXES, pairs)]
    ppermute x23, starting transfers between devices: 31.9 us -> 27.3 us  [send(): return lax.ppermute(value, AXES, pairs)]
  transfers between devices with their start and end apart: 24 -> 24, of which waited for: 11 -> 11; matrix products, arithmetic and copies ran while one was open for 6% -> 5% of each run, Pallas kernels for 9% -> 0%
where the time goes in v4:
time: 112 us; the launch traced here: 111 us
  waiting for transfers between devices  44.9 us (40%)
  starting transfers between devices  32.4 us (29%)
  Pallas kernels  13.7 us (12%)
  blocking collectives  12.5 us (11%)
  local copies, waits for them, and re-layouts  3.95 us (4%)
  other arithmetic  2.5 us (2%)
  between operations  1.57 us (1%)
    ppermute x23, waiting for transfers between devices, send(): return lax.ppermute(value, AXES, pairs)  38 us
    ppermute x23, starting transfers between devices, send(): return lax.ppermute(value, AXES, pairs)  27.3 us
    all_to_all x1, blocking collectives, local(): spread = lax.all_to_all(found, ('x', 'y'), 0, 0, tiled=True)  12.5 us
    pallas_call x1, Pallas kernels, ladder(): pl.pallas_call(functools.partial(ladder_kernel, count), out_shape=jax.Sha...  12 us
    all_to_all x1, waiting for transfers between devices, local(): total = lax.all_to_all(sent, ('zl', 'x', 'y'), 0, 0, tiled=True)  6.9 us
    all_to_all x1, starting transfers between devices, local(): total = lax.all_to_all(sent, ('zl', 'x', 'y'), 0, 0, tiled=True)  5.07 us
  transfers between devices with their start and end apart: 24, of which 11 were waited for; matrix products, arithmetic and copies ran while one was open for 5% of the time, Pallas kernels for 0%

profile of v4, /device:TPU:64, one launch (start us, length us, event | category | flops | bytes accessed | tf_op | source)
XLA Modules:
  0.0 111.5 jit_solution(11169334896501033684)
XLA Ops:
  0.0 1.0 constant_dynamic-slice_fusion.1
  1.0 2.0 %collective-permute-start = (bf16[320,256]{1,0:T(8,128)(2,1)S(1)}, bf16[320,256]{1,0:T(8,128)(2,1)S(1)}, u32[]{:S(2)}, u32[]{:S(2)}) collective-permute-start(bf16[320,256]{1,0:T(8,128)(2,1)S(1)} %get-tuple-element.26), channel_id=1, source_target_pairs={{1,0},{0,1},{3,2},{2,3},{5,4},{4,5},{7,6},{6,7},{9,8},{8,9},{11,10... | collective-permute-start | bytes 491528 | tf_op jit(solution)/shard_map/ppermute | solution.py:27
  3.1 5.0 %collective-permute-done = bf16[320,256]{1,0:T(8,128)(2,1)S(1)} collective-permute-done((bf16[320,256]{1,0:T(8,128)(2,1)S(1)}, bf16[320,256]{1,0:T(8,128)(2,1)S(1)}, u32[]{:S(2)}, u32[]{:S(2)}) %collective-permute-start) | collective-permute-done | bytes 163872 | tf_op jit(solution)/shard_map/ppermute | solution.py:27
  8.2 1.6 %collective-permute-start.6 = (bf16[1024,256]{1,0:T(8,128)(2,1)S(1)}, bf16[1024,256]{1,0:T(8,128)(2,1)}, u32[]{:S(2)}, u32[]{:S(2)}) collective-permute-start(bf16[1024,256]{1,0:T(8,128)(2,1)S(1)} %collective-permute-done.1.refs_15_), channel_id=1, source_target_pairs={{193,0},{0,1},{195,2},{2,3},{197,4},{4,5},{199,6},{6,7},{201,8},{8... | collective-permute-start | bytes 1572872 | tf_op jit(solution)/shard_map/ppermute | solution.py:27
  9.8 2.8 %collective-permute-start.2 = (bf16[320,512]{1,0:T(8,128)(2,1)S(1)}, bf16[320,512]{1,0:T(8,128)(2,1)S(1)}, u32[]{:S(2)}, u32[]{:S(2)}) collective-permute-start(bf16[320,512]{1,0:T(8,128)(2,1)S(1)} %pad_maximum_fusion.1), channel_id=1, source_target_pairs={{8,0},{9,1},{10,2},{11,3},{12,4},{13,5},{14,6},{15,7},{16,8},{17,9... | collective-permute-start | bytes 983048 | tf_op jit(solution)/shard_map/ppermute | solution.py:27
  12.5 0.8 collective-permute-start.3
  13.3 0.9 collective-permute-start.4
  14.2 6.5 %collective-permute-done.2 = bf16[320,512]{1,0:T(8,128)(2,1)S(1)} collective-permute-done((bf16[320,512]{1,0:T(8,128)(2,1)S(1)}, bf16[320,512]{1,0:T(8,128)(2,1)S(1)}, u32[]{:S(2)}, u32[]{:S(2)}) %collective-permute-start.2) | collective-permute-done | bytes 327712 | tf_op jit(solution)/shard_map/ppermute | solution.py:27
  20.7 0.5 collective-permute-done.3
  21.2 3.4 %collective-permute-done.4 = bf16[320,512]{1,0:T(8,128)(2,1)S(1)} collective-permute-done((bf16[320,512]{1,0:T(8,128)(2,1)S(1)}, bf16[320,512]{1,0:T(8,128)(2,1)S(1)}, u32[]{:S(2)}, u32[]{:S(2)}) %collective-permute-start.4) | collective-permute-done | bytes 327712 | tf_op jit(solution)/shard_map/ppermute | solution.py:27
  24.8 3.1 %collective-permute-start.7 = (bf16[4,320,512]{2,1,0:T(8,128)(2,1)S(1)}, bf16[4,320,512]{2,1,0:T(8,128)(2,1)S(1)}, u32[]{:S(2)}, u32[]{:S(2)}) collective-permute-start(bf16[4,320,512]{2,1,0:T(8,128)(2,1)S(1)} %pad_maximum_fusion.refs_5_), channel_id=1, source_target_pairs={{2,0},{3,1},{4,2},{5,3},{6,4},{7,5},{0,6},{1,7},{10,8},{11,9},{12,... | collective-permute-start | bytes 3932168 | tf_op jit(solution)/shard_map/ppermute | solution.py:27
  27.9 3.7 %collective-permute-start.9 = (bf16[1024,256]{1,0:T(8,128)(2,1)}, bf16[1024,256]{1,0:T(8,128)(2,1)}, u32[]{:S(2)}, u32[]{:S(2)}) collective-permute-start(bf16[1024,256]{1,0:T(8,128)(2,1)} %collective-permute-done.5.refs_11_), channel_id=1, source_target_pairs={{193,0},{0,1},{195,2},{2,3},{197,4},{4,5},{199,6},{6,7},{201,8},{8... | collective-permute-start | bytes 1572872 | tf_op jit(solution)/shard_map/ppermute | solution.py:27
  32.0 6.6 %collective-permute-done.9.refs_12_ = bf16[1024,256]{1,0:T(8,128)(2,1)} collective-permute-done((bf16[1024,256]{1,0:T(8,128)(2,1)}, bf16[1024,256]{1,0:T(8,128)(2,1)}, u32[]{:S(2)}, u32[]{:S(2)}) %collective-permute-start.9) | collective-permute-done | bytes 524320 | tf_op jit(solution)/shard_map/ppermute | solution.py:27
  38.7 2.5 %collective-permute-start.13 = (bf16[1024,256]{1,0:T(8,128)(2,1)}, bf16[1024,256]{1,0:T(8,128)(2,1)}, u32[]{:S(2)}, u32[]{:S(2)}) collective-permute-start(bf16[1024,256]{1,0:T(8,128)(2,1)} %collective-permute-done.9.refs_12_), channel_id=1, source_target_pairs={{193,0},{0,1},{195,2},{2,3},{197,4},{4,5},{199,6},{6,7},{201,8},{8... | collective-permute-start | bytes 1572872 | tf_op jit(solution)/shard_map/ppermute | solution.py:27
  41.1 0.9 dynamic-slice_convert_fusion
  42.3 1.9 %collective-permute-done.10.refs_17_ = bf16[1024,256]{1,0:T(8,128)(2,1)} collective-permute-done((bf16[1024,256]{1,0:T(8,128)(2,1)}, bf16[1024,256]{1,0:T(8,128)(2,1)}, u32[]{:S(2)}, u32[]{:S(2)}) %collective-permute-start.10) | collective-permute-done | bytes 524320 | tf_op jit(solution)/shard_map/ppermute | solution.py:27
  44.3 2.5 %collective-permute-start.15 = (bf16[1024,256]{1,0:T(8,128)(2,1)}, bf16[1024,256]{1,0:T(8,128)(2,1)}, u32[]{:S(2)}, u32[]{:S(2)}) collective-permute-start(bf16[1024,256]{1,0:T(8,128)(2,1)} %collective-permute-done.10.refs_17_), channel_id=1, source_target_pairs={{193,0},{0,1},{195,2},{2,3},{197,4},{4,5},{199,6},{6,7},{201,8},{8... | collective-permute-start | bytes 1572872 | tf_op jit(solution)/shard_map/ppermute | solution.py:27
  46.8 3.1 %collective-permute-done.13.refs_13_ = bf16[1024,256]{1,0:T(8,128)(2,1)} collective-permute-done((bf16[1024,256]{1,0:T(8,128)(2,1)}, bf16[1024,256]{1,0:T(8,128)(2,1)}, u32[]{:S(2)}, u32[]{:S(2)}) %collective-permute-start.13) | collective-permute-done | bytes 524320 | tf_op jit(solution)/shard_map/ppermute | solution.py:27
  50.4 2.5 %collective-permute-start.14 = (bf16[1024,256]{1,0:T(8,128)(2,1)}, bf16[1024,256]{1,0:T(8,128)(2,1)}, u32[]{:S(2)}, u32[]{:S(2)}) collective-permute-start(bf16[1024,256]{1,0:T(8,128)(2,1)} %collective-permute-done.13.refs_13_), channel_id=1, source_target_pairs={{193,0},{0,1},{195,2},{2,3},{197,4},{4,5},{199,6},{6,7},{201,8},{8... | collective-permute-start | bytes 1572872 | tf_op jit(solution)/shard_map/ppermute | solution.py:27
  53.3 1.2 %slice.7 = bf16[2,320,512]{2,1,0:T(8,128)(2,1)S(1)} slice(bf16[4,320,512]{2,1,0:T(8,128)(2,1)} %collective-permute-done.8.refs_7_), slice={[2:4], [0:320], [0:512]} | slice | bytes 1310720 | tf_op jit(solution)/shard_map/slice | solution.py:73
  54.5 3.3 %collective-permute-start.11 = (bf16[2,320,512]{2,1,0:T(8,128)(2,1)S(1)}, bf16[2,320,512]{2,1,0:T(8,128)(2,1)S(1)}, u32[]{:S(2)}, u32[]{:S(2)}) collective-permute-start(bf16[2,320,512]{2,1,0:T(8,128)(2,1)S(1)} %slice.6), channel_id=1, source_target_pairs={{2,0},{3,1},{4,2},{5,3},{6,4},{7,5},{0,6},{1,7},{10,8},{11,9},{12,... | collective-permute-start | bytes 1966088 | tf_op jit(solution)/shard_map/ppermute | solution.py:27
  58.6 2.5 %collective-permute-done.14.refs_14_ = bf16[1024,256]{1,0:T(8,128)(2,1)} collective-permute-done((bf16[1024,256]{1,0:T(8,128)(2,1)}, bf16[1024,256]{1,0:T(8,128)(2,1)}, u32[]{:S(2)}, u32[]{:S(2)}) %collective-permute-start.14) | collective-permute-done | bytes 524320 | tf_op jit(solution)/shard_map/ppermute | solution.py:27
  61.3 4.6 %collective-permute-done.11.refs_8_ = bf16[2,320,512]{2,1,0:T(8,128)(2,1)S(1)} collective-permute-done((bf16[2,320,512]{2,1,0:T(8,128)(2,1)S(1)}, bf16[2,320,512]{2,1,0:T(8,128)(2,1)S(1)}, u32[]{:S(2)}, u32[]{:S(2)}) %collective-permute-start.11) | collective-permute-done | bytes 655392 | tf_op jit(solution)/shard_map/ppermute | solution.py:27
  65.9 3.7 %collective-permute-done.12.refs_9_ = bf16[2,320,512]{2,1,0:T(8,128)(2,1)S(1)} collective-permute-done((bf16[2,320,512]{2,1,0:T(8,128)(2,1)S(1)}, bf16[2,320,512]{2,1,0:T(8,128)(2,1)S(1)}, u32[]{:S(2)}, u32[]{:S(2)}) %collective-permute-start.12) | collective-permute-done | bytes 655392 | tf_op jit(solution)/shard_map/ppermute | solution.py:27
  69.6 12.0 %ladder.1 = bf16[16,20,512]{2,1,0:T(8,128)(2,1)S(1)} custom-call(s32[1]{0:T(128)} %bitcast.refs_0_, s32[16]{0:T(128)S(1)} %add_multiply_fusion.1.refs_1_, s32[16]{0:T(128)S(1)} %get-tuple-element.23.refs_2_, s32[64]{0:T(128)S(1)} %select_reduce_fusion.refs_3_, f32[20480]{0:T(1024)S(1)} %reshape.63.refs_4_, bf16[4,320,512]{2,1,0:T(8,128)(2,1)S(1)} %pad_maximum_fusion.refs_5_, ...), custom_call_target="tpu_custom_call" | custom-call | flops 2684354560 | bytes 18874368 | tf_op jit(solution)/shard_map/ladder/pallas_call | solution.py:143
  81.6 12.5 %all_to_all.10.src_ref = bf16[16,20,512]{2,1,0:T(8,128)(2,1)S(1)} all-to-all(bf16[16,20,512]{2,1,0:T(8,128)(2,1)S(1)} %ladder.1), channel_id=1, replica_groups=mesh['zh'=4,'core'=2,'x'=4,'y'=4,'zl'=2] {'x','y'}, dimensions={0} | all-to-all | bytes 655360 | tf_op jit(solution)/shard_map/all_to_all | solution.py:214
  94.1 1.7 %reorder.1 = bf16[32,20,256]{2,1,0:T(8,128)(2,1)} custom-call(s32[64]{0:T(128)S(1)} %copy-done.1, bf16[16,20,512]{2,1,0:T(8,128)(2,1)S(1)} %all_to_all.10.src_ref), custom_call_target="tpu_custom_call" | custom-call | bytes 1048576 | tf_op jit(solution)/shard_map/reorder/pallas_call | solution.py:176
  95.8 5.1 %all-to-all-start.1 = ((bf16[32,20,256]{2,1,0:T(8,128)(2,1)}), bf16[32,20,256]{2,1,0:T(8,128)(2,1)S(1)}, u32[]{:S(2)}, u32[]{:S(2)}) async-start(bf16[32,20,256]{2,1,0:T(8,128)(2,1)} %reorder.1), calls=%async_computation.1 | async-start | bytes 786432 | tf_op jit(solution)/shard_map/all_to_all | solution.py:216
  100.9 0.6 fusion.9
  102.8 0.8 fusion.8
  103.6 6.9 %all-to-all-done.1 = bf16[32,20,256]{2,1,0:T(8,128)(2,1)S(1)} async-done(((bf16[32,20,256]{2,1,0:T(8,128)(2,1)}), bf16[32,20,256]{2,1,0:T(8,128)(2,1)S(1)}, u32[]{:S(2)}, u32[]{:S(2)}) %all-to-all-start.1) | async-done | bytes 327712 | tf_op jit(solution)/shard_map/all_to_all | solution.py:216
  110.6 0.9 add_convert_fusion
  (56 shorter events, 2.7 us)
Async XLA Ops:
  0.0 8.2 %collective-permute-start.1 = (bf16[1024,256]{1,0:T(8,128)(2,1)}, bf16[1024,256]{1,0:T(8,128)(2,1)S(1)}, u32[]{:S(2)}, u32[]{:S(2)}) collective-permute-start(bf16[1024,256]{1,0:T(8,128)(2,1)} %refs_10_.1), channel_id=1, source_target_pairs={{32,0},{33,1},{34,2},{35,3},{36,4},{37,5},{38,6},{39,7},{40,8},{41... | collective-permute-start | bytes 1572872 | tf_op jit(solution)/shard_map/ppermute | solution.py:27
  1.0 7.2 %collective-permute-start = (bf16[320,256]{1,0:T(8,128)(2,1)S(1)}, bf16[320,256]{1,0:T(8,128)(2,1)S(1)}, u32[]{:S(2)}, u32[]{:S(2)}) collective-permute-start(bf16[320,256]{1,0:T(8,128)(2,1)S(1)} %get-tuple-element.26), channel_id=1, source_target_pairs={{1,0},{0,1},{3,2},{2,3},{5,4},{4,5},{7,6},{6,7},{9,8},{8,9},{11,10... | collective-permute-start | bytes 491528 | tf_op jit(solution)/shard_map/ppermute | solution.py:27
  3.0 21.8 %collective-permute-start.5 = (bf16[1024,256]{1,0:T(8,128)(2,1)}, bf16[1024,256]{1,0:T(8,128)(2,1)}, u32[]{:S(2)}, u32[]{:S(2)}) collective-permute-start(bf16[1024,256]{1,0:T(8,128)(2,1)} %refs_10_.1), channel_id=1, source_target_pairs={{193,0},{0,1},{195,2},{2,3},{197,4},{4,5},{199,6},{6,7},{201,8},{8... | collective-permute-start | bytes 1572872 | tf_op jit(solution)/shard_map/ppermute | solution.py:27
  8.2 16.6 %collective-permute-start.6 = (bf16[1024,256]{1,0:T(8,128)(2,1)S(1)}, bf16[1024,256]{1,0:T(8,128)(2,1)}, u32[]{:S(2)}, u32[]{:S(2)}) collective-permute-start(bf16[1024,256]{1,0:T(8,128)(2,1)S(1)} %collective-permute-done.1.refs_15_), channel_id=1, source_target_pairs={{193,0},{0,1},{195,2},{2,3},{197,4},{4,5},{199,6},{6,7},{201,8},{8... | collective-permute-start | bytes 1572872 | tf_op jit(solution)/shard_map/ppermute | solution.py:27
  9.8 10.9 %collective-permute-start.2 = (bf16[320,512]{1,0:T(8,128)(2,1)S(1)}, bf16[320,512]{1,0:T(8,128)(2,1)S(1)}, u32[]{:S(2)}, u32[]{:S(2)}) collective-permute-start(bf16[320,512]{1,0:T(8,128)(2,1)S(1)} %pad_maximum_fusion.1), channel_id=1, source_target_pairs={{8,0},{9,1},{10,2},{11,3},{12,4},{13,5},{14,6},{15,7},{16,8},{17,9... | collective-permute-start | bytes 983048 | tf_op jit(solution)/shard_map/ppermute | solution.py:27
  12.5 8.7 %collective-permute-start.3 = (bf16[320,512]{1,0:T(8,128)(2,1)S(1)}, bf16[320,512]{1,0:T(8,128)(2,1)S(1)}, u32[]{:S(2)}, u32[]{:S(2)}) collective-permute-start(bf16[320,512]{1,0:T(8,128)(2,1)S(1)} %pad_maximum_fusion.1), channel_id=1, source_target_pairs={{16,0},{17,1},{18,2},{19,3},{20,4},{21,5},{22,6},{23,7},{24,8},{25... | collective-permute-start | bytes 983048 | tf_op jit(solution)/shard_map/ppermute | solution.py:27
  13.3 11.3 %collective-permute-start.4 = (bf16[320,512]{1,0:T(8,128)(2,1)S(1)}, bf16[320,512]{1,0:T(8,128)(2,1)S(1)}, u32[]{:S(2)}, u32[]{:S(2)}) collective-permute-start(bf16[320,512]{1,0:T(8,128)(2,1)S(1)} %pad_maximum_fusion.1), channel_id=1, source_target_pairs={{24,0},{25,1},{26,2},{27,3},{28,4},{29,5},{30,6},{31,7},{0,8},{1,9... | collective-permute-start | bytes 983048 | tf_op jit(solution)/shard_map/ppermute | solution.py:27
  24.6 17.5 %copy-start.6 = (s32[16]{0:T(128)S(1)}, s32[16]{0:T(128)}, u32[]{:S(2)}) copy-start(s32[16]{0:T(128)} %constant.106.clone) | copy-start | bytes 196
  24.6 17.6 %copy-start.7 = (s32[16]{0:T(128)S(1)}, s32[16]{0:T(128)}, u32[]{:S(2)}) copy-start(s32[16]{0:T(128)} %constant.107.clone) | copy-start | bytes 196
  24.8 25.1 %collective-permute-start.7 = (bf16[4,320,512]{2,1,0:T(8,128)(2,1)S(1)}, bf16[4,320,512]{2,1,0:T(8,128)(2,1)S(1)}, u32[]{:S(2)}, u32[]{:S(2)}) collective-permute-start(bf16[4,320,512]{2,1,0:T(8,128)(2,1)S(1)} %pad_maximum_fusion.refs_5_), channel_id=1, source_target_pairs={{2,0},{3,1},{4,2},{5,3},{6,4},{7,5},{0,6},{1,7},{10,8},{11,9},{12,... | collective-permute-start | bytes 3932168 | tf_op jit(solution)/shard_map/ppermute | solution.py:27
  27.9 22.5 %collective-permute-start.8 = (bf16[4,320,512]{2,1,0:T(8,128)(2,1)S(1)}, bf16[4,320,512]{2,1,0:T(8,128)(2,1)}, u32[]{:S(2)}, u32[]{:S(2)}) collective-permute-start(bf16[4,320,512]{2,1,0:T(8,128)(2,1)S(1)} %pad_maximum_fusion.refs_5_), channel_id=1, source_target_pairs={{6,0},{7,1},{0,2},{1,3},{2,4},{3,5},{4,6},{5,7},{14,8},{15,9},{8,1... | collective-permute-start | bytes 3932168 | tf_op jit(solution)/shard_map/ppermute | solution.py:27
  27.9 10.7 %collective-permute-start.9 = (bf16[1024,256]{1,0:T(8,128)(2,1)}, bf16[1024,256]{1,0:T(8,128)(2,1)}, u32[]{:S(2)}, u32[]{:S(2)}) collective-permute-start(bf16[1024,256]{1,0:T(8,128)(2,1)} %collective-permute-done.5.refs_11_), channel_id=1, source_target_pairs={{193,0},{0,1},{195,2},{2,3},{197,4},{4,5},{199,6},{6,7},{201,8},{8... | collective-permute-start | bytes 1572872 | tf_op jit(solution)/shard_map/ppermute | solution.py:27
  31.6 10.6 %collective-permute-start.16 = (bf16[1024,256]{1,0:T(8,128)(2,1)}, bf16[1024,256]{1,0:T(8,128)(2,1)}, u32[]{:S(2)}, u32[]{:S(2)}) collective-permute-start(bf16[1024,256]{1,0:T(8,128)(2,1)} %collective-permute-done.5.refs_11_), channel_id=1, source_target_pairs={{32,0},{33,1},{34,2},{35,3},{36,4},{37,5},{38,6},{39,7},{40,8},{41... | collective-permute-start | bytes 1572872 | tf_op jit(solution)/shard_map/ppermute | solution.py:27
  31.6 12.6 %collective-permute-start.10 = (bf16[1024,256]{1,0:T(8,128)(2,1)}, bf16[1024,256]{1,0:T(8,128)(2,1)}, u32[]{:S(2)}, u32[]{:S(2)}) collective-permute-start(bf16[1024,256]{1,0:T(8,128)(2,1)} %collective-permute-done.6.refs_16_), channel_id=1, source_target_pairs={{193,0},{0,1},{195,2},{2,3},{197,4},{4,5},{199,6},{6,7},{201,8},{8... | collective-permute-start | bytes 1572872 | tf_op jit(solution)/shard_map/ppermute | solution.py:27
  38.7 11.2 %collective-permute-start.13 = (bf16[1024,256]{1,0:T(8,128)(2,1)}, bf16[1024,256]{1,0:T(8,128)(2,1)}, u32[]{:S(2)}, u32[]{:S(2)}) collective-permute-start(bf16[1024,256]{1,0:T(8,128)(2,1)} %collective-permute-done.9.refs_12_), channel_id=1, source_target_pairs={{193,0},{0,1},{195,2},{2,3},{197,4},{4,5},{199,6},{6,7},{201,8},{8... | collective-permute-start | bytes 1572872 | tf_op jit(solution)/shard_map/ppermute | solution.py:27
  42.2 12.2 %collective-permute-start.17 = (bf16[1024,256]{1,0:T(8,128)(2,1)}, bf16[1024,256]{1,0:T(8,128)(2,1)}, u32[]{:S(2)}, u32[]{:S(2)}) collective-permute-start(bf16[1024,256]{1,0:T(8,128)(2,1)} %collective-permute-done.6.refs_16_), channel_id=1, source_target_pairs={{32,0},{33,1},{34,2},{35,3},{36,4},{37,5},{38,6},{39,7},{40,8},{41... | collective-permute-start | bytes 1572872 | tf_op jit(solution)/shard_map/ppermute | solution.py:27
  44.3 13.5 %collective-permute-start.15 = (bf16[1024,256]{1,0:T(8,128)(2,1)}, bf16[1024,256]{1,0:T(8,128)(2,1)}, u32[]{:S(2)}, u32[]{:S(2)}) collective-permute-start(bf16[1024,256]{1,0:T(8,128)(2,1)} %collective-permute-done.10.refs_17_), channel_id=1, source_target_pairs={{193,0},{0,1},{195,2},{2,3},{197,4},{4,5},{199,6},{6,7},{201,8},{8... | collective-permute-start | bytes 1572872 | tf_op jit(solution)/shard_map/ppermute | solution.py:27
  49.9 8.1 %collective-permute-start.18 = (bf16[1024,256]{1,0:T(8,128)(2,1)}, bf16[1024,256]{1,0:T(8,128)(2,1)}, u32[]{:S(2)}, u32[]{:S(2)}) collective-permute-start(bf16[1024,256]{1,0:T(8,128)(2,1)} %collective-permute-done.9.refs_12_), channel_id=1, source_target_pairs={{32,0},{33,1},{34,2},{35,3},{36,4},{37,5},{38,6},{39,7},{40,8},{41... | collective-permute-start | bytes 1572872 | tf_op jit(solution)/shard_map/ppermute | solution.py:27
  49.9 8.2 %collective-permute-start.19 = (bf16[1024,256]{1,0:T(8,128)(2,1)}, bf16[1024,256]{1,0:T(8,128)(2,1)}, u32[]{:S(2)}, u32[]{:S(2)}) collective-permute-start(bf16[1024,256]{1,0:T(8,128)(2,1)} %collective-permute-done.10.refs_17_), channel_id=1, source_target_pairs={{32,0},{33,1},{34,2},{35,3},{36,4},{37,5},{38,6},{39,7},{40,8},{41... | collective-permute-start | bytes 1572872 | tf_op jit(solution)/shard_map/ppermute | solution.py:27
  50.4 10.7 %collective-permute-start.14 = (bf16[1024,256]{1,0:T(8,128)(2,1)}, bf16[1024,256]{1,0:T(8,128)(2,1)}, u32[]{:S(2)}, u32[]{:S(2)}) collective-permute-start(bf16[1024,256]{1,0:T(8,128)(2,1)} %collective-permute-done.13.refs_13_), channel_id=1, source_target_pairs={{193,0},{0,1},{195,2},{2,3},{197,4},{4,5},{199,6},{6,7},{201,8},{8... | collective-permute-start | bytes 1572872 | tf_op jit(solution)/shard_map/ppermute | solution.py:27
  53.2 4.6 %copy-start.1 = (s32[64]{0:T(128)S(1)}, s32[64]{0:T(128)}, u32[]{:S(2)}) copy-start(s32[64]{0:T(128)} %owner_ref.1) | copy-start | bytes 772
  53.2 8.0 %copy-start.4 = (s32[16]{0:T(128)S(1)}, s32[16]{0:T(128)}, u32[]{:S(2)}) copy-start(s32[16]{0:T(128)} %constant.108.clone) | copy-start | bytes 196
  53.2 8.0 %copy-start.5 = (s32[16]{0:T(128)S(1)}, s32[16]{0:T(128)}, u32[]{:S(2)}) copy-start(s32[16]{0:T(128)} %constant.109.clone) | copy-start | bytes 196
  53.2 16.4 %copy-start = (bf16[1024,256]{1,0:T(8,128)(2,1)S(1)}, bf16[1024,256]{1,0:T(8,128)(2,1)}, u32[]{:S(2)}) copy-start(bf16[1024,256]{1,0:T(8,128)(2,1)} %refs_10_.1) | copy-start | bytes 1572868
  54.5 11.4 %collective-permute-start.11 = (bf16[2,320,512]{2,1,0:T(8,128)(2,1)S(1)}, bf16[2,320,512]{2,1,0:T(8,128)(2,1)S(1)}, u32[]{:S(2)}, u32[]{:S(2)}) collective-permute-start(bf16[2,320,512]{2,1,0:T(8,128)(2,1)S(1)} %slice.6), channel_id=1, source_target_pairs={{2,0},{3,1},{4,2},{5,3},{6,4},{7,5},{0,6},{1,7},{10,8},{11,9},{12,... | collective-permute-start | bytes 1966088 | tf_op jit(solution)/shard_map/ppermute | solution.py:27
  57.8 11.8 %collective-permute-start.12 = (bf16[2,320,512]{2,1,0:T(8,128)(2,1)S(1)}, bf16[2,320,512]{2,1,0:T(8,128)(2,1)S(1)}, u32[]{:S(2)}, u32[]{:S(2)}) collective-permute-start(bf16[2,320,512]{2,1,0:T(8,128)(2,1)S(1)} %slice.7), channel_id=1, source_target_pairs={{6,0},{7,1},{0,2},{1,3},{2,4},{3,5},{4,6},{5,7},{14,8},{15,9},{8,1... | collective-permute-start | bytes 1966088 | tf_op jit(solution)/shard_map/ppermute | solution.py:27
  58.0 3.3 %collective-permute-start.20 = (bf16[1024,256]{1,0:T(8,128)(2,1)}, bf16[1024,256]{1,0:T(8,128)(2,1)S(1)}, u32[]{:S(2)}, u32[]{:S(2)}) collective-permute-start(bf16[1024,256]{1,0:T(8,128)(2,1)} %collective-permute-done.13.refs_13_), channel_id=1, source_target_pairs={{32,0},{33,1},{34,2},{35,3},{36,4},{37,5},{38,6},{39,7},{40,8},{41... | collective-permute-start | bytes 1572872 | tf_op jit(solution)/shard_map/ppermute | solution.py:27
  58.1 3.2 %collective-permute-start.21 = (bf16[1024,256]{1,0:T(8,128)(2,1)}, bf16[1024,256]{1,0:T(8,128)(2,1)S(1)}, u32[]{:S(2)}, u32[]{:S(2)}) collective-permute-start(bf16[1024,256]{1,0:T(8,128)(2,1)} %collective-permute-done.15.refs_18_), channel_id=1, source_target_pairs={{32,0},{33,1},{34,2},{35,3},{36,4},{37,5},{38,6},{39,7},{40,8},{41... | collective-permute-start | bytes 1572872 | tf_op jit(solution)/shard_map/ppermute | solution.py:27
  61.1 8.5 %collective-permute-start.22 = (bf16[1024,256]{1,0:T(8,128)(2,1)}, bf16[1024,256]{1,0:T(8,128)(2,1)S(1)}, u32[]{:S(2)}, u32[]{:S(2)}) collective-permute-start(bf16[1024,256]{1,0:T(8,128)(2,1)} %collective-permute-done.14.refs_14_), channel_id=1, source_target_pairs={{32,0},{33,1},{34,2},{35,3},{36,4},{37,5},{38,6},{39,7},{40,8},{41... | collective-permute-start | bytes 1572872 | tf_op jit(solution)/shard_map/ppermute | solution.py:27
  94.1 16.5 %copy-start.2 = (bf16[640,256]{1,0:T(8,128)(2,1)S(1)}, bf16[640,256]{1,0:T(8,128)(2,1)}, u32[]{:S(2)}) copy-start(bf16[640,256]{1,0:T(8,128)(2,1)} %param.10) | copy-start | bytes 983044
  94.1 16.5 %copy-start.3 = (f32[640]{0:T(1024)S(1)}, f32[640]{0:T(1024)}, u32[]{:S(2)}) copy-start(f32[640]{0:T(1024)} %param.14) | copy-start | bytes 7684
  95.8 14.7 %all-to-all-start.1 = ((bf16[32,20,256]{2,1,0:T(8,128)(2,1)}), bf16[32,20,256]{2,1,0:T(8,128)(2,1)S(1)}, u32[]{:S(2)}, u32[]{:S(2)}) async-start(bf16[32,20,256]{2,1,0:T(8,128)(2,1)} %reorder.1), calls=%async_computation.1 | async-start | bytes 786432 | tf_op jit(solution)/shard_map/all_to_all | solution.py:216

commit v5 on v4

--- a/solution.py
+++ b/solution.py
@@ -63,20 +63,27 @@
             flips.append(swap(second[-1]))
 
     left, second[0] = tie(left, second[0])
-    advance()
-    block = jnp.stack([left] + [minor(left, d) for d in (1, 2, 3)])
-    block, first[1], second[1] = tie(block, first[1], second[1])
-    ahead, behind = major(block, 1), major(block, 3)
-    advance()
-    advance()
-    ahead, behind, first[2], second[2] = tie(ahead, behind, first[2], second[2])
-    far = [major(ahead[:2], 1), major(behind[2:], 3)]
-    advance()
-    return [block, ahead, behind] + far, first + second + flips
+    next1, next3, next2 = (minor(left, d) for d in (1, 3, 2))
+    advance()
+    near = jnp.stack([left, next1])
+    near, first[1] = tie(near, first[1])
+    near_ahead = major(near, 1)
+    advance()
+    rest = jnp.stack([next3, next2])
+    rest, first[2], second[1] = tie(rest, first[2], second[1])
+    rest_behind, rest_ahead, near_behind = major(rest, 3), major(rest, 1), major(near, 3)
+    advance()
+    near_ahead, second[2] = tie(near_ahead, second[2])
+    near_far = major(near_ahead, 1)
+    rest_behind, first[3] = tie(rest_behind, first[3])
+    rest_far = major(rest_behind, 3)
+    advance()
+    blocks = [near, rest, near_ahead, rest_ahead, near_behind, rest_behind, near_far, rest_far]
+    return blocks, first + second + flips
 
 
 def amplitude_steps():
-    return [(d, e) for d in (0, 1, 3, 2) for e in range(4)]
+    return [(d, e) for d in (0, 1, 3, 2) for e in (0, 1, 3, 2)]
 
 
 def panel_steps():
@@ -86,7 +93,7 @@
 
 def ladder_kernel(count, *refs):
     line_ref, first_ref, part_ref, place_ref, screen_ref = refs[:5]
-    blocks, refs = refs[5:10], refs[10:]
+    blocks, refs = refs[5:13], refs[13:]
     panels, refs = refs[:count], refs[count:]
     out_ref, left_ref, held, total, left_sem, sems = refs
     depth, width = held.shape[1:]

time: 112 us -> 116 us (1.036)
  waiting for transfers between devices: 44.9 us -> 31.2 us
  starting transfers between devices: 32.4 us -> 41.1 us
  local copies, waits for them, and re-layouts: 3.95 us -> 9.01 us
  blocking collectives: 12.5 us -> 15.5 us
    ppermute x23 -> x25, waiting for transfers between devices: 38 us -> 24.2 us  [send(): return lax.ppermute(value, AXES, pairs)]
    ppermute x23 -> x25, starting transfers between devices: 27.3 us -> 34.7 us  [send(): return lax.ppermute(value, AXES, pairs)]
    unnamed x16 -> x30, local copies, waits for them, and re-layouts: 0.04 us -> 6.3 us
    all_to_all x1, blocking collectives: 12.5 us -> 15.5 us  [local(): spread = lax.all_to_all(found, ('x', 'y'), 0, 0, tiled=True)]
    all_to_all x1, starting transfers between devices: 5.07 us -> 6.34 us  [local(): total = lax.all_to_all(sent, ('zl', 'x', 'y'), 0, 0, tiled=True)]
    slice x2 -> x0, local copies, waits for them, and re-layouts: 1.22 us -> none  [gather(): far = [major(ahead[:2], 1), major(behind[2:], 3)]]
  transfers between devices with their start and end apart: 24 -> 26, of which waited for: 11 -> 11; matrix products, arithmetic and copies ran while one was open for 5% -> 4% of each run, Pallas kernels for 0% -> 0%
where the time goes in v5:
time: 116 us; the launch traced here: 115 us
  starting transfers between devices  41.1 us (35%)
  waiting for transfers between devices  31.2 us (27%)
  blocking collectives  15.5 us (13%)
  Pallas kernels  14 us (12%)
  local copies, waits for them, and re-layouts  9.01 us (8%)
  other arithmetic  2.46 us (2%)
  between operations  1.48 us (1%)
    ppermute x25, starting transfers between devices, send(): return lax.ppermute(value, AXES, pairs)  34.7 us
    ppermute x25, waiting for transfers between devices, send(): return lax.ppermute(value, AXES, pairs)  24.2 us
    all_to_all x1, blocking collectives, local(): spread = lax.all_to_all(found, ('x', 'y'), 0, 0, tiled=True)  15.5 us
    pallas_call x1, Pallas kernels, ladder(): pl.pallas_call(functools.partial(ladder_kernel, count), out_shape=jax.Sha...  12.3 us
    all_to_all x1, waiting for transfers between devices, local(): total = lax.all_to_all(sent, ('zl', 'x', 'y'), 0, 0, tiled=True)  6.95 us
    all_to_all x1, starting transfers between devices, local(): total = lax.all_to_all(sent, ('zl', 'x', 'y'), 0, 0, tiled=True)  6.34 us
    unnamed x30, local copies, waits for them, and re-layouts  6.3 us
  transfers between devices with their start and end apart: 26, of which 11 were waited for; matrix products, arithmetic and copies ran while one was open for 4% of the time, Pallas kernels for 0%

profile of v5, /device:TPU:64, one launch (start us, length us, event | category | flops | bytes accessed | tf_op | source)
XLA Modules:
  0.0 114.7 jit_solution(3784792200848214184)
XLA Ops:
  0.0 1.1 constant_dynamic-slice_fusion.1
  1.1 2.0 %collective-permute-start = (bf16[320,256]{1,0:T(8,128)(2,1)S(1)}, bf16[320,256]{1,0:T(8,128)(2,1)S(1)}, u32[]{:S(2)}, u32[]{:S(2)}) collective-permute-start(bf16[320,256]{1,0:T(8,128)(2,1)S(1)} %get-tuple-element.30), channel_id=1, source_target_pairs={{1,0},{0,1},{3,2},{2,3},{5,4},{4,5},{7,6},{6,7},{9,8},{8,9},{11,10... | collective-permute-start | bytes 491528 | tf_op jit(solution)/shard_map/ppermute | solution.py:27
  3.2 5.0 %collective-permute-done = bf16[320,256]{1,0:T(8,128)(2,1)S(1)} collective-permute-done((bf16[320,256]{1,0:T(8,128)(2,1)S(1)}, bf16[320,256]{1,0:T(8,128)(2,1)S(1)}, u32[]{:S(2)}, u32[]{:S(2)}) %collective-permute-start) | collective-permute-done | bytes 163872 | tf_op jit(solution)/shard_map/ppermute | solution.py:27
  8.3 2.8 %collective-permute-start.2 = (bf16[320,512]{1,0:T(8,128)(2,1)S(1)}, bf16[320,512]{1,0:T(8,128)(2,1)S(1)}, u32[]{:S(2)}, u32[]{:S(2)}) collective-permute-start(bf16[320,512]{1,0:T(8,128)(2,1)S(1)} %pad_maximum_fusion.2), channel_id=1, source_target_pairs={{8,0},{9,1},{10,2},{11,3},{12,4},{13,5},{14,6},{15,7},{16,8},{17,9... | collective-permute-start | bytes 983048 | tf_op jit(solution)/shard_map/ppermute | solution.py:27
  11.1 1.4 %collective-permute-start.7 = (bf16[1024,256]{1,0:T(8,128)(2,1)S(1)}, bf16[1024,256]{1,0:T(8,128)(2,1)}, u32[]{:S(2)}, u32[]{:S(2)}) collective-permute-start(bf16[1024,256]{1,0:T(8,128)(2,1)S(1)} %collective-permute-done.1.refs_18_), channel_id=1, source_target_pairs={{193,0},{0,1},{195,2},{2,3},{197,4},{4,5},{199,6},{6,7},{201,8},{8... | collective-permute-start | bytes 1572872 | tf_op jit(solution)/shard_map/ppermute | solution.py:27
  12.5 3.2 %collective-permute-done.2 = bf16[320,512]{1,0:T(8,128)(2,1)S(1)} collective-permute-done((bf16[320,512]{1,0:T(8,128)(2,1)S(1)}, bf16[320,512]{1,0:T(8,128)(2,1)S(1)}, u32[]{:S(2)}, u32[]{:S(2)}) %collective-permute-start.2) | collective-permute-done | bytes 327712 | tf_op jit(solution)/shard_map/ppermute | solution.py:27
  15.8 1.5 %collective-permute-start.6 = (bf16[1024,256]{1,0:T(8,128)(2,1)S(1)}, bf16[1024,256]{1,0:T(8,128)(2,1)}, u32[]{:S(2)}, u32[]{:S(2)}) collective-permute-start(bf16[1024,256]{1,0:T(8,128)(2,1)S(1)} %collective-permute-done.3.refs_14_), channel_id=1, source_target_pairs={{193,0},{0,1},{195,2},{2,3},{197,4},{4,5},{199,6},{6,7},{201,8},{8... | collective-permute-start | bytes 1572872 | tf_op jit(solution)/shard_map/ppermute | solution.py:27
  17.3 2.7 %collective-permute-start.5 = (bf16[320,512]{1,0:T(8,128)(2,1)S(1)}, bf16[320,512]{1,0:T(8,128)(2,1)S(1)}, u32[]{:S(2)}, u32[]{:S(2)}) collective-permute-start(bf16[320,512]{1,0:T(8,128)(2,1)S(1)} %pad_maximum_fusion.2), channel_id=1, source_target_pairs={{16,0},{17,1},{18,2},{19,3},{20,4},{21,5},{22,6},{23,7},{24,8},{25... | collective-permute-start | bytes 983048 | tf_op jit(solution)/shard_map/ppermute | solution.py:27
  20.0 3.0 %collective-permute-start.8 = (bf16[2,320,512]{2,1,0:T(8,128)(2,1)S(1)}, bf16[2,320,512]{2,1,0:T(8,128)(2,1)S(1)}, u32[]{:S(2)}, u32[]{:S(2)}) collective-permute-start(bf16[2,320,512]{2,1,0:T(8,128)(2,1)S(1)} %pad_maximum_fusion.refs_5_), channel_id=1, source_target_pairs={{2,0},{3,1},{4,2},{5,3},{6,4},{7,5},{0,6},{1,7},{10,8},{11,9},{12,... | collective-permute-start | bytes 1966088 | tf_op jit(solution)/shard_map/ppermute | solution.py:27
  23.1 2.8 %collective-permute-done.5 = bf16[320,512]{1,0:T(8,128)(2,1)S(1)} collective-permute-done((bf16[320,512]{1,0:T(8,128)(2,1)S(1)}, bf16[320,512]{1,0:T(8,128)(2,1)S(1)}, u32[]{:S(2)}, u32[]{:S(2)}) %collective-permute-start.5) | collective-permute-done | bytes 327712 | tf_op jit(solution)/shard_map/ppermute | solution.py:27
  26.0 1.6 %collective-permute-start.12 = (bf16[2,320,512]{2,1,0:T(8,128)(2,1)S(1)}, bf16[2,320,512]{2,1,0:T(8,128)(2,1)S(1)}, u32[]{:S(2)}, u32[]{:S(2)}) collective-permute-start(bf16[2,320,512]{2,1,0:T(8,128)(2,1)S(1)} %pad_maximum_fusion.1.refs_6_), channel_id=1, source_target_pairs={{6,0},{7,1},{0,2},{1,3},{2,4},{3,5},{4,6},{5,7},{14,8},{15,9},{8,1... | collective-permute-start | bytes 1966088 | tf_op jit(solution)/shard_map/ppermute | solution.py:27
  27.6 3.6 %collective-permute-start.13 = (bf16[1024,256]{1,0:T(8,128)(2,1)}, bf16[1024,256]{1,0:T(8,128)(2,1)}, u32[]{:S(2)}, u32[]{:S(2)}) collective-permute-start(bf16[1024,256]{1,0:T(8,128)(2,1)} %collective-permute-done.6.refs_15_), channel_id=1, source_target_pairs={{193,0},{0,1},{195,2},{2,3},{197,4},{4,5},{199,6},{6,7},{201,8},{8... | collective-permute-start | bytes 1572872 | tf_op jit(solution)/shard_map/ppermute | solution.py:27
  31.2 1.6 %collective-permute-start.11 = (bf16[2,320,512]{2,1,0:T(8,128)(2,1)S(1)}, bf16[2,320,512]{2,1,0:T(8,128)(2,1)S(1)}, u32[]{:S(2)}, u32[]{:S(2)}) collective-permute-start(bf16[2,320,512]{2,1,0:T(8,128)(2,1)S(1)} %pad_maximum_fusion.refs_5_), channel_id=1, source_target_pairs={{6,0},{7,1},{0,2},{1,3},{2,4},{3,5},{4,6},{5,7},{14,8},{15,9},{8,1... | collective-permute-start | bytes 1966088 | tf_op jit(solution)/shard_map/ppermute | solution.py:27
  33.6 2.6 %collective-permute-start.9 = (bf16[1024,256]{1,0:T(8,128)(2,1)}, bf16[1024,256]{1,0:T(8,128)(2,1)}, u32[]{:S(2)}, u32[]{:S(2)}) collective-permute-start(bf16[1024,256]{1,0:T(8,128)(2,1)} %collective-permute-done.7.refs_19_), channel_id=1, source_target_pairs={{193,0},{0,1},{195,2},{2,3},{197,4},{4,5},{199,6},{6,7},{201,8},{8... | collective-permute-start | bytes 1572872 | tf_op jit(solution)/shard_map/ppermute | solution.py:27
  36.9 1.4 %collective-permute-done.13.refs_16_ = bf16[1024,256]{1,0:T(8,128)(2,1)} collective-permute-done((bf16[1024,256]{1,0:T(8,128)(2,1)}, bf16[1024,256]{1,0:T(8,128)(2,1)}, u32[]{:S(2)}, u32[]{:S(2)}) %collective-permute-start.13) | collective-permute-done | bytes 524320 | tf_op jit(solution)/shard_map/ppermute | solution.py:27
  38.2 1.7 %collective-permute-start.10 = (bf16[2,320,512]{2,1,0:T(8,128)(2,1)S(1)}, bf16[2,320,512]{2,1,0:T(8,128)(2,1)}, u32[]{:S(2)}, u32[]{:S(2)}) collective-permute-start(bf16[2,320,512]{2,1,0:T(8,128)(2,1)S(1)} %pad_maximum_fusion.1.refs_6_), channel_id=1, source_target_pairs={{2,0},{3,1},{4,2},{5,3},{6,4},{7,5},{0,6},{1,7},{10,8},{11,9},{12,... | collective-permute-start | bytes 1966088 | tf_op jit(solution)/shard_map/ppermute | solution.py:27
  40.9 1.1 collective-permute-start.20
  42.1 1.8 %collective-permute-done.9.refs_20_ = bf16[1024,256]{1,0:T(8,128)(2,1)} collective-permute-done((bf16[1024,256]{1,0:T(8,128)(2,1)}, bf16[1024,256]{1,0:T(8,128)(2,1)}, u32[]{:S(2)}, u32[]{:S(2)}) %collective-permute-start.9) | collective-permute-done | bytes 524320 | tf_op jit(solution)/shard_map/ppermute | solution.py:27
  43.8 2.6 %collective-permute-start.17 = (bf16[1024,256]{1,0:T(8,128)(2,1)}, bf16[1024,256]{1,0:T(8,128)(2,1)}, u32[]{:S(2)}, u32[]{:S(2)}) collective-permute-start(bf16[1024,256]{1,0:T(8,128)(2,1)} %collective-permute-done.9.refs_20_), channel_id=1, source_target_pairs={{193,0},{0,1},{195,2},{2,3},{197,4},{4,5},{199,6},{6,7},{201,8},{8... | collective-permute-start | bytes 1572872 | tf_op jit(solution)/shard_map/ppermute | solution.py:27
  46.4 3.8 %collective-permute-start.16 = (bf16[1024,256]{1,0:T(8,128)(2,1)}, bf16[1024,256]{1,0:T(8,128)(2,1)}, u32[]{:S(2)}, u32[]{:S(2)}) collective-permute-start(bf16[1024,256]{1,0:T(8,128)(2,1)} %collective-permute-done.13.refs_16_), channel_id=1, source_target_pairs={{193,0},{0,1},{195,2},{2,3},{197,4},{4,5},{199,6},{6,7},{201,8},{8... | collective-permute-start | bytes 1572872 | tf_op jit(solution)/shard_map/ppermute | solution.py:27
  50.5 1.7 %collective-permute-start.14 = (bf16[2,320,512]{2,1,0:T(8,128)(2,1)S(1)}, bf16[2,320,512]{2,1,0:T(8,128)(2,1)S(1)}, u32[]{:S(2)}, u32[]{:S(2)}) collective-permute-start(bf16[2,320,512]{2,1,0:T(8,128)(2,1)S(1)} %collective-permute-done.8.refs_7_), channel_id=1, source_target_pairs={{2,0},{3,1},{4,2},{5,3},{6,4},{7,5},{0,6},{1,7},{10,8},{11,9},{12,... | collective-permute-start | bytes 1966088 | tf_op jit(solution)/shard_map/ppermute | solution.py:27
  54.0 5.1 %collective-permute-done.16.refs_17_ = bf16[1024,256]{1,0:T(8,128)(2,1)} collective-permute-done((bf16[1024,256]{1,0:T(8,128)(2,1)}, bf16[1024,256]{1,0:T(8,128)(2,1)}, u32[]{:S(2)}, u32[]{:S(2)}) %collective-permute-start.16) | collective-permute-done | bytes 524320 | tf_op jit(solution)/shard_map/ppermute | solution.py:27
  59.9 1.3 %collective-permute-done.14.refs_11_ = bf16[2,320,512]{2,1,0:T(8,128)(2,1)S(1)} collective-permute-done((bf16[2,320,512]{2,1,0:T(8,128)(2,1)S(1)}, bf16[2,320,512]{2,1,0:T(8,128)(2,1)S(1)}, u32[]{:S(2)}, u32[]{:S(2)}) %collective-permute-start.14) | collective-permute-done | bytes 655392 | tf_op jit(solution)/shard_map/ppermute | solution.py:27
  61.2 2.9 %collective-permute-done.15.refs_12_ = bf16[2,320,512]{2,1,0:T(8,128)(2,1)S(1)} collective-permute-done((bf16[2,320,512]{2,1,0:T(8,128)(2,1)S(1)}, bf16[2,320,512]{2,1,0:T(8,128)(2,1)S(1)}, u32[]{:S(2)}, u32[]{:S(2)}) %collective-permute-start.15) | collective-permute-done | bytes 655392 | tf_op jit(solution)/shard_map/ppermute | solution.py:27
  64.1 1.0 copy-done.1
  65.1 1.0 copy-done.3
  66.2 1.0 copy-done.5
  68.2 12.3 %ladder.1 = bf16[16,20,512]{2,1,0:T(8,128)(2,1)S(1)} custom-call(s32[1]{0:T(128)} %bitcast.refs_0_, s32[16]{0:T(128)S(1)} %add_multiply_fusion.1.refs_1_, s32[16]{0:T(128)S(1)} %get-tuple-element.27.refs_2_, s32[64]{0:T(128)S(1)} %select_reduce_fusion.refs_3_, f32[20480]{0:T(1024)S(1)} %reshape.63.refs_4_, bf16[2,320,512]{2,1,0:T(8,128)(2,1)S(1)} %pad_maximum_fusion.refs_5_, ...), custom_call_target="tpu_custom_call" | custom-call | flops 2684354560 | bytes 18874368 | tf_op jit(solution)/shard_map/ladder/pallas_call | solution.py:150
  80.5 15.5 %all_to_all.10.src_ref = bf16[16,20,512]{2,1,0:T(8,128)(2,1)S(1)} all-to-all(bf16[16,20,512]{2,1,0:T(8,128)(2,1)S(1)} %ladder.1), channel_id=1, replica_groups=mesh['zh'=4,'core'=2,'x'=4,'y'=4,'zl'=2] {'x','y'}, dimensions={0} | all-to-all | bytes 655360 | tf_op jit(solution)/shard_map/all_to_all | solution.py:221
  96.1 1.7 %reorder.1 = bf16[32,20,256]{2,1,0:T(8,128)(2,1)} custom-call(s32[64]{0:T(128)S(1)} %copy-done.8, bf16[16,20,512]{2,1,0:T(8,128)(2,1)S(1)} %all_to_all.10.src_ref), custom_call_target="tpu_custom_call" | custom-call | bytes 1048576 | tf_op jit(solution)/shard_map/reorder/pallas_call | solution.py:183
  97.8 6.3 %all-to-all-start.1 = ((bf16[32,20,256]{2,1,0:T(8,128)(2,1)}), bf16[32,20,256]{2,1,0:T(8,128)(2,1)S(1)}, u32[]{:S(2)}, u32[]{:S(2)}) async-start(bf16[32,20,256]{2,1,0:T(8,128)(2,1)} %reorder.1), calls=%async_computation.1 | async-start | bytes 786432 | tf_op jit(solution)/shard_map/all_to_all | solution.py:223
  106.8 7.0 %all-to-all-done.1 = bf16[32,20,256]{2,1,0:T(8,128)(2,1)S(1)} async-done(((bf16[32,20,256]{2,1,0:T(8,128)(2,1)}), bf16[32,20,256]{2,1,0:T(8,128)(2,1)S(1)}, u32[]{:S(2)}, u32[]{:S(2)}) %all-to-all-start.1) | async-done | bytes 327712 | tf_op jit(solution)/shard_map/all_to_all | solution.py:223
  (73 shorter events, 9.0 us)
Async XLA Ops:
  0.0 3.1 %copy-start = (bf16[1024,256]{1,0:T(8,128)(2,1)S(1)}, bf16[1024,256]{1,0:T(8,128)(2,1)}, u32[]{:S(2)}) copy-start(bf16[1024,256]{1,0:T(8,128)(2,1)} %refs_13_.1) | copy-start | bytes 1572868
  0.0 8.3 %collective-permute-start.1 = (bf16[1024,256]{1,0:T(8,128)(2,1)}, bf16[1024,256]{1,0:T(8,128)(2,1)S(1)}, u32[]{:S(2)}, u32[]{:S(2)}) collective-permute-start(bf16[1024,256]{1,0:T(8,128)(2,1)} %refs_13_.1), channel_id=1, source_target_pairs={{32,0},{33,1},{34,2},{35,3},{36,4},{37,5},{38,6},{39,7},{40,8},{41... | collective-permute-start | bytes 1572872 | tf_op jit(solution)/shard_map/ppermute | solution.py:27
  1.1 7.2 %collective-permute-start = (bf16[320,256]{1,0:T(8,128)(2,1)S(1)}, bf16[320,256]{1,0:T(8,128)(2,1)S(1)}, u32[]{:S(2)}, u32[]{:S(2)}) collective-permute-start(bf16[320,256]{1,0:T(8,128)(2,1)S(1)} %get-tuple-element.30), channel_id=1, source_target_pairs={{1,0},{0,1},{3,2},{2,3},{5,4},{4,5},{7,6},{6,7},{9,8},{8,9},{11,10... | collective-permute-start | bytes 491528 | tf_op jit(solution)/shard_map/ppermute | solution.py:27
  3.1 12.7 %collective-permute-start.3 = (bf16[1024,256]{1,0:T(8,128)(2,1)S(1)}, bf16[1024,256]{1,0:T(8,128)(2,1)S(1)}, u32[]{:S(2)}, u32[]{:S(2)}) collective-permute-start(bf16[1024,256]{1,0:T(8,128)(2,1)S(1)} %copy-done), channel_id=1, source_target_pairs={{193,0},{0,1},{195,2},{2,3},{197,4},{4,5},{199,6},{6,7},{201,8},{8... | collective-permute-start | bytes 1572872 | tf_op jit(solution)/shard_map/ppermute | solution.py:27
  8.3 7.5 %copy-start.2 = (bf16[1024,256]{1,0:T(8,128)(2,1)}, bf16[1024,256]{1,0:T(8,128)(2,1)S(1)}, u32[]{:S(2)}) copy-start(bf16[1024,256]{1,0:T(8,128)(2,1)S(1)} %collective-permute-done.1.refs_18_) | copy-start | bytes 1572868
  8.3 7.4 %collective-permute-start.2 = (bf16[320,512]{1,0:T(8,128)(2,1)S(1)}, bf16[320,512]{1,0:T(8,128)(2,1)S(1)}, u32[]{:S(2)}, u32[]{:S(2)}) collective-permute-start(bf16[320,512]{1,0:T(8,128)(2,1)S(1)} %pad_maximum_fusion.2), channel_id=1, source_target_pairs={{8,0},{9,1},{10,2},{11,3},{12,4},{13,5},{14,6},{15,7},{16,8},{17,9... | collective-permute-start | bytes 983048 | tf_op jit(solution)/shard_map/ppermute | solution.py:27
  11.1 11.9 %collective-permute-start.4 = (bf16[320,512]{1,0:T(8,128)(2,1)S(1)}, bf16[320,512]{1,0:T(8,128)(2,1)S(1)}, u32[]{:S(2)}, u32[]{:S(2)}) collective-permute-start(bf16[320,512]{1,0:T(8,128)(2,1)S(1)} %pad_maximum_fusion.2), channel_id=1, source_target_pairs={{24,0},{25,1},{26,2},{27,3},{28,4},{29,5},{30,6},{31,7},{0,8},{1,9... | collective-permute-start | bytes 983048 | tf_op jit(solution)/shard_map/ppermute | solution.py:27
  11.1 14.8 %collective-permute-start.7 = (bf16[1024,256]{1,0:T(8,128)(2,1)S(1)}, bf16[1024,256]{1,0:T(8,128)(2,1)}, u32[]{:S(2)}, u32[]{:S(2)}) collective-permute-start(bf16[1024,256]{1,0:T(8,128)(2,1)S(1)} %collective-permute-done.1.refs_18_), channel_id=1, source_target_pairs={{193,0},{0,1},{195,2},{2,3},{197,4},{4,5},{199,6},{6,7},{201,8},{8... | collective-permute-start | bytes 1572872 | tf_op jit(solution)/shard_map/ppermute | solution.py:27
  15.8 10.1 %copy-start.4 = (bf16[1024,256]{1,0:T(8,128)(2,1)}, bf16[1024,256]{1,0:T(8,128)(2,1)S(1)}, u32[]{:S(2)}) copy-start(bf16[1024,256]{1,0:T(8,128)(2,1)S(1)} %collective-permute-done.3.refs_14_) | copy-start | bytes 1572868
  15.8 10.2 %collective-permute-start.6 = (bf16[1024,256]{1,0:T(8,128)(2,1)S(1)}, bf16[1024,256]{1,0:T(8,128)(2,1)}, u32[]{:S(2)}, u32[]{:S(2)}) collective-permute-start(bf16[1024,256]{1,0:T(8,128)(2,1)S(1)} %collective-permute-done.3.refs_14_), channel_id=1, source_target_pairs={{193,0},{0,1},{195,2},{2,3},{197,4},{4,5},{199,6},{6,7},{201,8},{8... | collective-permute-start | bytes 1572872 | tf_op jit(solution)/shard_map/ppermute | solution.py:27
  17.3 8.6 %collective-permute-start.5 = (bf16[320,512]{1,0:T(8,128)(2,1)S(1)}, bf16[320,512]{1,0:T(8,128)(2,1)S(1)}, u32[]{:S(2)}, u32[]{:S(2)}) collective-permute-start(bf16[320,512]{1,0:T(8,128)(2,1)S(1)} %pad_maximum_fusion.2), channel_id=1, source_target_pairs={{16,0},{17,1},{18,2},{19,3},{20,4},{21,5},{22,6},{23,7},{24,8},{25... | collective-permute-start | bytes 983048 | tf_op jit(solution)/shard_map/ppermute | solution.py:27
  20.0 16.1 %collective-permute-start.8 = (bf16[2,320,512]{2,1,0:T(8,128)(2,1)S(1)}, bf16[2,320,512]{2,1,0:T(8,128)(2,1)S(1)}, u32[]{:S(2)}, u32[]{:S(2)}) collective-permute-start(bf16[2,320,512]{2,1,0:T(8,128)(2,1)S(1)} %pad_maximum_fusion.refs_5_), channel_id=1, source_target_pairs={{2,0},{3,1},{4,2},{5,3},{6,4},{7,5},{0,6},{1,7},{10,8},{11,9},{12,... | collective-permute-start | bytes 1966088 | tf_op jit(solution)/shard_map/ppermute | solution.py:27
  23.1 9.7 %collective-permute-start.18 = (bf16[1024,256]{1,0:T(8,128)(2,1)S(1)}, bf16[1024,256]{1,0:T(8,128)(2,1)S(1)}, u32[]{:S(2)}, u32[]{:S(2)}) collective-permute-start(bf16[1024,256]{1,0:T(8,128)(2,1)S(1)} %collective-permute-done.3.refs_14_), channel_id=1, source_target_pairs={{32,0},{33,1},{34,2},{35,3},{36,4},{37,5},{38,6},{39,7},{40,8},{41... | collective-permute-start | bytes 1572872 | tf_op jit(solution)/shard_map/ppermute | solution.py:27
  26.0 14.9 %collective-permute-start.12 = (bf16[2,320,512]{2,1,0:T(8,128)(2,1)S(1)}, bf16[2,320,512]{2,1,0:T(8,128)(2,1)S(1)}, u32[]{:S(2)}, u32[]{:S(2)}) collective-permute-start(bf16[2,320,512]{2,1,0:T(8,128)(2,1)S(1)} %pad_maximum_fusion.1.refs_6_), channel_id=1, source_target_pairs={{6,0},{7,1},{0,2},{1,3},{2,4},{3,5},{4,6},{5,7},{14,8},{15,9},{8,1... | collective-permute-start | bytes 1966088 | tf_op jit(solution)/shard_map/ppermute | solution.py:27
  27.6 10.6 %collective-permute-start.13 = (bf16[1024,256]{1,0:T(8,128)(2,1)}, bf16[1024,256]{1,0:T(8,128)(2,1)}, u32[]{:S(2)}, u32[]{:S(2)}) collective-permute-start(bf16[1024,256]{1,0:T(8,128)(2,1)} %collective-permute-done.6.refs_15_), channel_id=1, source_target_pairs={{193,0},{0,1},{195,2},{2,3},{197,4},{4,5},{199,6},{6,7},{201,8},{8... | collective-permute-start | bytes 1572872 | tf_op jit(solution)/shard_map/ppermute | solution.py:27
  31.2 15.2 %collective-permute-start.11 = (bf16[2,320,512]{2,1,0:T(8,128)(2,1)S(1)}, bf16[2,320,512]{2,1,0:T(8,128)(2,1)S(1)}, u32[]{:S(2)}, u32[]{:S(2)}) collective-permute-start(bf16[2,320,512]{2,1,0:T(8,128)(2,1)S(1)} %pad_maximum_fusion.refs_5_), channel_id=1, source_target_pairs={{6,0},{7,1},{0,2},{1,3},{2,4},{3,5},{4,6},{5,7},{14,8},{15,9},{8,1... | collective-permute-start | bytes 1966088 | tf_op jit(solution)/shard_map/ppermute | solution.py:27
  33.6 10.3 %collective-permute-start.9 = (bf16[1024,256]{1,0:T(8,128)(2,1)}, bf16[1024,256]{1,0:T(8,128)(2,1)}, u32[]{:S(2)}, u32[]{:S(2)}) collective-permute-start(bf16[1024,256]{1,0:T(8,128)(2,1)} %collective-permute-done.7.refs_19_), channel_id=1, source_target_pairs={{193,0},{0,1},{195,2},{2,3},{197,4},{4,5},{199,6},{6,7},{201,8},{8... | collective-permute-start | bytes 1572872 | tf_op jit(solution)/shard_map/ppermute | solution.py:27
  36.2 10.3 %collective-permute-start.19 = (bf16[1024,256]{1,0:T(8,128)(2,1)}, bf16[1024,256]{1,0:T(8,128)(2,1)}, u32[]{:S(2)}, u32[]{:S(2)}) collective-permute-start(bf16[1024,256]{1,0:T(8,128)(2,1)} %collective-permute-done.7.refs_19_), channel_id=1, source_target_pairs={{32,0},{33,1},{34,2},{35,3},{36,4},{37,5},{38,6},{39,7},{40,8},{41... | collective-permute-start | bytes 1572872 | tf_op jit(solution)/shard_map/ppermute | solution.py:27
  38.2 14.1 %collective-permute-start.10 = (bf16[2,320,512]{2,1,0:T(8,128)(2,1)S(1)}, bf16[2,320,512]{2,1,0:T(8,128)(2,1)}, u32[]{:S(2)}, u32[]{:S(2)}) collective-permute-start(bf16[2,320,512]{2,1,0:T(8,128)(2,1)S(1)} %pad_maximum_fusion.1.refs_6_), channel_id=1, source_target_pairs={{2,0},{3,1},{4,2},{5,3},{6,4},{7,5},{0,6},{1,7},{10,8},{11,9},{12,... | collective-permute-start | bytes 1966088 | tf_op jit(solution)/shard_map/ppermute | solution.py:27
  40.9 9.6 %collective-permute-start.20 = (bf16[1024,256]{1,0:T(8,128)(2,1)}, bf16[1024,256]{1,0:T(8,128)(2,1)}, u32[]{:S(2)}, u32[]{:S(2)}) collective-permute-start(bf16[1024,256]{1,0:T(8,128)(2,1)} %collective-permute-done.6.refs_15_), channel_id=1, source_target_pairs={{32,0},{33,1},{34,2},{35,3},{36,4},{37,5},{38,6},{39,7},{40,8},{41... | collective-permute-start | bytes 1572872 | tf_op jit(solution)/shard_map/ppermute | solution.py:27
  43.8 9.6 %collective-permute-start.17 = (bf16[1024,256]{1,0:T(8,128)(2,1)}, bf16[1024,256]{1,0:T(8,128)(2,1)}, u32[]{:S(2)}, u32[]{:S(2)}) collective-permute-start(bf16[1024,256]{1,0:T(8,128)(2,1)} %collective-permute-done.9.refs_20_), channel_id=1, source_target_pairs={{193,0},{0,1},{195,2},{2,3},{197,4},{4,5},{199,6},{6,7},{201,8},{8... | collective-permute-start | bytes 1572872 | tf_op jit(solution)/shard_map/ppermute | solution.py:27
  46.4 7.0 %collective-permute-start.21 = (bf16[1024,256]{1,0:T(8,128)(2,1)}, bf16[1024,256]{1,0:T(8,128)(2,1)}, u32[]{:S(2)}, u32[]{:S(2)}) collective-permute-start(bf16[1024,256]{1,0:T(8,128)(2,1)} %collective-permute-done.9.refs_20_), channel_id=1, source_target_pairs={{32,0},{33,1},{34,2},{35,3},{36,4},{37,5},{38,6},{39,7},{40,8},{41... | collective-permute-start | bytes 1572872 | tf_op jit(solution)/shard_map/ppermute | solution.py:27
  46.4 12.6 %collective-permute-start.16 = (bf16[1024,256]{1,0:T(8,128)(2,1)}, bf16[1024,256]{1,0:T(8,128)(2,1)}, u32[]{:S(2)}, u32[]{:S(2)}) collective-permute-start(bf16[1024,256]{1,0:T(8,128)(2,1)} %collective-permute-done.13.refs_16_), channel_id=1, source_target_pairs={{193,0},{0,1},{195,2},{2,3},{197,4},{4,5},{199,6},{6,7},{201,8},{8... | collective-permute-start | bytes 1572872 | tf_op jit(solution)/shard_map/ppermute | solution.py:27
  50.5 10.7 %collective-permute-start.14 = (bf16[2,320,512]{2,1,0:T(8,128)(2,1)S(1)}, bf16[2,320,512]{2,1,0:T(8,128)(2,1)S(1)}, u32[]{:S(2)}, u32[]{:S(2)}) collective-permute-start(bf16[2,320,512]{2,1,0:T(8,128)(2,1)S(1)} %collective-permute-done.8.refs_7_), channel_id=1, source_target_pairs={{2,0},{3,1},{4,2},{5,3},{6,4},{7,5},{0,6},{1,7},{10,8},{11,9},{12,... | collective-permute-start | bytes 1966088 | tf_op jit(solution)/shard_map/ppermute | solution.py:27
  52.3 11.8 %collective-permute-start.15 = (bf16[2,320,512]{2,1,0:T(8,128)(2,1)S(1)}, bf16[2,320,512]{2,1,0:T(8,128)(2,1)S(1)}, u32[]{:S(2)}, u32[]{:S(2)}) collective-permute-start(bf16[2,320,512]{2,1,0:T(8,128)(2,1)S(1)} %collective-permute-done.12.refs_10_), channel_id=1, source_target_pairs={{6,0},{7,1},{0,2},{1,3},{2,4},{3,5},{4,6},{5,7},{14,8},{15,9},{8,1... | collective-permute-start | bytes 1966088 | tf_op jit(solution)/shard_map/ppermute | solution.py:27
  52.8 6.4 %copy-start.11 = (s32[16]{0:T(128)S(1)}, s32[16]{0:T(128)}, u32[]{:S(2)}) copy-start(s32[16]{0:T(128)} %constant.108.clone) | copy-start | bytes 196
  53.5 7.7 %collective-permute-start.22 = (bf16[1024,256]{1,0:T(8,128)(2,1)}, bf16[1024,256]{1,0:T(8,128)(2,1)S(1)}, u32[]{:S(2)}, u32[]{:S(2)}) collective-permute-start(bf16[1024,256]{1,0:T(8,128)(2,1)} %collective-permute-done.13.refs_16_), channel_id=1, source_target_pairs={{32,0},{33,1},{34,2},{35,3},{36,4},{37,5},{38,6},{39,7},{40,8},{41... | collective-permute-start | bytes 1572872 | tf_op jit(solution)/shard_map/ppermute | solution.py:27
  53.5 7.7 %collective-permute-start.23 = (bf16[1024,256]{1,0:T(8,128)(2,1)}, bf16[1024,256]{1,0:T(8,128)(2,1)S(1)}, u32[]{:S(2)}, u32[]{:S(2)}) collective-permute-start(bf16[1024,256]{1,0:T(8,128)(2,1)} %collective-permute-done.17.refs_21_), channel_id=1, source_target_pairs={{32,0},{33,1},{34,2},{35,3},{36,4},{37,5},{38,6},{39,7},{40,8},{41... | collective-permute-start | bytes 1572872 | tf_op jit(solution)/shard_map/ppermute | solution.py:27
  59.1 5.0 %collective-permute-start.24 = (bf16[1024,256]{1,0:T(8,128)(2,1)}, bf16[1024,256]{1,0:T(8,128)(2,1)S(1)}, u32[]{:S(2)}, u32[]{:S(2)}) collective-permute-start(bf16[1024,256]{1,0:T(8,128)(2,1)} %collective-permute-done.16.refs_17_), channel_id=1, source_target_pairs={{32,0},{33,1},{34,2},{35,3},{36,4},{37,5},{38,6},{39,7},{40,8},{41... | collective-permute-start | bytes 1572872 | tf_op jit(solution)/shard_map/ppermute | solution.py:27
  97.8 15.9 %all-to-all-start.1 = ((bf16[32,20,256]{2,1,0:T(8,128)(2,1)}), bf16[32,20,256]{2,1,0:T(8,128)(2,1)S(1)}, u32[]{:S(2)}, u32[]{:S(2)}) async-start(bf16[32,20,256]{2,1,0:T(8,128)(2,1)} %reorder.1), calls=%async_computation.1 | async-start | bytes 786432 | tf_op jit(solution)/shard_map/all_to_all | solution.py:223
  106.8 7.0 %copy-start.9 = (bf16[640,256]{1,0:T(8,128)(2,1)S(1)}, bf16[640,256]{1,0:T(8,128)(2,1)}, u32[]{:S(2)}) copy-start(bf16[640,256]{1,0:T(8,128)(2,1)} %param.10) | copy-start | bytes 983044
  106.8 7.0 %copy-start.10 = (f32[640]{0:T(1024)S(1)}, f32[640]{0:T(1024)}, u32[]{:S(2)}) copy-start(f32[640]{0:T(1024)} %param.14) | copy-start | bytes 7684
  (9 other events, 9.1 us)

commit v6 on v4

--- a/solution.py
+++ b/solution.py
@@ -53,26 +53,29 @@
 
 def gather(left, panel):
     other = swap(panel)
+    left, other = tie(left, other)
     first, second, flips = [panel], [other], []
 
     def advance():
         first.append(ring(first[-1]))
-        flips.append(swap(first[-1]))
         if len(second) < ZH:
             second.append(ring(second[-1]))
-            flips.append(swap(second[-1]))
-
-    left, second[0] = tie(left, second[0])
-    advance()
-    block = jnp.stack([left] + [minor(left, d) for d in (1, 2, 3)])
-    block, first[1], second[1] = tie(block, first[1], second[1])
+
+    advance()
+    nearest = minor(left, 1)
+    first[1], nearest = tie(first[1], nearest)
+    block = jnp.stack([left, nearest] + [minor(left, d) for d in (2, 3)])
+    advance()
+    block, first[2], second[1] = tie(block, first[2], second[1])
     ahead, behind = major(block, 1), major(block, 3)
     advance()
     advance()
-    ahead, behind, first[2], second[2] = tie(ahead, behind, first[2], second[2])
+    ahead, first[3], second[3] = tie(ahead, first[3], second[3])
+    behind, first[4] = tie(behind, first[4])
     far = [major(ahead[:2], 1), major(behind[2:], 3)]
-    advance()
-    return [block, ahead, behind] + far, first + second + flips
+    both = [jnp.stack([a, b]) for a, b in zip(first[1:], second[1:])]
+    flips = [swap(b) for b in both] + [swap(first[-1])]
+    return [block, ahead, behind] + far, [panel, other] + both + flips[:-1] + [first[-1], flips[-1]]
 
 
 def amplitude_steps():
@@ -80,8 +83,8 @@
 
 
 def panel_steps():
-    steps = [(d, 0) for d in range(5)] + [(d, 1) for d in range(4)]
-    return steps + [(-d, flip) for d in (1, 2, 3) for flip in (1, 0)] + [(-4, 1)]
+    steps = [(0, 0), (0, 1)] + [(d, flip) for d in (1, 2, 3) for flip in (0, 1)]
+    return steps + [(-d, flip) for d in (1, 2, 3) for flip in (1, 0)] + [(4, 0), (-4, 1)]
 
 
 def ladder_kernel(count, *refs):
@@ -99,14 +102,18 @@
         n = block.shape[0]
         copies.append(pltpu.make_async_copy(block, left_ref.at[at : at + n], left_sem.at[i]))
         at += n
-    fetch = [pltpu.make_async_copy(panel, held.at[g], sems.at[g]) for g, panel in enumerate(panels)]
+    fetch, g = [], 0
+    for panel in panels:
+        for part in [panel] if len(panel.shape) == 2 else [panel.at[i] for i in range(panel.shape[0])]:
+            fetch.append(pltpu.make_async_copy(part, held.at[g], sems.at[g]))
+            g += 1
     for c in copies + fetch:
         c.start()
     total[...] = jnp.zeros_like(total)
     for c in copies:
         c.wait()
 
-    @pl.loop(0, count)
+    @pl.loop(0, held.shape[0])
     def _(g):
         pltpu.make_async_copy(panels[0], held.at[g], sems.at[g]).wait()
         part, first = part_ref[g], first_ref[g]
@@ -138,12 +145,12 @@
 def ladder(line, where, place, screen, blocks, panels):
     depth, width = panels[0].shape
     rows = blocks[0].shape[1]
-    count, pieces = len(panels), sum(b.shape[0] for b in blocks)
+    count, pieces = where[0].shape[0], sum(b.shape[0] for b in blocks)
     chunks = NX * NY
     return pl.pallas_call(
-        functools.partial(ladder_kernel, count),
+        functools.partial(ladder_kernel, len(panels)),
         out_shape=jax.ShapeDtypeStruct((chunks, rows // chunks, ZL * width), jnp.bfloat16),
-        in_specs=[SMEM] * 5 + [HBM] * (len(blocks) + count),
+        in_specs=[SMEM] * 5 + [HBM] * (len(blocks) + len(panels)),
         out_specs=VMEM,
         scratch_shapes=[
             pltpu.VMEM((pieces,) + blocks[0].shape[1:], jnp.bfloat16),

time: 112 us -> 125 us (1.12)
  waiting for transfers between devices: 44.9 us -> 49.5 us
  other arithmetic: 2.5 us -> 6.74 us
  starting transfers between devices: 32.4 us -> 35.1 us
  local copies, waits for them, and re-layouts: 3.95 us -> 5.94 us
    ppermute x23 -> x20, waiting for transfers between devices: 38 us -> 42.7 us  [send(): return lax.ppermute(value, AXES, pairs)]
    another operation x1 -> x4, other arithmetic: 0.16 us -> 3.73 us  [the longest x3 3.57 us: gather(): both = [jnp.stack([a, b]) for a, b in zip(first[1:], second[1:])]]
    ppermute x23 -> x20, starting transfers between devices: 27.3 us -> 29.3 us  [send(): return lax.ppermute(value, AXES, pairs)]
  transfers between devices with their start and end apart: 24 -> 21, of which waited for: 11 -> 13; matrix products, arithmetic and copies ran while one was open for 5% -> 9% of each run, Pallas kernels for 0% -> 0%
where the time goes in v6:
time: 125 us
  waiting for transfers between devices  49.5 us (40%)
  starting transfers between devices  35.1 us (28%)
  Pallas kernels  14.1 us (11%)
  blocking collectives  11.7 us (9%)
  other arithmetic  6.74 us (5%)
  local copies, waits for them, and re-layouts  5.94 us (5%)
  between operations  1.6 us (1%)
    ppermute x20, waiting for transfers between devices, send(): return lax.ppermute(value, AXES, pairs)  42.7 us
    ppermute x20, starting transfers between devices, send(): return lax.ppermute(value, AXES, pairs)  29.3 us
    pallas_call x1, Pallas kernels, ladder(): pl.pallas_call(functools.partial(ladder_kernel, len(panels)), out_shape=j...  12.4 us
    all_to_all x1, blocking collectives, local(): spread = lax.all_to_all(found, ('x', 'y'), 0, 0, tiled=True)  11.7 us
    all_to_all x1, waiting for transfers between devices, local(): total = lax.all_to_all(sent, ('zl', 'x', 'y'), 0, 0, tiled=True)  6.79 us
    all_to_all x1, starting transfers between devices, local(): total = lax.all_to_all(sent, ('zl', 'x', 'y'), 0, 0, tiled=True)  5.79 us
    another operation x3, other arithmetic, gather(): both = [jnp.stack([a, b]) for a, b in zip(first[1:], second[1:])]  3.57 us
  transfers between devices with their start and end apart: 21, of which 13 were waited for; matrix products, arithmetic and copies ran while one was open for 9% of the time, Pallas kernels for 0%

profile of v6, /device:TPU:64, one launch (start us, length us, event | category | flops | bytes accessed | tf_op | source)
XLA Modules:
  0.0 124.7 jit_solution(4787738268590680973)
XLA Ops:
  1.0 2.0 %collective-permute-start = (bf16[320,256]{1,0:T(8,128)(2,1)S(1)}, bf16[320,256]{1,0:T(8,128)(2,1)S(1)}, u32[]{:S(2)}, u32[]{:S(2)}) collective-permute-start(bf16[320,256]{1,0:T(8,128)(2,1)S(1)} %get-tuple-element.32), channel_id=1, source_target_pairs={{1,0},{0,1},{3,2},{2,3},{5,4},{4,5},{7,6},{6,7},{9,8},{8,9},{11,10... | collective-permute-start | bytes 491528 | tf_op jit(solution)/shard_map/ppermute | solution.py:27
  3.1 5.0 %collective-permute-done = bf16[320,256]{1,0:T(8,128)(2,1)S(1)} collective-permute-done((bf16[320,256]{1,0:T(8,128)(2,1)S(1)}, bf16[320,256]{1,0:T(8,128)(2,1)S(1)}, u32[]{:S(2)}, u32[]{:S(2)}) %collective-permute-start) | collective-permute-done | bytes 163872 | tf_op jit(solution)/shard_map/ppermute | solution.py:27
  8.2 2.8 %collective-permute-start.3 = (bf16[320,512]{1,0:T(8,128)(2,1)S(1)}, bf16[320,512]{1,0:T(8,128)(2,1)S(1)}, u32[]{:S(2)}, u32[]{:S(2)}) collective-permute-start(bf16[320,512]{1,0:T(8,128)(2,1)S(1)} %pad_maximum_fusion.4), channel_id=1, source_target_pairs={{8,0},{9,1},{10,2},{11,3},{12,4},{13,5},{14,6},{15,7},{16,8},{17,9... | collective-permute-start | bytes 983048 | tf_op jit(solution)/shard_map/ppermute | solution.py:27
  11.1 1.5 %collective-permute-start.7 = (bf16[1024,256]{1,0:T(8,128)(2,1)S(1)}, bf16[1024,256]{1,0:T(8,128)(2,1)S(1)}, u32[]{:S(2)}, u32[]{:S(2)}) collective-permute-start(bf16[1024,256]{1,0:T(8,128)(2,1)S(1)} %collective-permute-done.1.refs_11_), channel_id=1, source_target_pairs={{193,0},{0,1},{195,2},{2,3},{197,4},{4,5},{199,6},{6,7},{201,8},{8... | collective-permute-start | bytes 1572872 | tf_op jit(solution)/shard_map/ppermute | solution.py:27
  12.9 2.7 %collective-permute-done.3 = bf16[320,512]{1,0:T(8,128)(2,1)S(1)} collective-permute-done((bf16[320,512]{1,0:T(8,128)(2,1)S(1)}, bf16[320,512]{1,0:T(8,128)(2,1)S(1)}, u32[]{:S(2)}, u32[]{:S(2)}) %collective-permute-start.3) | collective-permute-done | bytes 327712 | tf_op jit(solution)/shard_map/ppermute | solution.py:27
  15.7 1.5 %collective-permute-start.6 = (bf16[1024,256]{1,0:T(8,128)(2,1)S(1)}, bf16[1024,256]{1,0:T(8,128)(2,1)}, u32[]{:S(2)}, u32[]{:S(2)}) collective-permute-start(bf16[1024,256]{1,0:T(8,128)(2,1)S(1)} %collective-permute-done.2), channel_id=1, source_target_pairs={{193,0},{0,1},{195,2},{2,3},{197,4},{4,5},{199,6},{6,7},{201,8},{8... | collective-permute-start | bytes 1572872 | tf_op jit(solution)/shard_map/ppermute | solution.py:27
  17.1 1.2 collective-permute-start.5
  18.4 3.9 %collective-permute-start.4 = (bf16[320,512]{1,0:T(8,128)(2,1)S(1)}, bf16[320,512]{1,0:T(8,128)(2,1)S(1)}, u32[]{:S(2)}, u32[]{:S(2)}) collective-permute-start(bf16[320,512]{1,0:T(8,128)(2,1)S(1)} %pad_maximum_fusion.4), channel_id=1, source_target_pairs={{16,0},{17,1},{18,2},{19,3},{20,4},{21,5},{22,6},{23,7},{24,8},{25... | collective-permute-start | bytes 983048 | tf_op jit(solution)/shard_map/ppermute | solution.py:27
  22.3 3.6 %collective-permute-done.5 = bf16[320,512]{1,0:T(8,128)(2,1)S(1)} collective-permute-done((bf16[320,512]{1,0:T(8,128)(2,1)S(1)}, bf16[320,512]{1,0:T(8,128)(2,1)S(1)}, u32[]{:S(2)}, u32[]{:S(2)}) %collective-permute-start.5) | collective-permute-done | bytes 327712 | tf_op jit(solution)/shard_map/ppermute | solution.py:27
  25.9 5.0 %collective-permute-done.4 = bf16[320,512]{1,0:T(8,128)(2,1)S(1)} collective-permute-done((bf16[320,512]{1,0:T(8,128)(2,1)S(1)}, bf16[320,512]{1,0:T(8,128)(2,1)S(1)}, u32[]{:S(2)}, u32[]{:S(2)}) %collective-permute-start.4) | collective-permute-done | bytes 327712 | tf_op jit(solution)/shard_map/ppermute | solution.py:27
  31.1 3.7 %collective-permute-start.8 = (bf16[4,320,512]{2,1,0:T(8,128)(2,1)S(1)}, bf16[4,320,512]{2,1,0:T(8,128)(2,1)}, u32[]{:S(2)}, u32[]{:S(2)}) collective-permute-start(bf16[4,320,512]{2,1,0:T(8,128)(2,1)S(1)} %pad_maximum_fusion.refs_5_), channel_id=1, source_target_pairs={{2,0},{3,1},{4,2},{5,3},{6,4},{7,5},{0,6},{1,7},{10,8},{11,9},{12,... | collective-permute-start | bytes 3932168 | tf_op jit(solution)/shard_map/ppermute | solution.py:27
  34.7 5.2 %collective-permute-start.10 = (bf16[1024,256]{1,0:T(8,128)(2,1)S(1)}, bf16[1024,256]{1,0:T(8,128)(2,1)}, u32[]{:S(2)}, u32[]{:S(2)}) collective-permute-start(bf16[1024,256]{1,0:T(8,128)(2,1)S(1)} %collective-permute-done.7), channel_id=1, source_target_pairs={{193,0},{0,1},{195,2},{2,3},{197,4},{4,5},{199,6},{6,7},{201,8},{8... | collective-permute-start | bytes 1572872 | tf_op jit(solution)/shard_map/ppermute | solution.py:27
  40.0 6.7 %collective-permute-done.10 = bf16[1024,256]{1,0:T(8,128)(2,1)} collective-permute-done((bf16[1024,256]{1,0:T(8,128)(2,1)S(1)}, bf16[1024,256]{1,0:T(8,128)(2,1)}, u32[]{:S(2)}, u32[]{:S(2)}) %collective-permute-start.10) | collective-permute-done | bytes 524320 | tf_op jit(solution)/shard_map/ppermute | solution.py:27
  46.7 2.6 %collective-permute-start.11 = (bf16[1024,256]{1,0:T(8,128)(2,1)}, bf16[1024,256]{1,0:T(8,128)(2,1)S(1)}, u32[]{:S(2)}, u32[]{:S(2)}) collective-permute-start(bf16[1024,256]{1,0:T(8,128)(2,1)} %collective-permute-done.10), channel_id=1, source_target_pairs={{193,0},{0,1},{195,2},{2,3},{197,4},{4,5},{199,6},{6,7},{201,8},{8... | collective-permute-start | bytes 1572872 | tf_op jit(solution)/shard_map/ppermute | solution.py:27
  49.5 1.3 %pad_maximum_fusion.2.refs_13_ = bf16[2,1024,256]{2,1,0:T(8,128)(2,1)S(1)} fusion(bf16[1,1024,256]{2,1,0:T(8,128)(2,1)} %bitcast.8, bf16[1,1024,256]{2,1,0:T(8,128)(2,1)} %bitcast.7), kind=kLoop, calls=%fused_computation.2 | loop fusion | flops 524288 | bytes 2097152 | tf_op jit(solution)/shard_map/stack | solution.py:76
  50.8 1.6 %collective-permute-done.9 = bf16[1024,256]{1,0:T(8,128)(2,1)} collective-permute-done((bf16[1024,256]{1,0:T(8,128)(2,1)}, bf16[1024,256]{1,0:T(8,128)(2,1)}, u32[]{:S(2)}, u32[]{:S(2)}) %collective-permute-start.9) | collective-permute-done | bytes 524320 | tf_op jit(solution)/shard_map/ppermute | solution.py:27
  52.4 5.6 %collective-permute-done.11 = bf16[1024,256]{1,0:T(8,128)(2,1)S(1)} collective-permute-done((bf16[1024,256]{1,0:T(8,128)(2,1)}, bf16[1024,256]{1,0:T(8,128)(2,1)S(1)}, u32[]{:S(2)}, u32[]{:S(2)}) %collective-permute-start.11) | collective-permute-done | bytes 524320 | tf_op jit(solution)/shard_map/ppermute | solution.py:27
  58.0 2.4 %collective-permute-start.13 = (bf16[1024,256]{1,0:T(8,128)(2,1)}, bf16[1024,256]{1,0:T(8,128)(2,1)}, u32[]{:S(2)}, u32[]{:S(2)}) collective-permute-start(bf16[1024,256]{1,0:T(8,128)(2,1)} %collective-permute-done.9), channel_id=1, source_target_pairs={{193,0},{0,1},{195,2},{2,3},{197,4},{4,5},{199,6},{6,7},{201,8},{8... | collective-permute-start | bytes 1572872 | tf_op jit(solution)/shard_map/ppermute | solution.py:27
  60.4 2.2 %pad_maximum_fusion.3.refs_14_ = bf16[2,1024,256]{2,1,0:T(8,128)(2,1)} fusion(bf16[1,1024,256]{2,1,0:T(8,128)(2,1)S(1)} %bitcast.16, bf16[1,1024,256]{2,1,0:T(8,128)(2,1)} %bitcast.9), kind=kLoop, calls=%fused_computation.3 | loop fusion | flops 524288 | bytes 2097152 | tf_op jit(solution)/shard_map/stack | solution.py:76
  62.8 1.6 %dynamic-slice_convert_fusion = f32[5,64,64]{2,1,0:T(8,128)} fusion(s32[10,64,64]{2,1,0:T(8,128)} %param.13, s32[]{:T(128)S(6)} %select_n.75), kind=kLoop, calls=%fused_computation.6 | loop fusion | flops 20480 | bytes 163844 | tf_op jit(solution)/shard_map/convert_element_type | solution.py:215
  65.5 2.0 %collective-permute-done.13.refs_18_ = bf16[1024,256]{1,0:T(8,128)(2,1)} collective-permute-done((bf16[1024,256]{1,0:T(8,128)(2,1)}, bf16[1024,256]{1,0:T(8,128)(2,1)}, u32[]{:S(2)}, u32[]{:S(2)}) %collective-permute-start.13) | collective-permute-done | bytes 524320 | tf_op jit(solution)/shard_map/ppermute | solution.py:27
  67.5 1.1 slice.6
  69.5 1.1 slice.7
  70.6 1.4 %collective-permute-start.15 = (bf16[2,320,512]{2,1,0:T(8,128)(2,1)S(1)}, bf16[2,320,512]{2,1,0:T(8,128)(2,1)S(1)}, u32[]{:S(2)}, u32[]{:S(2)}) collective-permute-start(bf16[2,320,512]{2,1,0:T(8,128)(2,1)S(1)} %slice.7), channel_id=1, source_target_pairs={{6,0},{7,1},{0,2},{1,3},{2,4},{3,5},{4,6},{5,7},{14,8},{15,9},{8,1... | collective-permute-start | bytes 1966088 | tf_op jit(solution)/shard_map/ppermute | solution.py:27
  72.4 1.9 %collective-permute-done.19.refs_19_ = bf16[1024,256]{1,0:T(8,128)(2,1)S(1)} collective-permute-done((bf16[1024,256]{1,0:T(8,128)(2,1)}, bf16[1024,256]{1,0:T(8,128)(2,1)S(1)}, u32[]{:S(2)}, u32[]{:S(2)}) %collective-permute-start.19) | collective-permute-done | bytes 524320 | tf_op jit(solution)/shard_map/ppermute | solution.py:27
  74.4 5.0 %collective-permute-done.14.refs_8_ = bf16[2,320,512]{2,1,0:T(8,128)(2,1)S(1)} collective-permute-done((bf16[2,320,512]{2,1,0:T(8,128)(2,1)S(1)}, bf16[2,320,512]{2,1,0:T(8,128)(2,1)S(1)}, u32[]{:S(2)}, u32[]{:S(2)}) %collective-permute-start.14) | collective-permute-done | bytes 655392 | tf_op jit(solution)/shard_map/ppermute | solution.py:27
  79.3 3.2 %collective-permute-done.15.refs_9_ = bf16[2,320,512]{2,1,0:T(8,128)(2,1)S(1)} collective-permute-done((bf16[2,320,512]{2,1,0:T(8,128)(2,1)S(1)}, bf16[2,320,512]{2,1,0:T(8,128)(2,1)S(1)}, u32[]{:S(2)}, u32[]{:S(2)}) %collective-permute-start.15) | collective-permute-done | bytes 655392 | tf_op jit(solution)/shard_map/ppermute | solution.py:27
  82.5 12.4 %ladder.1 = bf16[16,20,512]{2,1,0:T(8,128)(2,1)S(1)} custom-call(s32[1]{0:T(128)} %bitcast.refs_0_, s32[16]{0:T(128)S(1)} %add_multiply_fusion.1.refs_1_, s32[16]{0:T(128)S(1)} %get-tuple-element.29.refs_2_, s32[64]{0:T(128)S(1)} %select_reduce_fusion.refs_3_, f32[20480]{0:T(1024)S(1)} %reshape.63.refs_4_, bf16[4,320,512]{2,1,0:T(8,128)(2,1)S(1)} %pad_maximum_fusion.refs_5_, ...), custom_call_target="tpu_custom_call" | custom-call | flops 2684354560 | bytes 18874368 | tf_op jit(solution)/shard_map/ladder/pallas_call | solution.py:150
  94.8 11.7 %all_to_all.10.src_ref = bf16[16,20,512]{2,1,0:T(8,128)(2,1)S(1)} all-to-all(bf16[16,20,512]{2,1,0:T(8,128)(2,1)S(1)} %ladder.1), channel_id=1, replica_groups=mesh['zh'=4,'core'=2,'x'=4,'y'=4,'zl'=2] {'x','y'}, dimensions={0} | all-to-all | bytes 655360 | tf_op jit(solution)/shard_map/all_to_all | solution.py:221
  106.6 1.7 %reorder.1 = bf16[32,20,256]{2,1,0:T(8,128)(2,1)} custom-call(s32[64]{0:T(128)S(1)} %copy-done.3, bf16[16,20,512]{2,1,0:T(8,128)(2,1)S(1)} %all_to_all.10.src_ref), custom_call_target="tpu_custom_call" | custom-call | bytes 1048576 | tf_op jit(solution)/shard_map/reorder/pallas_call | solution.py:183
  108.3 5.8 %all-to-all-start.1 = ((bf16[32,20,256]{2,1,0:T(8,128)(2,1)}), bf16[32,20,256]{2,1,0:T(8,128)(2,1)S(1)}, u32[]{:S(2)}, u32[]{:S(2)}) async-start(bf16[32,20,256]{2,1,0:T(8,128)(2,1)} %reorder.1), calls=%async_computation.1 | async-start | bytes 786432 | tf_op jit(solution)/shard_map/all_to_all | solution.py:223
  116.9 6.8 %all-to-all-done.1 = bf16[32,20,256]{2,1,0:T(8,128)(2,1)S(1)} async-done(((bf16[32,20,256]{2,1,0:T(8,128)(2,1)}), bf16[32,20,256]{2,1,0:T(8,128)(2,1)S(1)}, u32[]{:S(2)}, u32[]{:S(2)}) %all-to-all-start.1) | async-done | bytes 327712 | tf_op jit(solution)/shard_map/all_to_all | solution.py:223
  (57 shorter events, 6.9 us)
Async XLA Ops:
  0.0 8.2 %collective-permute-start.1 = (bf16[1024,256]{1,0:T(8,128)(2,1)}, bf16[1024,256]{1,0:T(8,128)(2,1)S(1)}, u32[]{:S(2)}, u32[]{:S(2)}) collective-permute-start(bf16[1024,256]{1,0:T(8,128)(2,1)} %refs_10_.1), channel_id=1, source_target_pairs={{32,0},{33,1},{34,2},{35,3},{36,4},{37,5},{38,6},{39,7},{40,8},{41... | collective-permute-start | bytes 1572872 | tf_op jit(solution)/shard_map/ppermute | solution.py:27
  1.0 7.2 %collective-permute-start = (bf16[320,256]{1,0:T(8,128)(2,1)S(1)}, bf16[320,256]{1,0:T(8,128)(2,1)S(1)}, u32[]{:S(2)}, u32[]{:S(2)}) collective-permute-start(bf16[320,256]{1,0:T(8,128)(2,1)S(1)} %get-tuple-element.32), channel_id=1, source_target_pairs={{1,0},{0,1},{3,2},{2,3},{5,4},{4,5},{7,6},{6,7},{9,8},{8,9},{11,10... | collective-permute-start | bytes 491528 | tf_op jit(solution)/shard_map/ppermute | solution.py:27
  3.0 9.9 %collective-permute-start.2 = (bf16[1024,256]{1,0:T(8,128)(2,1)}, bf16[1024,256]{1,0:T(8,128)(2,1)S(1)}, u32[]{:S(2)}, u32[]{:S(2)}) collective-permute-start(bf16[1024,256]{1,0:T(8,128)(2,1)} %refs_10_.1), channel_id=1, source_target_pairs={{193,0},{0,1},{195,2},{2,3},{197,4},{4,5},{199,6},{6,7},{201,8},{8... | collective-permute-start | bytes 1572872 | tf_op jit(solution)/shard_map/ppermute | solution.py:27
  8.2 22.8 %copy-start.1 = (bf16[1024,256]{1,0:T(8,128)(2,1)}, bf16[1024,256]{1,0:T(8,128)(2,1)S(1)}, u32[]{:S(2)}) copy-start(bf16[1024,256]{1,0:T(8,128)(2,1)S(1)} %collective-permute-done.1.refs_11_) | copy-start | bytes 1572868
  8.2 7.4 %collective-permute-start.3 = (bf16[320,512]{1,0:T(8,128)(2,1)S(1)}, bf16[320,512]{1,0:T(8,128)(2,1)S(1)}, u32[]{:S(2)}, u32[]{:S(2)}) collective-permute-start(bf16[320,512]{1,0:T(8,128)(2,1)S(1)} %pad_maximum_fusion.4), channel_id=1, source_target_pairs={{8,0},{9,1},{10,2},{11,3},{12,4},{13,5},{14,6},{15,7},{16,8},{17,9... | collective-permute-start | bytes 983048 | tf_op jit(solution)/shard_map/ppermute | solution.py:27
  11.1 20.0 %collective-permute-start.7 = (bf16[1024,256]{1,0:T(8,128)(2,1)S(1)}, bf16[1024,256]{1,0:T(8,128)(2,1)S(1)}, u32[]{:S(2)}, u32[]{:S(2)}) collective-permute-start(bf16[1024,256]{1,0:T(8,128)(2,1)S(1)} %collective-permute-done.1.refs_11_), channel_id=1, source_target_pairs={{193,0},{0,1},{195,2},{2,3},{197,4},{4,5},{199,6},{6,7},{201,8},{8... | collective-permute-start | bytes 1572872 | tf_op jit(solution)/shard_map/ppermute | solution.py:27
  15.7 15.4 %collective-permute-start.6 = (bf16[1024,256]{1,0:T(8,128)(2,1)S(1)}, bf16[1024,256]{1,0:T(8,128)(2,1)}, u32[]{:S(2)}, u32[]{:S(2)}) collective-permute-start(bf16[1024,256]{1,0:T(8,128)(2,1)S(1)} %collective-permute-done.2), channel_id=1, source_target_pairs={{193,0},{0,1},{195,2},{2,3},{197,4},{4,5},{199,6},{6,7},{201,8},{8... | collective-permute-start | bytes 1572872 | tf_op jit(solution)/shard_map/ppermute | solution.py:27
  17.1 8.7 %collective-permute-start.5 = (bf16[320,512]{1,0:T(8,128)(2,1)S(1)}, bf16[320,512]{1,0:T(8,128)(2,1)S(1)}, u32[]{:S(2)}, u32[]{:S(2)}) collective-permute-start(bf16[320,512]{1,0:T(8,128)(2,1)S(1)} %pad_maximum_fusion.4), channel_id=1, source_target_pairs={{24,0},{25,1},{26,2},{27,3},{28,4},{29,5},{30,6},{31,7},{0,8},{1,9... | collective-permute-start | bytes 983048 | tf_op jit(solution)/shard_map/ppermute | solution.py:27
  18.4 12.5 %collective-permute-start.4 = (bf16[320,512]{1,0:T(8,128)(2,1)S(1)}, bf16[320,512]{1,0:T(8,128)(2,1)S(1)}, u32[]{:S(2)}, u32[]{:S(2)}) collective-permute-start(bf16[320,512]{1,0:T(8,128)(2,1)S(1)} %pad_maximum_fusion.4), channel_id=1, source_target_pairs={{16,0},{17,1},{18,2},{19,3},{20,4},{21,5},{22,6},{23,7},{24,8},{25... | collective-permute-start | bytes 983048 | tf_op jit(solution)/shard_map/ppermute | solution.py:27
  30.9 18.4 %copy-start.8 = (s32[16]{0:T(128)S(1)}, s32[16]{0:T(128)}, u32[]{:S(2)}) copy-start(s32[16]{0:T(128)} %constant.106.clone) | copy-start | bytes 196
  30.9 18.4 %copy-start.9 = (s32[16]{0:T(128)S(1)}, s32[16]{0:T(128)}, u32[]{:S(2)}) copy-start(s32[16]{0:T(128)} %constant.107.clone) | copy-start | bytes 196
  31.1 29.3 %collective-permute-start.8 = (bf16[4,320,512]{2,1,0:T(8,128)(2,1)S(1)}, bf16[4,320,512]{2,1,0:T(8,128)(2,1)}, u32[]{:S(2)}, u32[]{:S(2)}) collective-permute-start(bf16[4,320,512]{2,1,0:T(8,128)(2,1)S(1)} %pad_maximum_fusion.refs_5_), channel_id=1, source_target_pairs={{2,0},{3,1},{4,2},{5,3},{6,4},{7,5},{0,6},{1,7},{10,8},{11,9},{12,... | collective-permute-start | bytes 3932168 | tf_op jit(solution)/shard_map/ppermute | solution.py:27
  34.7 11.9 %collective-permute-start.10 = (bf16[1024,256]{1,0:T(8,128)(2,1)S(1)}, bf16[1024,256]{1,0:T(8,128)(2,1)}, u32[]{:S(2)}, u32[]{:S(2)}) collective-permute-start(bf16[1024,256]{1,0:T(8,128)(2,1)S(1)} %collective-permute-done.7), channel_id=1, source_target_pairs={{193,0},{0,1},{195,2},{2,3},{197,4},{4,5},{199,6},{6,7},{201,8},{8... | collective-permute-start | bytes 1572872 | tf_op jit(solution)/shard_map/ppermute | solution.py:27
  40.0 27.5 %collective-permute-start.12 = (bf16[4,320,512]{2,1,0:T(8,128)(2,1)S(1)}, bf16[4,320,512]{2,1,0:T(8,128)(2,1)}, u32[]{:S(2)}, u32[]{:S(2)}) collective-permute-start(bf16[4,320,512]{2,1,0:T(8,128)(2,1)S(1)} %pad_maximum_fusion.refs_5_), channel_id=1, source_target_pairs={{6,0},{7,1},{0,2},{1,3},{2,4},{3,5},{4,6},{5,7},{14,8},{15,9},{8,1... | collective-permute-start | bytes 3932168 | tf_op jit(solution)/shard_map/ppermute | solution.py:27
  40.0 12.4 %collective-permute-start.9 = (bf16[1024,256]{1,0:T(8,128)(2,1)}, bf16[1024,256]{1,0:T(8,128)(2,1)}, u32[]{:S(2)}, u32[]{:S(2)}) collective-permute-start(bf16[1024,256]{1,0:T(8,128)(2,1)} %collective-permute-done.6), channel_id=1, source_target_pairs={{193,0},{0,1},{195,2},{2,3},{197,4},{4,5},{199,6},{6,7},{201,8},{8... | collective-permute-start | bytes 1572872 | tf_op jit(solution)/shard_map/ppermute | solution.py:27
  46.7 11.3 %collective-permute-start.11 = (bf16[1024,256]{1,0:T(8,128)(2,1)}, bf16[1024,256]{1,0:T(8,128)(2,1)S(1)}, u32[]{:S(2)}, u32[]{:S(2)}) collective-permute-start(bf16[1024,256]{1,0:T(8,128)(2,1)} %collective-permute-done.10), channel_id=1, source_target_pairs={{193,0},{0,1},{195,2},{2,3},{197,4},{4,5},{199,6},{6,7},{201,8},{8... | collective-permute-start | bytes 1572872 | tf_op jit(solution)/shard_map/ppermute | solution.py:27
  49.4 22.8 %collective-permute-start.16 = (bf16[2,1024,256]{2,1,0:T(8,128)(2,1)S(1)}, bf16[2,1024,256]{2,1,0:T(8,128)(2,1)}, u32[]{:S(2)}, u32[]{:S(2)}) collective-permute-start(bf16[2,1024,256]{2,1,0:T(8,128)(2,1)S(1)} %pad_maximum_fusion.1.refs_12_), channel_id=1, source_target_pairs={{32,0},{33,1},{34,2},{35,3},{36,4},{37,5},{38,6},{39,7},{40,8},{41... | collective-permute-start | bytes 3145736 | tf_op jit(solution)/shard_map/ppermute | solution.py:27
  52.4 20.0 %collective-permute-start.17 = (bf16[2,1024,256]{2,1,0:T(8,128)(2,1)S(1)}, bf16[2,1024,256]{2,1,0:T(8,128)(2,1)}, u32[]{:S(2)}, u32[]{:S(2)}) collective-permute-start(bf16[2,1024,256]{2,1,0:T(8,128)(2,1)S(1)} %pad_maximum_fusion.2.refs_13_), channel_id=1, source_target_pairs={{32,0},{33,1},{34,2},{35,3},{36,4},{37,5},{38,6},{39,7},{40,8},{41... | collective-permute-start | bytes 3145736 | tf_op jit(solution)/shard_map/ppermute | solution.py:27
  58.0 9.5 %collective-permute-start.13 = (bf16[1024,256]{1,0:T(8,128)(2,1)}, bf16[1024,256]{1,0:T(8,128)(2,1)}, u32[]{:S(2)}, u32[]{:S(2)}) collective-permute-start(bf16[1024,256]{1,0:T(8,128)(2,1)} %collective-permute-done.9), channel_id=1, source_target_pairs={{193,0},{0,1},{195,2},{2,3},{197,4},{4,5},{199,6},{6,7},{201,8},{8... | collective-permute-start | bytes 1572872 | tf_op jit(solution)/shard_map/ppermute | solution.py:27
  62.6 19.9 %collective-permute-start.18 = (bf16[2,1024,256]{2,1,0:T(8,128)(2,1)}, bf16[2,1024,256]{2,1,0:T(8,128)(2,1)}, u32[]{:S(2)}, u32[]{:S(2)}) collective-permute-start(bf16[2,1024,256]{2,1,0:T(8,128)(2,1)} %pad_maximum_fusion.3.refs_14_), channel_id=1, source_target_pairs={{32,0},{33,1},{34,2},{35,3},{36,4},{37,5},{38,6},{39,7},{40,8},{41... | collective-permute-start | bytes 3145736 | tf_op jit(solution)/shard_map/ppermute | solution.py:27
  65.4 6.5 %copy-start.3 = (s32[64]{0:T(128)S(1)}, s32[64]{0:T(128)}, u32[]{:S(2)}) copy-start(s32[64]{0:T(128)} %owner_ref.1) | copy-start | bytes 772
  65.5 6.9 %copy-start.6 = (s32[16]{0:T(128)S(1)}, s32[16]{0:T(128)}, u32[]{:S(2)}) copy-start(s32[16]{0:T(128)} %constant.108.clone) | copy-start | bytes 196
  65.5 6.9 %copy-start.7 = (s32[16]{0:T(128)S(1)}, s32[16]{0:T(128)}, u32[]{:S(2)}) copy-start(s32[16]{0:T(128)} %constant.109.clone) | copy-start | bytes 196
  65.5 17.0 %copy-start = (bf16[1024,256]{1,0:T(8,128)(2,1)S(1)}, bf16[1024,256]{1,0:T(8,128)(2,1)}, u32[]{:S(2)}) copy-start(bf16[1024,256]{1,0:T(8,128)(2,1)} %refs_10_.1) | copy-start | bytes 1572868
  65.5 17.0 %copy-start.2 = (bf16[1024,256]{1,0:T(8,128)(2,1)S(1)}, bf16[1024,256]{1,0:T(8,128)(2,1)}, u32[]{:S(2)}) copy-start(bf16[1024,256]{1,0:T(8,128)(2,1)} %copy-done.1) | copy-start | bytes 1572868
  68.6 10.7 %collective-permute-start.14 = (bf16[2,320,512]{2,1,0:T(8,128)(2,1)S(1)}, bf16[2,320,512]{2,1,0:T(8,128)(2,1)S(1)}, u32[]{:S(2)}, u32[]{:S(2)}) collective-permute-start(bf16[2,320,512]{2,1,0:T(8,128)(2,1)S(1)} %slice.6), channel_id=1, source_target_pairs={{2,0},{3,1},{4,2},{5,3},{6,4},{7,5},{0,6},{1,7},{10,8},{11,9},{12,... | collective-permute-start | bytes 1966088 | tf_op jit(solution)/shard_map/ppermute | solution.py:27
  70.6 11.9 %collective-permute-start.15 = (bf16[2,320,512]{2,1,0:T(8,128)(2,1)S(1)}, bf16[2,320,512]{2,1,0:T(8,128)(2,1)S(1)}, u32[]{:S(2)}, u32[]{:S(2)}) collective-permute-start(bf16[2,320,512]{2,1,0:T(8,128)(2,1)S(1)} %slice.7), channel_id=1, source_target_pairs={{6,0},{7,1},{0,2},{1,3},{2,4},{3,5},{4,6},{5,7},{14,8},{15,9},{8,1... | collective-permute-start | bytes 1966088 | tf_op jit(solution)/shard_map/ppermute | solution.py:27
  72.1 2.2 %collective-permute-start.19 = (bf16[1024,256]{1,0:T(8,128)(2,1)}, bf16[1024,256]{1,0:T(8,128)(2,1)S(1)}, u32[]{:S(2)}, u32[]{:S(2)}) collective-permute-start(bf16[1024,256]{1,0:T(8,128)(2,1)} %collective-permute-done.13.refs_18_), channel_id=1, source_target_pairs={{32,0},{33,1},{34,2},{35,3},{36,4},{37,5},{38,6},{39,7},{40,8},{41... | collective-permute-start | bytes 1572872 | tf_op jit(solution)/shard_map/ppermute | solution.py:27
  106.6 17.2 %copy-start.4 = (bf16[640,256]{1,0:T(8,128)(2,1)S(1)}, bf16[640,256]{1,0:T(8,128)(2,1)}, u32[]{:S(2)}) copy-start(bf16[640,256]{1,0:T(8,128)(2,1)} %param.10) | copy-start | bytes 983044
  106.6 17.2 %copy-start.5 = (f32[640]{0:T(1024)S(1)}, f32[640]{0:T(1024)}, u32[]{:S(2)}) copy-start(f32[640]{0:T(1024)} %param.14) | copy-start | bytes 7684
  108.3 15.4 %all-to-all-start.1 = ((bf16[32,20,256]{2,1,0:T(8,128)(2,1)}), bf16[32,20,256]{2,1,0:T(8,128)(2,1)S(1)}, u32[]{:S(2)}, u32[]{:S(2)}) async-start(bf16[32,20,256]{2,1,0:T(8,128)(2,1)} %reorder.1), calls=%async_computation.1 | async-start | bytes 786432 | tf_op jit(solution)/shard_map/all_to_all | solution.py:223

commit v7 on v4

--- a/solution.py
+++ b/solution.py
@@ -85,14 +85,14 @@
 
 
 def ladder_kernel(count, *refs):
-    line_ref, first_ref, part_ref, place_ref, screen_ref = refs[:5]
-    blocks, refs = refs[5:10], refs[10:]
+    first_ref, part_ref, place_ref, screen_ref = refs[:4]
+    blocks, refs = refs[4:9], refs[9:]
     panels, refs = refs[:count], refs[count:]
     out_ref, left_ref, held, total, left_sem, sems = refs
     depth, width = held.shape[1:]
     rows = left_ref.shape[1]
     tiles = place_ref.shape[0]
-    line, per, wide = line_ref[0], depth // TILE, left_ref.shape[2] // TILE
+    per, wide, across = depth // TILE, left_ref.shape[2] // TILE, ZL * width // TILE
 
     copies, at = [], 0
     for i, block in enumerate(blocks):
@@ -111,14 +111,13 @@
         pltpu.make_async_copy(panels[0], held.at[g], sems.at[g]).wait()
         part, first = part_ref[g], first_ref[g]
         for j in range(width // TILE):
-            wanted = (line * ZL + part) * 2 + j
             left = []
             for r in range(per):
                 at = place_ref[first + r]
                 column = pl.ds(pl.multiple_of(lax.rem(at, wide) * TILE, TILE), TILE)
                 strips = []
                 for b in range(rows // PBLK):
-                    mark = screen_ref[(b * tiles + first + r) * tiles + wanted]
+                    mark = screen_ref[(b * tiles + first + r) * across + part * (width // TILE) + j]
                     strip = left_ref[at // wide, b * PBLK : (b + 1) * PBLK, column]
                     strips.append(strip * jnp.full((PBLK, TILE), mark, jnp.float32).astype(strip.dtype))
                 left.append(jnp.concatenate(strips, axis=0))
@@ -135,7 +134,7 @@
             out_ref[c, :, i * TILE : (i + 1) * TILE] = strip.astype(out_ref.dtype)
 
 
-def ladder(line, where, place, screen, blocks, panels):
+def ladder(where, place, screen, blocks, panels):
     depth, width = panels[0].shape
     rows = blocks[0].shape[1]
     count, pieces = len(panels), sum(b.shape[0] for b in blocks)
@@ -143,7 +142,7 @@
     return pl.pallas_call(
         functools.partial(ladder_kernel, count),
         out_shape=jax.ShapeDtypeStruct((chunks, rows // chunks, ZL * width), jnp.bfloat16),
-        in_specs=[SMEM] * 5 + [HBM] * (len(blocks) + count),
+        in_specs=[SMEM] * 4 + [HBM] * (len(blocks) + count),
         out_specs=VMEM,
         scratch_shapes=[
             pltpu.VMEM((pieces,) + blocks[0].shape[1:], jnp.bfloat16),
@@ -159,7 +158,7 @@
             transcendentals=0,
         ),
         name="ladder",
-    )(line, *where, place, screen, *blocks, *panels)
+    )(*where, place, screen, *blocks, *panels)
 
 
 def reorder_kernel(owner_ref, src_ref, dst_ref):
@@ -192,9 +191,9 @@
     line = x * NY + y
     steps = jnp.arange(tiles, dtype=jnp.int32)
 
-    mine = lax.dynamic_slice_in_dim(amplitudes, zl * half, half, 0)
     other = lax.dynamic_slice_in_dim(amplitudes, (1 - zl) * half, half, 0)
     other = send(other, lambda zh, core, x, y, zl: (zh, core, x, y, 1 - zl))
+    mine = lax.dynamic_slice_in_dim(amplitudes, zl * half, half, 0)
     blocks, panels = gather(jnp.concatenate([mine, other], axis=1), integrals)
 
     far, close = (jnp.array(v, jnp.int32) for v in zip(*amplitude_steps()))
@@ -204,13 +203,16 @@
     held = jnp.sum(jnp.where(slots[:, None] == steps[None, :], tile_owner[None, :], 0), axis=1)
     place = jnp.sum(jnp.where(held[:, None] == steps[None, :], steps[:, None], 0), axis=0)
 
-    screen = lax.dynamic_slice_in_dim(screening, zl * (half // PBLK), half // PBLK, 0)
+    across = ZL * width // TILE
+    screen = lax.dynamic_slice(
+        screening, (zl * (half // PBLK), 0, line * across), (half // PBLK, tiles, across)
+    )
     screen = screen.astype(jnp.float32).reshape(-1)
     step, flip = (jnp.array(v, jnp.int32) for v in zip(*panel_steps()))
     chip = (zh * ZL + zl + step * (2 * core - 1)) % (ZH * ZL)
     first = (chip // ZL * CORE + (core ^ flip)) * (integrals.shape[0] // TILE)
     where = (first.astype(jnp.int32), (chip % ZL).astype(jnp.int32))
-    found = ladder(jnp.stack([line]).astype(jnp.int32), where, place, screen, blocks, panels)
+    found = ladder(where, place, screen, blocks, panels)
     spread = lax.all_to_all(found, ("x", "y"), 0, 0, tiled=True)
     sent = reorder(tile_owner, spread)
     total = lax.all_to_all(sent, ("zl", "x", "y"), 0, 0, tiled=True)

time: 112 us -> 111 us (level)
  Pallas kernels: 13.7 us -> 12.5 us
    pallas_call x1, Pallas kernels: 12 us -> 10.8 us  [ladder(): pl.pallas_call(functools.partial(ladder_kernel, count), out_shape=jax.Sha...]
where the time goes in v7:
time: 111 us; the launch traced here: 110 us
  waiting for transfers between devices  44.8 us (40%)
  starting transfers between devices  32.4 us (29%)
  Pallas kernels  12.5 us (11%)
  blocking collectives  12.4 us (11%)
  local copies, waits for them, and re-layouts  4 us (4%)
  other arithmetic  2.59 us (2%)
  between operations  1.56 us (1%)
    ppermute x23, waiting for transfers between devices, send(): return lax.ppermute(value, AXES, pairs)  37.9 us
    ppermute x23, starting transfers between devices, send(): return lax.ppermute(value, AXES, pairs)  27.3 us
    all_to_all x1, blocking collectives, local(): spread = lax.all_to_all(found, ('x', 'y'), 0, 0, tiled=True)  12.4 us
    pallas_call x1, Pallas kernels, ladder(): pl.pallas_call(functools.partial(ladder_kernel, count), out_shape=jax.Sha...  10.8 us
    all_to_all x1, waiting for transfers between devices, local(): total = lax.all_to_all(sent, ('zl', 'x', 'y'), 0, 0, tiled=True)  6.9 us
    all_to_all x1, starting transfers between devices, local(): total = lax.all_to_all(sent, ('zl', 'x', 'y'), 0, 0, tiled=True)  5.1 us
  transfers between devices with their start and end apart: 24, of which 11 were waited for; matrix products, arithmetic and copies ran while one was open for 5% of the time, Pallas kernels for 0%

profile of v7, /device:TPU:64, one launch (start us, length us, event | category | flops | bytes accessed | tf_op | source)
XLA Modules:
  0.0 110.3 jit_solution(16966713161416619213)
XLA Ops:
  0.0 1.0 constant_dynamic-slice_fusion.1
  1.0 2.0 %collective-permute-start = (bf16[320,256]{1,0:T(8,128)(2,1)S(1)}, bf16[320,256]{1,0:T(8,128)(2,1)S(1)}, u32[]{:S(2)}, u32[]{:S(2)}) collective-permute-start(bf16[320,256]{1,0:T(8,128)(2,1)S(1)} %get-tuple-element.26), channel_id=1, source_target_pairs={{1,0},{0,1},{3,2},{2,3},{5,4},{4,5},{7,6},{6,7},{9,8},{8,9},{11,10... | collective-permute-start | bytes 491528 | tf_op jit(solution)/shard_map/ppermute | solution.py:27
  3.1 5.0 %collective-permute-done = bf16[320,256]{1,0:T(8,128)(2,1)S(1)} collective-permute-done((bf16[320,256]{1,0:T(8,128)(2,1)S(1)}, bf16[320,256]{1,0:T(8,128)(2,1)S(1)}, u32[]{:S(2)}, u32[]{:S(2)}) %collective-permute-start) | collective-permute-done | bytes 163872 | tf_op jit(solution)/shard_map/ppermute | solution.py:27
  8.2 1.6 %collective-permute-start.6 = (bf16[1024,256]{1,0:T(8,128)(2,1)S(1)}, bf16[1024,256]{1,0:T(8,128)(2,1)}, u32[]{:S(2)}, u32[]{:S(2)}) collective-permute-start(bf16[1024,256]{1,0:T(8,128)(2,1)S(1)} %collective-permute-done.1.refs_14_), channel_id=1, source_target_pairs={{193,0},{0,1},{195,2},{2,3},{197,4},{4,5},{199,6},{6,7},{201,8},{8... | collective-permute-start | bytes 1572872 | tf_op jit(solution)/shard_map/ppermute | solution.py:27
  9.8 2.8 %collective-permute-start.2 = (bf16[320,512]{1,0:T(8,128)(2,1)S(1)}, bf16[320,512]{1,0:T(8,128)(2,1)S(1)}, u32[]{:S(2)}, u32[]{:S(2)}) collective-permute-start(bf16[320,512]{1,0:T(8,128)(2,1)S(1)} %pad_maximum_fusion.1), channel_id=1, source_target_pairs={{8,0},{9,1},{10,2},{11,3},{12,4},{13,5},{14,6},{15,7},{16,8},{17,9... | collective-permute-start | bytes 983048 | tf_op jit(solution)/shard_map/ppermute | solution.py:27
  12.5 0.8 collective-permute-start.3
  13.3 0.9 collective-permute-start.4
  14.2 6.5 %collective-permute-done.2 = bf16[320,512]{1,0:T(8,128)(2,1)S(1)} collective-permute-done((bf16[320,512]{1,0:T(8,128)(2,1)S(1)}, bf16[320,512]{1,0:T(8,128)(2,1)S(1)}, u32[]{:S(2)}, u32[]{:S(2)}) %collective-permute-start.2) | collective-permute-done | bytes 327712 | tf_op jit(solution)/shard_map/ppermute | solution.py:27
  20.7 0.5 collective-permute-done.3
  21.2 3.4 %collective-permute-done.4 = bf16[320,512]{1,0:T(8,128)(2,1)S(1)} collective-permute-done((bf16[320,512]{1,0:T(8,128)(2,1)S(1)}, bf16[320,512]{1,0:T(8,128)(2,1)S(1)}, u32[]{:S(2)}, u32[]{:S(2)}) %collective-permute-start.4) | collective-permute-done | bytes 327712 | tf_op jit(solution)/shard_map/ppermute | solution.py:27
  24.8 3.1 %collective-permute-start.7 = (bf16[4,320,512]{2,1,0:T(8,128)(2,1)S(1)}, bf16[4,320,512]{2,1,0:T(8,128)(2,1)S(1)}, u32[]{:S(2)}, u32[]{:S(2)}) collective-permute-start(bf16[4,320,512]{2,1,0:T(8,128)(2,1)S(1)} %pad_maximum_fusion.refs_4_), channel_id=1, source_target_pairs={{2,0},{3,1},{4,2},{5,3},{6,4},{7,5},{0,6},{1,7},{10,8},{11,9},{12,... | collective-permute-start | bytes 3932168 | tf_op jit(solution)/shard_map/ppermute | solution.py:27
  27.9 3.7 %collective-permute-start.9 = (bf16[1024,256]{1,0:T(8,128)(2,1)}, bf16[1024,256]{1,0:T(8,128)(2,1)}, u32[]{:S(2)}, u32[]{:S(2)}) collective-permute-start(bf16[1024,256]{1,0:T(8,128)(2,1)} %collective-permute-done.5.refs_10_), channel_id=1, source_target_pairs={{193,0},{0,1},{195,2},{2,3},{197,4},{4,5},{199,6},{6,7},{201,8},{8... | collective-permute-start | bytes 1572872 | tf_op jit(solution)/shard_map/ppermute | solution.py:27
  32.0 6.6 %collective-permute-done.9.refs_11_ = bf16[1024,256]{1,0:T(8,128)(2,1)} collective-permute-done((bf16[1024,256]{1,0:T(8,128)(2,1)}, bf16[1024,256]{1,0:T(8,128)(2,1)}, u32[]{:S(2)}, u32[]{:S(2)}) %collective-permute-start.9) | collective-permute-done | bytes 524320 | tf_op jit(solution)/shard_map/ppermute | solution.py:27
  38.7 2.5 %collective-permute-start.13 = (bf16[1024,256]{1,0:T(8,128)(2,1)}, bf16[1024,256]{1,0:T(8,128)(2,1)}, u32[]{:S(2)}, u32[]{:S(2)}) collective-permute-start(bf16[1024,256]{1,0:T(8,128)(2,1)} %collective-permute-done.9.refs_11_), channel_id=1, source_target_pairs={{193,0},{0,1},{195,2},{2,3},{197,4},{4,5},{199,6},{6,7},{201,8},{8... | collective-permute-start | bytes 1572872 | tf_op jit(solution)/shard_map/ppermute | solution.py:27
  41.1 1.0 dynamic-slice_convert_fusion
  42.5 1.8 %collective-permute-done.10.refs_16_ = bf16[1024,256]{1,0:T(8,128)(2,1)} collective-permute-done((bf16[1024,256]{1,0:T(8,128)(2,1)}, bf16[1024,256]{1,0:T(8,128)(2,1)}, u32[]{:S(2)}, u32[]{:S(2)}) %collective-permute-start.10) | collective-permute-done | bytes 524320 | tf_op jit(solution)/shard_map/ppermute | solution.py:27
  44.3 2.5 %collective-permute-start.15 = (bf16[1024,256]{1,0:T(8,128)(2,1)}, bf16[1024,256]{1,0:T(8,128)(2,1)}, u32[]{:S(2)}, u32[]{:S(2)}) collective-permute-start(bf16[1024,256]{1,0:T(8,128)(2,1)} %collective-permute-done.10.refs_16_), channel_id=1, source_target_pairs={{193,0},{0,1},{195,2},{2,3},{197,4},{4,5},{199,6},{6,7},{201,8},{8... | collective-permute-start | bytes 1572872 | tf_op jit(solution)/shard_map/ppermute | solution.py:27
  46.8 3.1 %collective-permute-done.13.refs_12_ = bf16[1024,256]{1,0:T(8,128)(2,1)} collective-permute-done((bf16[1024,256]{1,0:T(8,128)(2,1)}, bf16[1024,256]{1,0:T(8,128)(2,1)}, u32[]{:S(2)}, u32[]{:S(2)}) %collective-permute-start.13) | collective-permute-done | bytes 524320 | tf_op jit(solution)/shard_map/ppermute | solution.py:27
  50.4 2.5 %collective-permute-start.14 = (bf16[1024,256]{1,0:T(8,128)(2,1)}, bf16[1024,256]{1,0:T(8,128)(2,1)}, u32[]{:S(2)}, u32[]{:S(2)}) collective-permute-start(bf16[1024,256]{1,0:T(8,128)(2,1)} %collective-permute-done.13.refs_12_), channel_id=1, source_target_pairs={{193,0},{0,1},{195,2},{2,3},{197,4},{4,5},{199,6},{6,7},{201,8},{8... | collective-permute-start | bytes 1572872 | tf_op jit(solution)/shard_map/ppermute | solution.py:27
  53.3 1.2 %slice.7 = bf16[2,320,512]{2,1,0:T(8,128)(2,1)S(1)} slice(bf16[4,320,512]{2,1,0:T(8,128)(2,1)} %collective-permute-done.8.refs_6_), slice={[2:4], [0:320], [0:512]} | slice | bytes 1310720 | tf_op jit(solution)/shard_map/slice | solution.py:73
  54.5 3.3 %collective-permute-start.11 = (bf16[2,320,512]{2,1,0:T(8,128)(2,1)S(1)}, bf16[2,320,512]{2,1,0:T(8,128)(2,1)S(1)}, u32[]{:S(2)}, u32[]{:S(2)}) collective-permute-start(bf16[2,320,512]{2,1,0:T(8,128)(2,1)S(1)} %slice.6), channel_id=1, source_target_pairs={{2,0},{3,1},{4,2},{5,3},{6,4},{7,5},{0,6},{1,7},{10,8},{11,9},{12,... | collective-permute-start | bytes 1966088 | tf_op jit(solution)/shard_map/ppermute | solution.py:27
  58.6 2.5 %collective-permute-done.14.refs_13_ = bf16[1024,256]{1,0:T(8,128)(2,1)} collective-permute-done((bf16[1024,256]{1,0:T(8,128)(2,1)}, bf16[1024,256]{1,0:T(8,128)(2,1)}, u32[]{:S(2)}, u32[]{:S(2)}) %collective-permute-start.14) | collective-permute-done | bytes 524320 | tf_op jit(solution)/shard_map/ppermute | solution.py:27
  61.3 4.6 %collective-permute-done.11.refs_7_ = bf16[2,320,512]{2,1,0:T(8,128)(2,1)S(1)} collective-permute-done((bf16[2,320,512]{2,1,0:T(8,128)(2,1)S(1)}, bf16[2,320,512]{2,1,0:T(8,128)(2,1)S(1)}, u32[]{:S(2)}, u32[]{:S(2)}) %collective-permute-start.11) | collective-permute-done | bytes 655392 | tf_op jit(solution)/shard_map/ppermute | solution.py:27
  65.9 3.7 %collective-permute-done.12.refs_8_ = bf16[2,320,512]{2,1,0:T(8,128)(2,1)S(1)} collective-permute-done((bf16[2,320,512]{2,1,0:T(8,128)(2,1)S(1)}, bf16[2,320,512]{2,1,0:T(8,128)(2,1)S(1)}, u32[]{:S(2)}, u32[]{:S(2)}) %collective-permute-start.12) | collective-permute-done | bytes 655392 | tf_op jit(solution)/shard_map/ppermute | solution.py:27
  69.6 10.8 %ladder.1 = bf16[16,20,512]{2,1,0:T(8,128)(2,1)S(1)} custom-call(s32[16]{0:T(128)S(1)} %add_multiply_fusion.1.refs_0_, s32[16]{0:T(128)S(1)} %get-tuple-element.23.refs_1_, s32[64]{0:T(128)S(1)} %select_reduce_fusion.refs_2_, f32[1280]{0:T(1024)S(1)} %reshape.63.refs_3_, bf16[4,320,512]{2,1,0:T(8,128)(2,1)S(1)} %pad_maximum_fusion.refs_4_, ...), custom_call_target="tpu_custom_call" | custom-call | flops 2684354560 | bytes 18874368 | tf_op jit(solution)/shard_map/ladder/pallas_call | solution.py:142
  80.4 12.4 %all_to_all.10.src_ref = bf16[16,20,512]{2,1,0:T(8,128)(2,1)S(1)} all-to-all(bf16[16,20,512]{2,1,0:T(8,128)(2,1)S(1)} %ladder.1), channel_id=1, replica_groups=mesh['zh'=4,'core'=2,'x'=4,'y'=4,'zl'=2] {'x','y'}, dimensions={0} | all-to-all | bytes 655360 | tf_op jit(solution)/shard_map/all_to_all | solution.py:216
  92.9 1.7 %reorder.1 = bf16[32,20,256]{2,1,0:T(8,128)(2,1)} custom-call(s32[64]{0:T(128)S(1)} %copy-done.1, bf16[16,20,512]{2,1,0:T(8,128)(2,1)S(1)} %all_to_all.10.src_ref), custom_call_target="tpu_custom_call" | custom-call | bytes 1048576 | tf_op jit(solution)/shard_map/reorder/pallas_call | solution.py:175
  94.6 5.1 %all-to-all-start.1 = ((bf16[32,20,256]{2,1,0:T(8,128)(2,1)}), bf16[32,20,256]{2,1,0:T(8,128)(2,1)S(1)}, u32[]{:S(2)}, u32[]{:S(2)}) async-start(bf16[32,20,256]{2,1,0:T(8,128)(2,1)} %reorder.1), calls=%async_computation.1 | async-start | bytes 786432 | tf_op jit(solution)/shard_map/all_to_all | solution.py:218
  99.7 0.6 fusion.9
  101.6 0.8 fusion.8
  102.4 6.9 %all-to-all-done.1 = bf16[32,20,256]{2,1,0:T(8,128)(2,1)S(1)} async-done(((bf16[32,20,256]{2,1,0:T(8,128)(2,1)}), bf16[32,20,256]{2,1,0:T(8,128)(2,1)S(1)}, u32[]{:S(2)}, u32[]{:S(2)}) %all-to-all-start.1) | async-done | bytes 327712 | tf_op jit(solution)/shard_map/all_to_all | solution.py:218
  109.4 0.9 add_convert_fusion
  (56 shorter events, 2.8 us)
Async XLA Ops:
  0.0 8.2 %collective-permute-start.1 = (bf16[1024,256]{1,0:T(8,128)(2,1)}, bf16[1024,256]{1,0:T(8,128)(2,1)S(1)}, u32[]{:S(2)}, u32[]{:S(2)}) collective-permute-start(bf16[1024,256]{1,0:T(8,128)(2,1)} %refs_9_.1), channel_id=1, source_target_pairs={{32,0},{33,1},{34,2},{35,3},{36,4},{37,5},{38,6},{39,7},{40,8},{41... | collective-permute-start | bytes 1572872 | tf_op jit(solution)/shard_map/ppermute | solution.py:27
  1.0 7.2 %collective-permute-start = (bf16[320,256]{1,0:T(8,128)(2,1)S(1)}, bf16[320,256]{1,0:T(8,128)(2,1)S(1)}, u32[]{:S(2)}, u32[]{:S(2)}) collective-permute-start(bf16[320,256]{1,0:T(8,128)(2,1)S(1)} %get-tuple-element.26), channel_id=1, source_target_pairs={{1,0},{0,1},{3,2},{2,3},{5,4},{4,5},{7,6},{6,7},{9,8},{8,9},{11,10... | collective-permute-start | bytes 491528 | tf_op jit(solution)/shard_map/ppermute | solution.py:27
  3.0 21.8 %collective-permute-start.5 = (bf16[1024,256]{1,0:T(8,128)(2,1)}, bf16[1024,256]{1,0:T(8,128)(2,1)}, u32[]{:S(2)}, u32[]{:S(2)}) collective-permute-start(bf16[1024,256]{1,0:T(8,128)(2,1)} %refs_9_.1), channel_id=1, source_target_pairs={{193,0},{0,1},{195,2},{2,3},{197,4},{4,5},{199,6},{6,7},{201,8},{8... | collective-permute-start | bytes 1572872 | tf_op jit(solution)/shard_map/ppermute | solution.py:27
  8.2 16.6 %collective-permute-start.6 = (bf16[1024,256]{1,0:T(8,128)(2,1)S(1)}, bf16[1024,256]{1,0:T(8,128)(2,1)}, u32[]{:S(2)}, u32[]{:S(2)}) collective-permute-start(bf16[1024,256]{1,0:T(8,128)(2,1)S(1)} %collective-permute-done.1.refs_14_), channel_id=1, source_target_pairs={{193,0},{0,1},{195,2},{2,3},{197,4},{4,5},{199,6},{6,7},{201,8},{8... | collective-permute-start | bytes 1572872 | tf_op jit(solution)/shard_map/ppermute | solution.py:27
  9.8 10.9 %collective-permute-start.2 = (bf16[320,512]{1,0:T(8,128)(2,1)S(1)}, bf16[320,512]{1,0:T(8,128)(2,1)S(1)}, u32[]{:S(2)}, u32[]{:S(2)}) collective-permute-start(bf16[320,512]{1,0:T(8,128)(2,1)S(1)} %pad_maximum_fusion.1), channel_id=1, source_target_pairs={{8,0},{9,1},{10,2},{11,3},{12,4},{13,5},{14,6},{15,7},{16,8},{17,9... | collective-permute-start | bytes 983048 | tf_op jit(solution)/shard_map/ppermute | solution.py:27
  12.5 8.7 %collective-permute-start.3 = (bf16[320,512]{1,0:T(8,128)(2,1)S(1)}, bf16[320,512]{1,0:T(8,128)(2,1)S(1)}, u32[]{:S(2)}, u32[]{:S(2)}) collective-permute-start(bf16[320,512]{1,0:T(8,128)(2,1)S(1)} %pad_maximum_fusion.1), channel_id=1, source_target_pairs={{16,0},{17,1},{18,2},{19,3},{20,4},{21,5},{22,6},{23,7},{24,8},{25... | collective-permute-start | bytes 983048 | tf_op jit(solution)/shard_map/ppermute | solution.py:27
  13.3 11.3 %collective-permute-start.4 = (bf16[320,512]{1,0:T(8,128)(2,1)S(1)}, bf16[320,512]{1,0:T(8,128)(2,1)S(1)}, u32[]{:S(2)}, u32[]{:S(2)}) collective-permute-start(bf16[320,512]{1,0:T(8,128)(2,1)S(1)} %pad_maximum_fusion.1), channel_id=1, source_target_pairs={{24,0},{25,1},{26,2},{27,3},{28,4},{29,5},{30,6},{31,7},{0,8},{1,9... | collective-permute-start | bytes 983048 | tf_op jit(solution)/shard_map/ppermute | solution.py:27
  24.6 17.7 %copy-start.6 = (s32[16]{0:T(128)S(1)}, s32[16]{0:T(128)}, u32[]{:S(2)}) copy-start(s32[16]{0:T(128)} %constant.106.clone) | copy-start | bytes 196
  24.6 17.7 %copy-start.7 = (s32[16]{0:T(128)S(1)}, s32[16]{0:T(128)}, u32[]{:S(2)}) copy-start(s32[16]{0:T(128)} %constant.107.clone) | copy-start | bytes 196
  24.8 25.1 %collective-permute-start.7 = (bf16[4,320,512]{2,1,0:T(8,128)(2,1)S(1)}, bf16[4,320,512]{2,1,0:T(8,128)(2,1)S(1)}, u32[]{:S(2)}, u32[]{:S(2)}) collective-permute-start(bf16[4,320,512]{2,1,0:T(8,128)(2,1)S(1)} %pad_maximum_fusion.refs_4_), channel_id=1, source_target_pairs={{2,0},{3,1},{4,2},{5,3},{6,4},{7,5},{0,6},{1,7},{10,8},{11,9},{12,... | collective-permute-start | bytes 3932168 | tf_op jit(solution)/shard_map/ppermute | solution.py:27
  27.9 22.5 %collective-permute-start.8 = (bf16[4,320,512]{2,1,0:T(8,128)(2,1)S(1)}, bf16[4,320,512]{2,1,0:T(8,128)(2,1)}, u32[]{:S(2)}, u32[]{:S(2)}) collective-permute-start(bf16[4,320,512]{2,1,0:T(8,128)(2,1)S(1)} %pad_maximum_fusion.refs_4_), channel_id=1, source_target_pairs={{6,0},{7,1},{0,2},{1,3},{2,4},{3,5},{4,6},{5,7},{14,8},{15,9},{8,1... | collective-permute-start | bytes 3932168 | tf_op jit(solution)/shard_map/ppermute | solution.py:27
  27.9 10.7 %collective-permute-start.9 = (bf16[1024,256]{1,0:T(8,128)(2,1)}, bf16[1024,256]{1,0:T(8,128)(2,1)}, u32[]{:S(2)}, u32[]{:S(2)}) collective-permute-start(bf16[1024,256]{1,0:T(8,128)(2,1)} %collective-permute-done.5.refs_10_), channel_id=1, source_target_pairs={{193,0},{0,1},{195,2},{2,3},{197,4},{4,5},{199,6},{6,7},{201,8},{8... | collective-permute-start | bytes 1572872 | tf_op jit(solution)/shard_map/ppermute | solution.py:27
  31.6 10.7 %collective-permute-start.16 = (bf16[1024,256]{1,0:T(8,128)(2,1)}, bf16[1024,256]{1,0:T(8,128)(2,1)}, u32[]{:S(2)}, u32[]{:S(2)}) collective-permute-start(bf16[1024,256]{1,0:T(8,128)(2,1)} %collective-permute-done.5.refs_10_), channel_id=1, source_target_pairs={{32,0},{33,1},{34,2},{35,3},{36,4},{37,5},{38,6},{39,7},{40,8},{41... | collective-permute-start | bytes 1572872 | tf_op jit(solution)/shard_map/ppermute | solution.py:27
  31.6 12.6 %collective-permute-start.10 = (bf16[1024,256]{1,0:T(8,128)(2,1)}, bf16[1024,256]{1,0:T(8,128)(2,1)}, u32[]{:S(2)}, u32[]{:S(2)}) collective-permute-start(bf16[1024,256]{1,0:T(8,128)(2,1)} %collective-permute-done.6.refs_15_), channel_id=1, source_target_pairs={{193,0},{0,1},{195,2},{2,3},{197,4},{4,5},{199,6},{6,7},{201,8},{8... | collective-permute-start | bytes 1572872 | tf_op jit(solution)/shard_map/ppermute | solution.py:27
  38.7 11.2 %collective-permute-start.13 = (bf16[1024,256]{1,0:T(8,128)(2,1)}, bf16[1024,256]{1,0:T(8,128)(2,1)}, u32[]{:S(2)}, u32[]{:S(2)}) collective-permute-start(bf16[1024,256]{1,0:T(8,128)(2,1)} %collective-permute-done.9.refs_11_), channel_id=1, source_target_pairs={{193,0},{0,1},{195,2},{2,3},{197,4},{4,5},{199,6},{6,7},{201,8},{8... | collective-permute-start | bytes 1572872 | tf_op jit(solution)/shard_map/ppermute | solution.py:27
  42.4 12.1 %collective-permute-start.17 = (bf16[1024,256]{1,0:T(8,128)(2,1)}, bf16[1024,256]{1,0:T(8,128)(2,1)}, u32[]{:S(2)}, u32[]{:S(2)}) collective-permute-start(bf16[1024,256]{1,0:T(8,128)(2,1)} %collective-permute-done.6.refs_15_), channel_id=1, source_target_pairs={{32,0},{33,1},{34,2},{35,3},{36,4},{37,5},{38,6},{39,7},{40,8},{41... | collective-permute-start | bytes 1572872 | tf_op jit(solution)/shard_map/ppermute | solution.py:27
  44.3 13.5 %collective-permute-start.15 = (bf16[1024,256]{1,0:T(8,128)(2,1)}, bf16[1024,256]{1,0:T(8,128)(2,1)}, u32[]{:S(2)}, u32[]{:S(2)}) collective-permute-start(bf16[1024,256]{1,0:T(8,128)(2,1)} %collective-permute-done.10.refs_16_), channel_id=1, source_target_pairs={{193,0},{0,1},{195,2},{2,3},{197,4},{4,5},{199,6},{6,7},{201,8},{8... | collective-permute-start | bytes 1572872 | tf_op jit(solution)/shard_map/ppermute | solution.py:27
  49.9 8.1 %collective-permute-start.18 = (bf16[1024,256]{1,0:T(8,128)(2,1)}, bf16[1024,256]{1,0:T(8,128)(2,1)}, u32[]{:S(2)}, u32[]{:S(2)}) collective-permute-start(bf16[1024,256]{1,0:T(8,128)(2,1)} %collective-permute-done.9.refs_11_), channel_id=1, source_target_pairs={{32,0},{33,1},{34,2},{35,3},{36,4},{37,5},{38,6},{39,7},{40,8},{41... | collective-permute-start | bytes 1572872 | tf_op jit(solution)/shard_map/ppermute | solution.py:27
  49.9 8.2 %collective-permute-start.19 = (bf16[1024,256]{1,0:T(8,128)(2,1)}, bf16[1024,256]{1,0:T(8,128)(2,1)}, u32[]{:S(2)}, u32[]{:S(2)}) collective-permute-start(bf16[1024,256]{1,0:T(8,128)(2,1)} %collective-permute-done.10.refs_16_), channel_id=1, source_target_pairs={{32,0},{33,1},{34,2},{35,3},{36,4},{37,5},{38,6},{39,7},{40,8},{41... | collective-permute-start | bytes 1572872 | tf_op jit(solution)/shard_map/ppermute | solution.py:27
  50.4 10.7 %collective-permute-start.14 = (bf16[1024,256]{1,0:T(8,128)(2,1)}, bf16[1024,256]{1,0:T(8,128)(2,1)}, u32[]{:S(2)}, u32[]{:S(2)}) collective-permute-start(bf16[1024,256]{1,0:T(8,128)(2,1)} %collective-permute-done.13.refs_12_), channel_id=1, source_target_pairs={{193,0},{0,1},{195,2},{2,3},{197,4},{4,5},{199,6},{6,7},{201,8},{8... | collective-permute-start | bytes 1572872 | tf_op jit(solution)/shard_map/ppermute | solution.py:27
  53.2 4.6 %copy-start.1 = (s32[64]{0:T(128)S(1)}, s32[64]{0:T(128)}, u32[]{:S(2)}) copy-start(s32[64]{0:T(128)} %owner_ref.1) | copy-start | bytes 772
  53.2 8.0 %copy-start.4 = (s32[16]{0:T(128)S(1)}, s32[16]{0:T(128)}, u32[]{:S(2)}) copy-start(s32[16]{0:T(128)} %constant.108.clone) | copy-start | bytes 196
  53.2 8.1 %copy-start.5 = (s32[16]{0:T(128)S(1)}, s32[16]{0:T(128)}, u32[]{:S(2)}) copy-start(s32[16]{0:T(128)} %constant.109.clone) | copy-start | bytes 196
  53.2 16.4 %copy-start = (bf16[1024,256]{1,0:T(8,128)(2,1)S(1)}, bf16[1024,256]{1,0:T(8,128)(2,1)}, u32[]{:S(2)}) copy-start(bf16[1024,256]{1,0:T(8,128)(2,1)} %refs_9_.1) | copy-start | bytes 1572868
  54.5 11.4 %collective-permute-start.11 = (bf16[2,320,512]{2,1,0:T(8,128)(2,1)S(1)}, bf16[2,320,512]{2,1,0:T(8,128)(2,1)S(1)}, u32[]{:S(2)}, u32[]{:S(2)}) collective-permute-start(bf16[2,320,512]{2,1,0:T(8,128)(2,1)S(1)} %slice.6), channel_id=1, source_target_pairs={{2,0},{3,1},{4,2},{5,3},{6,4},{7,5},{0,6},{1,7},{10,8},{11,9},{12,... | collective-permute-start | bytes 1966088 | tf_op jit(solution)/shard_map/ppermute | solution.py:27
  57.8 11.8 %collective-permute-start.12 = (bf16[2,320,512]{2,1,0:T(8,128)(2,1)S(1)}, bf16[2,320,512]{2,1,0:T(8,128)(2,1)S(1)}, u32[]{:S(2)}, u32[]{:S(2)}) collective-permute-start(bf16[2,320,512]{2,1,0:T(8,128)(2,1)S(1)} %slice.7), channel_id=1, source_target_pairs={{6,0},{7,1},{0,2},{1,3},{2,4},{3,5},{4,6},{5,7},{14,8},{15,9},{8,1... | collective-permute-start | bytes 1966088 | tf_op jit(solution)/shard_map/ppermute | solution.py:27
  58.0 3.3 %collective-permute-start.20 = (bf16[1024,256]{1,0:T(8,128)(2,1)}, bf16[1024,256]{1,0:T(8,128)(2,1)S(1)}, u32[]{:S(2)}, u32[]{:S(2)}) collective-permute-start(bf16[1024,256]{1,0:T(8,128)(2,1)} %collective-permute-done.13.refs_12_), channel_id=1, source_target_pairs={{32,0},{33,1},{34,2},{35,3},{36,4},{37,5},{38,6},{39,7},{40,8},{41... | collective-permute-start | bytes 1572872 | tf_op jit(solution)/shard_map/ppermute | solution.py:27
  58.1 3.2 %collective-permute-start.21 = (bf16[1024,256]{1,0:T(8,128)(2,1)}, bf16[1024,256]{1,0:T(8,128)(2,1)S(1)}, u32[]{:S(2)}, u32[]{:S(2)}) collective-permute-start(bf16[1024,256]{1,0:T(8,128)(2,1)} %collective-permute-done.15.refs_17_), channel_id=1, source_target_pairs={{32,0},{33,1},{34,2},{35,3},{36,4},{37,5},{38,6},{39,7},{40,8},{41... | collective-permute-start | bytes 1572872 | tf_op jit(solution)/shard_map/ppermute | solution.py:27
  61.1 8.5 %collective-permute-start.22 = (bf16[1024,256]{1,0:T(8,128)(2,1)}, bf16[1024,256]{1,0:T(8,128)(2,1)S(1)}, u32[]{:S(2)}, u32[]{:S(2)}) collective-permute-start(bf16[1024,256]{1,0:T(8,128)(2,1)} %collective-permute-done.14.refs_13_), channel_id=1, source_target_pairs={{32,0},{33,1},{34,2},{35,3},{36,4},{37,5},{38,6},{39,7},{40,8},{41... | collective-permute-start | bytes 1572872 | tf_op jit(solution)/shard_map/ppermute | solution.py:27
  92.9 16.5 %copy-start.2 = (bf16[640,256]{1,0:T(8,128)(2,1)S(1)}, bf16[640,256]{1,0:T(8,128)(2,1)}, u32[]{:S(2)}) copy-start(bf16[640,256]{1,0:T(8,128)(2,1)} %param.10) | copy-start | bytes 983044
  92.9 16.5 %copy-start.3 = (f32[640]{0:T(1024)S(1)}, f32[640]{0:T(1024)}, u32[]{:S(2)}) copy-start(f32[640]{0:T(1024)} %param.14) | copy-start | bytes 7684
  94.6 14.7 %all-to-all-start.1 = ((bf16[32,20,256]{2,1,0:T(8,128)(2,1)}), bf16[32,20,256]{2,1,0:T(8,128)(2,1)S(1)}, u32[]{:S(2)}, u32[]{:S(2)}) async-start(bf16[32,20,256]{2,1,0:T(8,128)(2,1)} %reorder.1), calls=%async_computation.1 | async-start | bytes 786432 | tf_op jit(solution)/shard_map/all_to_all | solution.py:218

commit v8 on v7

--- a/solution.py
+++ b/solution.py
@@ -69,7 +69,7 @@
     ahead, behind = major(block, 1), major(block, 3)
     advance()
     advance()
-    ahead, behind, first[2], second[2] = tie(ahead, behind, first[2], second[2])
+    ahead, first[2], second[2] = tie(ahead, first[2], second[2])
     far = [major(ahead[:2], 1), major(behind[2:], 3)]
     advance()
     return [block, ahead, behind] + far, first + second + flips
@@ -110,22 +110,19 @@
     def _(g):
         pltpu.make_async_copy(panels[0], held.at[g], sems.at[g]).wait()
         part, first = part_ref[g], first_ref[g]
-        for j in range(width // TILE):
-            left = []
-            for r in range(per):
-                at = place_ref[first + r]
-                column = pl.ds(pl.multiple_of(lax.rem(at, wide) * TILE, TILE), TILE)
-                strips = []
+        for r in range(per):
+            at = place_ref[first + r]
+            column = pl.ds(pl.multiple_of(lax.rem(at, wide) * TILE, TILE), TILE)
+            found = jnp.dot(
+                left_ref[at // wide, :, column],
+                held[g, r * TILE : (r + 1) * TILE, :],
+                preferred_element_type=jnp.float32,
+            )
+            for j in range(width // TILE):
                 for b in range(rows // PBLK):
                     mark = screen_ref[(b * tiles + first + r) * across + part * (width // TILE) + j]
-                    strip = left_ref[at // wide, b * PBLK : (b + 1) * PBLK, column]
-                    strips.append(strip * jnp.full((PBLK, TILE), mark, jnp.float32).astype(strip.dtype))
-                left.append(jnp.concatenate(strips, axis=0))
-            total[part, j] += jnp.dot(
-                jnp.concatenate(left, axis=1),
-                held[g, :, j * TILE : (j + 1) * TILE],
-                preferred_element_type=jnp.float32,
-            )
+                    strip = slice(b * PBLK, (b + 1) * PBLK)
+                    total[part, j, strip, :] += mark * found[strip, j * TILE : (j + 1) * TILE]
 
     chunks, piece, _ = out_ref.shape
     for i in range(total.shape[0] * total.shape[1]):

time: 111 us -> 110 us (level)
  no operation moved by 1% of the time
where the time goes in v8:
time: 110 us
  waiting for transfers between devices  44.8 us (41%)
  starting transfers between devices  32.4 us (29%)
  blocking collectives  12.5 us (11%)
  Pallas kernels  12.1 us (11%)
  local copies, waits for them, and re-layouts  4 us (4%)
  other arithmetic  2.59 us (2%)
  between operations  1.56 us (1%)
    ppermute x23, waiting for transfers between devices, send(): return lax.ppermute(value, AXES, pairs)  37.9 us
    ppermute x23, starting transfers between devices, send(): return lax.ppermute(value, AXES, pairs)  27.3 us
    all_to_all x1, blocking collectives, local(): spread = lax.all_to_all(found, ('x', 'y'), 0, 0, tiled=True)  12.5 us
    pallas_call x1, Pallas kernels, ladder(): pl.pallas_call(functools.partial(ladder_kernel, count), out_shape=jax.Sha...  10.4 us
    all_to_all x1, waiting for transfers between devices, local(): total = lax.all_to_all(sent, ('zl', 'x', 'y'), 0, 0, tiled=True)  6.9 us
    all_to_all x1, starting transfers between devices, local(): total = lax.all_to_all(sent, ('zl', 'x', 'y'), 0, 0, tiled=True)  5.1 us
  transfers between devices with their start and end apart: 24, of which 11 were waited for; matrix products, arithmetic and copies ran while one was open for 5% of the time, Pallas kernels for 0%

profile of v8, /device:TPU:64, one launch (start us, length us, event | category | flops | bytes accessed | tf_op | source)
XLA Modules:
  0.0 109.8 jit_solution(9362167884837562559)
XLA Ops:
  0.0 1.0 constant_dynamic-slice_fusion.1
  1.0 2.0 %collective-permute-start = (bf16[320,256]{1,0:T(8,128)(2,1)S(1)}, bf16[320,256]{1,0:T(8,128)(2,1)S(1)}, u32[]{:S(2)}, u32[]{:S(2)}) collective-permute-start(bf16[320,256]{1,0:T(8,128)(2,1)S(1)} %get-tuple-element.24), channel_id=1, source_target_pairs={{1,0},{0,1},{3,2},{2,3},{5,4},{4,5},{7,6},{6,7},{9,8},{8,9},{11,10... | collective-permute-start | bytes 491528 | tf_op jit(solution)/shard_map/ppermute | solution.py:27
  3.1 5.0 %collective-permute-done = bf16[320,256]{1,0:T(8,128)(2,1)S(1)} collective-permute-done((bf16[320,256]{1,0:T(8,128)(2,1)S(1)}, bf16[320,256]{1,0:T(8,128)(2,1)S(1)}, u32[]{:S(2)}, u32[]{:S(2)}) %collective-permute-start) | collective-permute-done | bytes 163872 | tf_op jit(solution)/shard_map/ppermute | solution.py:27
  8.2 1.6 %collective-permute-start.6 = (bf16[1024,256]{1,0:T(8,128)(2,1)S(1)}, bf16[1024,256]{1,0:T(8,128)(2,1)}, u32[]{:S(2)}, u32[]{:S(2)}) collective-permute-start(bf16[1024,256]{1,0:T(8,128)(2,1)S(1)} %collective-permute-done.1.refs_14_), channel_id=1, source_target_pairs={{193,0},{0,1},{195,2},{2,3},{197,4},{4,5},{199,6},{6,7},{201,8},{8... | collective-permute-start | bytes 1572872 | tf_op jit(solution)/shard_map/ppermute | solution.py:27
  9.8 2.8 %collective-permute-start.2 = (bf16[320,512]{1,0:T(8,128)(2,1)S(1)}, bf16[320,512]{1,0:T(8,128)(2,1)S(1)}, u32[]{:S(2)}, u32[]{:S(2)}) collective-permute-start(bf16[320,512]{1,0:T(8,128)(2,1)S(1)} %pad_maximum_fusion.1), channel_id=1, source_target_pairs={{8,0},{9,1},{10,2},{11,3},{12,4},{13,5},{14,6},{15,7},{16,8},{17,9... | collective-permute-start | bytes 983048 | tf_op jit(solution)/shard_map/ppermute | solution.py:27
  12.5 0.8 collective-permute-start.3
  13.3 0.9 collective-permute-start.4
  14.2 6.5 %collective-permute-done.2 = bf16[320,512]{1,0:T(8,128)(2,1)S(1)} collective-permute-done((bf16[320,512]{1,0:T(8,128)(2,1)S(1)}, bf16[320,512]{1,0:T(8,128)(2,1)S(1)}, u32[]{:S(2)}, u32[]{:S(2)}) %collective-permute-start.2) | collective-permute-done | bytes 327712 | tf_op jit(solution)/shard_map/ppermute | solution.py:27
  20.7 0.5 collective-permute-done.3
  21.2 3.4 %collective-permute-done.4 = bf16[320,512]{1,0:T(8,128)(2,1)S(1)} collective-permute-done((bf16[320,512]{1,0:T(8,128)(2,1)S(1)}, bf16[320,512]{1,0:T(8,128)(2,1)S(1)}, u32[]{:S(2)}, u32[]{:S(2)}) %collective-permute-start.4) | collective-permute-done | bytes 327712 | tf_op jit(solution)/shard_map/ppermute | solution.py:27
  24.8 3.1 %collective-permute-start.7 = (bf16[4,320,512]{2,1,0:T(8,128)(2,1)S(1)}, bf16[4,320,512]{2,1,0:T(8,128)(2,1)S(1)}, u32[]{:S(2)}, u32[]{:S(2)}) collective-permute-start(bf16[4,320,512]{2,1,0:T(8,128)(2,1)S(1)} %pad_maximum_fusion.refs_4_), channel_id=1, source_target_pairs={{2,0},{3,1},{4,2},{5,3},{6,4},{7,5},{0,6},{1,7},{10,8},{11,9},{12,... | collective-permute-start | bytes 3932168 | tf_op jit(solution)/shard_map/ppermute | solution.py:27
  27.9 3.7 %collective-permute-start.8 = (bf16[1024,256]{1,0:T(8,128)(2,1)}, bf16[1024,256]{1,0:T(8,128)(2,1)}, u32[]{:S(2)}, u32[]{:S(2)}) collective-permute-start(bf16[1024,256]{1,0:T(8,128)(2,1)} %collective-permute-done.5.refs_10_), channel_id=1, source_target_pairs={{193,0},{0,1},{195,2},{2,3},{197,4},{4,5},{199,6},{6,7},{201,8},{8... | collective-permute-start | bytes 1572872 | tf_op jit(solution)/shard_map/ppermute | solution.py:27
  32.0 6.6 %collective-permute-done.8.refs_11_ = bf16[1024,256]{1,0:T(8,128)(2,1)} collective-permute-done((bf16[1024,256]{1,0:T(8,128)(2,1)}, bf16[1024,256]{1,0:T(8,128)(2,1)}, u32[]{:S(2)}, u32[]{:S(2)}) %collective-permute-start.8) | collective-permute-done | bytes 524320 | tf_op jit(solution)/shard_map/ppermute | solution.py:27
  38.7 2.5 %collective-permute-start.13 = (bf16[1024,256]{1,0:T(8,128)(2,1)}, bf16[1024,256]{1,0:T(8,128)(2,1)}, u32[]{:S(2)}, u32[]{:S(2)}) collective-permute-start(bf16[1024,256]{1,0:T(8,128)(2,1)} %collective-permute-done.8.refs_11_), channel_id=1, source_target_pairs={{193,0},{0,1},{195,2},{2,3},{197,4},{4,5},{199,6},{6,7},{201,8},{8... | collective-permute-start | bytes 1572872 | tf_op jit(solution)/shard_map/ppermute | solution.py:27
  41.1 1.0 dynamic-slice_convert_fusion
  42.5 1.8 %collective-permute-done.9.refs_16_ = bf16[1024,256]{1,0:T(8,128)(2,1)} collective-permute-done((bf16[1024,256]{1,0:T(8,128)(2,1)}, bf16[1024,256]{1,0:T(8,128)(2,1)}, u32[]{:S(2)}, u32[]{:S(2)}) %collective-permute-start.9) | collective-permute-done | bytes 524320 | tf_op jit(solution)/shard_map/ppermute | solution.py:27
  44.3 2.5 %collective-permute-start.15 = (bf16[1024,256]{1,0:T(8,128)(2,1)}, bf16[1024,256]{1,0:T(8,128)(2,1)}, u32[]{:S(2)}, u32[]{:S(2)}) collective-permute-start(bf16[1024,256]{1,0:T(8,128)(2,1)} %collective-permute-done.9.refs_16_), channel_id=1, source_target_pairs={{193,0},{0,1},{195,2},{2,3},{197,4},{4,5},{199,6},{6,7},{201,8},{8... | collective-permute-start | bytes 1572872 | tf_op jit(solution)/shard_map/ppermute | solution.py:27
  46.8 3.1 %collective-permute-done.13.refs_12_ = bf16[1024,256]{1,0:T(8,128)(2,1)} collective-permute-done((bf16[1024,256]{1,0:T(8,128)(2,1)}, bf16[1024,256]{1,0:T(8,128)(2,1)}, u32[]{:S(2)}, u32[]{:S(2)}) %collective-permute-start.13) | collective-permute-done | bytes 524320 | tf_op jit(solution)/shard_map/ppermute | solution.py:27
  50.4 2.5 %collective-permute-start.14 = (bf16[1024,256]{1,0:T(8,128)(2,1)}, bf16[1024,256]{1,0:T(8,128)(2,1)}, u32[]{:S(2)}, u32[]{:S(2)}) collective-permute-start(bf16[1024,256]{1,0:T(8,128)(2,1)} %collective-permute-done.13.refs_12_), channel_id=1, source_target_pairs={{193,0},{0,1},{195,2},{2,3},{197,4},{4,5},{199,6},{6,7},{201,8},{8... | collective-permute-start | bytes 1572872 | tf_op jit(solution)/shard_map/ppermute | solution.py:27
  53.3 1.2 %slice.8 = bf16[2,320,512]{2,1,0:T(8,128)(2,1)S(1)} slice(bf16[4,320,512]{2,1,0:T(8,128)(2,1)} %collective-permute-done.10.refs_6_), slice={[2:4], [0:320], [0:512]} | slice | bytes 1310720 | tf_op jit(solution)/shard_map/slice | solution.py:73
  54.5 3.3 %collective-permute-start.11 = (bf16[2,320,512]{2,1,0:T(8,128)(2,1)S(1)}, bf16[2,320,512]{2,1,0:T(8,128)(2,1)S(1)}, u32[]{:S(2)}, u32[]{:S(2)}) collective-permute-start(bf16[2,320,512]{2,1,0:T(8,128)(2,1)S(1)} %slice.6), channel_id=1, source_target_pairs={{2,0},{3,1},{4,2},{5,3},{6,4},{7,5},{0,6},{1,7},{10,8},{11,9},{12,... | collective-permute-start | bytes 1966088 | tf_op jit(solution)/shard_map/ppermute | solution.py:27
  58.6 2.5 %collective-permute-done.14.refs_13_ = bf16[1024,256]{1,0:T(8,128)(2,1)} collective-permute-done((bf16[1024,256]{1,0:T(8,128)(2,1)}, bf16[1024,256]{1,0:T(8,128)(2,1)}, u32[]{:S(2)}, u32[]{:S(2)}) %collective-permute-start.14) | collective-permute-done | bytes 524320 | tf_op jit(solution)/shard_map/ppermute | solution.py:27
  61.3 4.6 %collective-permute-done.11.refs_7_ = bf16[2,320,512]{2,1,0:T(8,128)(2,1)S(1)} collective-permute-done((bf16[2,320,512]{2,1,0:T(8,128)(2,1)S(1)}, bf16[2,320,512]{2,1,0:T(8,128)(2,1)S(1)}, u32[]{:S(2)}, u32[]{:S(2)}) %collective-permute-start.11) | collective-permute-done | bytes 655392 | tf_op jit(solution)/shard_map/ppermute | solution.py:27
  65.9 3.7 %collective-permute-done.12.refs_8_ = bf16[2,320,512]{2,1,0:T(8,128)(2,1)S(1)} collective-permute-done((bf16[2,320,512]{2,1,0:T(8,128)(2,1)S(1)}, bf16[2,320,512]{2,1,0:T(8,128)(2,1)S(1)}, u32[]{:S(2)}, u32[]{:S(2)}) %collective-permute-start.12) | collective-permute-done | bytes 655392 | tf_op jit(solution)/shard_map/ppermute | solution.py:27
  69.6 10.4 %ladder.1 = bf16[16,20,512]{2,1,0:T(8,128)(2,1)S(1)} custom-call(s32[16]{0:T(128)S(1)} %add_multiply_fusion.1.refs_0_, s32[16]{0:T(128)S(1)} %get-tuple-element.21.refs_1_, s32[64]{0:T(128)S(1)} %select_reduce_fusion.refs_2_, f32[1280]{0:T(1024)S(1)} %reshape.63.refs_3_, bf16[4,320,512]{2,1,0:T(8,128)(2,1)S(1)} %pad_maximum_fusion.refs_4_, ...), custom_call_target="tpu_custom_call" | custom-call | flops 2684354560 | bytes 18874368 | tf_op jit(solution)/shard_map/ladder/pallas_call | solution.py:139
  80.0 12.5 %all_to_all.10.src_ref = bf16[16,20,512]{2,1,0:T(8,128)(2,1)S(1)} all-to-all(bf16[16,20,512]{2,1,0:T(8,128)(2,1)S(1)} %ladder.1), channel_id=1, replica_groups=mesh['zh'=4,'core'=2,'x'=4,'y'=4,'zl'=2] {'x','y'}, dimensions={0} | all-to-all | bytes 655360 | tf_op jit(solution)/shard_map/all_to_all | solution.py:213
  92.4 1.7 %reorder.1 = bf16[32,20,256]{2,1,0:T(8,128)(2,1)} custom-call(s32[64]{0:T(128)S(1)} %copy-done.1, bf16[16,20,512]{2,1,0:T(8,128)(2,1)S(1)} %all_to_all.10.src_ref), custom_call_target="tpu_custom_call" | custom-call | bytes 1048576 | tf_op jit(solution)/shard_map/reorder/pallas_call | solution.py:172
  94.2 5.1 %all-to-all-start.1 = ((bf16[32,20,256]{2,1,0:T(8,128)(2,1)}), bf16[32,20,256]{2,1,0:T(8,128)(2,1)S(1)}, u32[]{:S(2)}, u32[]{:S(2)}) async-start(bf16[32,20,256]{2,1,0:T(8,128)(2,1)} %reorder.1), calls=%async_computation.1 | async-start | bytes 786432 | tf_op jit(solution)/shard_map/all_to_all | solution.py:215
  99.3 0.6 fusion.9
  101.2 0.8 fusion.8
  102.0 6.9 %all-to-all-done.1 = bf16[32,20,256]{2,1,0:T(8,128)(2,1)S(1)} async-done(((bf16[32,20,256]{2,1,0:T(8,128)(2,1)}), bf16[32,20,256]{2,1,0:T(8,128)(2,1)S(1)}, u32[]{:S(2)}, u32[]{:S(2)}) %all-to-all-start.1) | async-done | bytes 327712 | tf_op jit(solution)/shard_map/all_to_all | solution.py:215
  108.9 0.9 add_convert_fusion
  (56 shorter events, 2.8 us)
Async XLA Ops:
  0.0 8.2 %collective-permute-start.1 = (bf16[1024,256]{1,0:T(8,128)(2,1)}, bf16[1024,256]{1,0:T(8,128)(2,1)S(1)}, u32[]{:S(2)}, u32[]{:S(2)}) collective-permute-start(bf16[1024,256]{1,0:T(8,128)(2,1)} %refs_9_.1), channel_id=1, source_target_pairs={{32,0},{33,1},{34,2},{35,3},{36,4},{37,5},{38,6},{39,7},{40,8},{41... | collective-permute-start | bytes 1572872 | tf_op jit(solution)/shard_map/ppermute | solution.py:27
  1.0 7.2 %collective-permute-start = (bf16[320,256]{1,0:T(8,128)(2,1)S(1)}, bf16[320,256]{1,0:T(8,128)(2,1)S(1)}, u32[]{:S(2)}, u32[]{:S(2)}) collective-permute-start(bf16[320,256]{1,0:T(8,128)(2,1)S(1)} %get-tuple-element.24), channel_id=1, source_target_pairs={{1,0},{0,1},{3,2},{2,3},{5,4},{4,5},{7,6},{6,7},{9,8},{8,9},{11,10... | collective-permute-start | bytes 491528 | tf_op jit(solution)/shard_map/ppermute | solution.py:27
  3.0 21.8 %collective-permute-start.5 = (bf16[1024,256]{1,0:T(8,128)(2,1)}, bf16[1024,256]{1,0:T(8,128)(2,1)}, u32[]{:S(2)}, u32[]{:S(2)}) collective-permute-start(bf16[1024,256]{1,0:T(8,128)(2,1)} %refs_9_.1), channel_id=1, source_target_pairs={{193,0},{0,1},{195,2},{2,3},{197,4},{4,5},{199,6},{6,7},{201,8},{8... | collective-permute-start | bytes 1572872 | tf_op jit(solution)/shard_map/ppermute | solution.py:27
  8.2 16.6 %collective-permute-start.6 = (bf16[1024,256]{1,0:T(8,128)(2,1)S(1)}, bf16[1024,256]{1,0:T(8,128)(2,1)}, u32[]{:S(2)}, u32[]{:S(2)}) collective-permute-start(bf16[1024,256]{1,0:T(8,128)(2,1)S(1)} %collective-permute-done.1.refs_14_), channel_id=1, source_target_pairs={{193,0},{0,1},{195,2},{2,3},{197,4},{4,5},{199,6},{6,7},{201,8},{8... | collective-permute-start | bytes 1572872 | tf_op jit(solution)/shard_map/ppermute | solution.py:27
  9.8 10.9 %collective-permute-start.2 = (bf16[320,512]{1,0:T(8,128)(2,1)S(1)}, bf16[320,512]{1,0:T(8,128)(2,1)S(1)}, u32[]{:S(2)}, u32[]{:S(2)}) collective-permute-start(bf16[320,512]{1,0:T(8,128)(2,1)S(1)} %pad_maximum_fusion.1), channel_id=1, source_target_pairs={{8,0},{9,1},{10,2},{11,3},{12,4},{13,5},{14,6},{15,7},{16,8},{17,9... | collective-permute-start | bytes 983048 | tf_op jit(solution)/shard_map/ppermute | solution.py:27
  12.5 8.7 %collective-permute-start.3 = (bf16[320,512]{1,0:T(8,128)(2,1)S(1)}, bf16[320,512]{1,0:T(8,128)(2,1)S(1)}, u32[]{:S(2)}, u32[]{:S(2)}) collective-permute-start(bf16[320,512]{1,0:T(8,128)(2,1)S(1)} %pad_maximum_fusion.1), channel_id=1, source_target_pairs={{16,0},{17,1},{18,2},{19,3},{20,4},{21,5},{22,6},{23,7},{24,8},{25... | collective-permute-start | bytes 983048 | tf_op jit(solution)/shard_map/ppermute | solution.py:27
  13.3 11.3 %collective-permute-start.4 = (bf16[320,512]{1,0:T(8,128)(2,1)S(1)}, bf16[320,512]{1,0:T(8,128)(2,1)S(1)}, u32[]{:S(2)}, u32[]{:S(2)}) collective-permute-start(bf16[320,512]{1,0:T(8,128)(2,1)S(1)} %pad_maximum_fusion.1), channel_id=1, source_target_pairs={{24,0},{25,1},{26,2},{27,3},{28,4},{29,5},{30,6},{31,7},{0,8},{1,9... | collective-permute-start | bytes 983048 | tf_op jit(solution)/shard_map/ppermute | solution.py:27
  24.6 17.7 %copy-start.6 = (s32[16]{0:T(128)S(1)}, s32[16]{0:T(128)}, u32[]{:S(2)}) copy-start(s32[16]{0:T(128)} %constant.106.clone) | copy-start | bytes 196
  24.6 17.7 %copy-start.7 = (s32[16]{0:T(128)S(1)}, s32[16]{0:T(128)}, u32[]{:S(2)}) copy-start(s32[16]{0:T(128)} %constant.107.clone) | copy-start | bytes 196
  24.8 25.1 %collective-permute-start.7 = (bf16[4,320,512]{2,1,0:T(8,128)(2,1)S(1)}, bf16[4,320,512]{2,1,0:T(8,128)(2,1)S(1)}, u32[]{:S(2)}, u32[]{:S(2)}) collective-permute-start(bf16[4,320,512]{2,1,0:T(8,128)(2,1)S(1)} %pad_maximum_fusion.refs_4_), channel_id=1, source_target_pairs={{2,0},{3,1},{4,2},{5,3},{6,4},{7,5},{0,6},{1,7},{10,8},{11,9},{12,... | collective-permute-start | bytes 3932168 | tf_op jit(solution)/shard_map/ppermute | solution.py:27
  27.9 22.5 %collective-permute-start.10 = (bf16[4,320,512]{2,1,0:T(8,128)(2,1)S(1)}, bf16[4,320,512]{2,1,0:T(8,128)(2,1)}, u32[]{:S(2)}, u32[]{:S(2)}) collective-permute-start(bf16[4,320,512]{2,1,0:T(8,128)(2,1)S(1)} %pad_maximum_fusion.refs_4_), channel_id=1, source_target_pairs={{6,0},{7,1},{0,2},{1,3},{2,4},{3,5},{4,6},{5,7},{14,8},{15,9},{8,1... | collective-permute-start | bytes 3932168 | tf_op jit(solution)/shard_map/ppermute | solution.py:27
  27.9 10.7 %collective-permute-start.8 = (bf16[1024,256]{1,0:T(8,128)(2,1)}, bf16[1024,256]{1,0:T(8,128)(2,1)}, u32[]{:S(2)}, u32[]{:S(2)}) collective-permute-start(bf16[1024,256]{1,0:T(8,128)(2,1)} %collective-permute-done.5.refs_10_), channel_id=1, source_target_pairs={{193,0},{0,1},{195,2},{2,3},{197,4},{4,5},{199,6},{6,7},{201,8},{8... | collective-permute-start | bytes 1572872 | tf_op jit(solution)/shard_map/ppermute | solution.py:27
  31.6 10.7 %collective-permute-start.16 = (bf16[1024,256]{1,0:T(8,128)(2,1)}, bf16[1024,256]{1,0:T(8,128)(2,1)}, u32[]{:S(2)}, u32[]{:S(2)}) collective-permute-start(bf16[1024,256]{1,0:T(8,128)(2,1)} %collective-permute-done.5.refs_10_), channel_id=1, source_target_pairs={{32,0},{33,1},{34,2},{35,3},{36,4},{37,5},{38,6},{39,7},{40,8},{41... | collective-permute-start | bytes 1572872 | tf_op jit(solution)/shard_map/ppermute | solution.py:27
  31.6 12.6 %collective-permute-start.9 = (bf16[1024,256]{1,0:T(8,128)(2,1)}, bf16[1024,256]{1,0:T(8,128)(2,1)}, u32[]{:S(2)}, u32[]{:S(2)}) collective-permute-start(bf16[1024,256]{1,0:T(8,128)(2,1)} %collective-permute-done.6.refs_15_), channel_id=1, source_target_pairs={{193,0},{0,1},{195,2},{2,3},{197,4},{4,5},{199,6},{6,7},{201,8},{8... | collective-permute-start | bytes 1572872 | tf_op jit(solution)/shard_map/ppermute | solution.py:27
  38.7 11.2 %collective-permute-start.13 = (bf16[1024,256]{1,0:T(8,128)(2,1)}, bf16[1024,256]{1,0:T(8,128)(2,1)}, u32[]{:S(2)}, u32[]{:S(2)}) collective-permute-start(bf16[1024,256]{1,0:T(8,128)(2,1)} %collective-permute-done.8.refs_11_), channel_id=1, source_target_pairs={{193,0},{0,1},{195,2},{2,3},{197,4},{4,5},{199,6},{6,7},{201,8},{8... | collective-permute-start | bytes 1572872 | tf_op jit(solution)/shard_map/ppermute | solution.py:27
  42.4 12.1 %collective-permute-start.17 = (bf16[1024,256]{1,0:T(8,128)(2,1)}, bf16[1024,256]{1,0:T(8,128)(2,1)}, u32[]{:S(2)}, u32[]{:S(2)}) collective-permute-start(bf16[1024,256]{1,0:T(8,128)(2,1)} %collective-permute-done.6.refs_15_), channel_id=1, source_target_pairs={{32,0},{33,1},{34,2},{35,3},{36,4},{37,5},{38,6},{39,7},{40,8},{41... | collective-permute-start | bytes 1572872 | tf_op jit(solution)/shard_map/ppermute | solution.py:27
  44.3 13.5 %collective-permute-start.15 = (bf16[1024,256]{1,0:T(8,128)(2,1)}, bf16[1024,256]{1,0:T(8,128)(2,1)}, u32[]{:S(2)}, u32[]{:S(2)}) collective-permute-start(bf16[1024,256]{1,0:T(8,128)(2,1)} %collective-permute-done.9.refs_16_), channel_id=1, source_target_pairs={{193,0},{0,1},{195,2},{2,3},{197,4},{4,5},{199,6},{6,7},{201,8},{8... | collective-permute-start | bytes 1572872 | tf_op jit(solution)/shard_map/ppermute | solution.py:27
  49.9 8.1 %collective-permute-start.18 = (bf16[1024,256]{1,0:T(8,128)(2,1)}, bf16[1024,256]{1,0:T(8,128)(2,1)}, u32[]{:S(2)}, u32[]{:S(2)}) collective-permute-start(bf16[1024,256]{1,0:T(8,128)(2,1)} %collective-permute-done.8.refs_11_), channel_id=1, source_target_pairs={{32,0},{33,1},{34,2},{35,3},{36,4},{37,5},{38,6},{39,7},{40,8},{41... | collective-permute-start | bytes 1572872 | tf_op jit(solution)/shard_map/ppermute | solution.py:27
  49.9 8.2 %collective-permute-start.19 = (bf16[1024,256]{1,0:T(8,128)(2,1)}, bf16[1024,256]{1,0:T(8,128)(2,1)}, u32[]{:S(2)}, u32[]{:S(2)}) collective-permute-start(bf16[1024,256]{1,0:T(8,128)(2,1)} %collective-permute-done.9.refs_16_), channel_id=1, source_target_pairs={{32,0},{33,1},{34,2},{35,3},{36,4},{37,5},{38,6},{39,7},{40,8},{41... | collective-permute-start | bytes 1572872 | tf_op jit(solution)/shard_map/ppermute | solution.py:27
  50.4 10.7 %collective-permute-start.14 = (bf16[1024,256]{1,0:T(8,128)(2,1)}, bf16[1024,256]{1,0:T(8,128)(2,1)}, u32[]{:S(2)}, u32[]{:S(2)}) collective-permute-start(bf16[1024,256]{1,0:T(8,128)(2,1)} %collective-permute-done.13.refs_12_), channel_id=1, source_target_pairs={{193,0},{0,1},{195,2},{2,3},{197,4},{4,5},{199,6},{6,7},{201,8},{8... | collective-permute-start | bytes 1572872 | tf_op jit(solution)/shard_map/ppermute | solution.py:27
  53.2 4.6 %copy-start.1 = (s32[64]{0:T(128)S(1)}, s32[64]{0:T(128)}, u32[]{:S(2)}) copy-start(s32[64]{0:T(128)} %owner_ref.1) | copy-start | bytes 772
  53.2 8.0 %copy-start.4 = (s32[16]{0:T(128)S(1)}, s32[16]{0:T(128)}, u32[]{:S(2)}) copy-start(s32[16]{0:T(128)} %constant.108.clone) | copy-start | bytes 196
  53.2 8.1 %copy-start.5 = (s32[16]{0:T(128)S(1)}, s32[16]{0:T(128)}, u32[]{:S(2)}) copy-start(s32[16]{0:T(128)} %constant.109.clone) | copy-start | bytes 196
  53.2 16.4 %copy-start = (bf16[1024,256]{1,0:T(8,128)(2,1)S(1)}, bf16[1024,256]{1,0:T(8,128)(2,1)}, u32[]{:S(2)}) copy-start(bf16[1024,256]{1,0:T(8,128)(2,1)} %refs_9_.1) | copy-start | bytes 1572868
  54.5 11.4 %collective-permute-start.11 = (bf16[2,320,512]{2,1,0:T(8,128)(2,1)S(1)}, bf16[2,320,512]{2,1,0:T(8,128)(2,1)S(1)}, u32[]{:S(2)}, u32[]{:S(2)}) collective-permute-start(bf16[2,320,512]{2,1,0:T(8,128)(2,1)S(1)} %slice.6), channel_id=1, source_target_pairs={{2,0},{3,1},{4,2},{5,3},{6,4},{7,5},{0,6},{1,7},{10,8},{11,9},{12,... | collective-permute-start | bytes 1966088 | tf_op jit(solution)/shard_map/ppermute | solution.py:27
  57.8 11.8 %collective-permute-start.12 = (bf16[2,320,512]{2,1,0:T(8,128)(2,1)S(1)}, bf16[2,320,512]{2,1,0:T(8,128)(2,1)S(1)}, u32[]{:S(2)}, u32[]{:S(2)}) collective-permute-start(bf16[2,320,512]{2,1,0:T(8,128)(2,1)S(1)} %slice.8), channel_id=1, source_target_pairs={{6,0},{7,1},{0,2},{1,3},{2,4},{3,5},{4,6},{5,7},{14,8},{15,9},{8,1... | collective-permute-start | bytes 1966088 | tf_op jit(solution)/shard_map/ppermute | solution.py:27
  58.0 3.3 %collective-permute-start.20 = (bf16[1024,256]{1,0:T(8,128)(2,1)}, bf16[1024,256]{1,0:T(8,128)(2,1)S(1)}, u32[]{:S(2)}, u32[]{:S(2)}) collective-permute-start(bf16[1024,256]{1,0:T(8,128)(2,1)} %collective-permute-done.13.refs_12_), channel_id=1, source_target_pairs={{32,0},{33,1},{34,2},{35,3},{36,4},{37,5},{38,6},{39,7},{40,8},{41... | collective-permute-start | bytes 1572872 | tf_op jit(solution)/shard_map/ppermute | solution.py:27
  58.1 3.2 %collective-permute-start.21 = (bf16[1024,256]{1,0:T(8,128)(2,1)}, bf16[1024,256]{1,0:T(8,128)(2,1)S(1)}, u32[]{:S(2)}, u32[]{:S(2)}) collective-permute-start(bf16[1024,256]{1,0:T(8,128)(2,1)} %collective-permute-done.15.refs_17_), channel_id=1, source_target_pairs={{32,0},{33,1},{34,2},{35,3},{36,4},{37,5},{38,6},{39,7},{40,8},{41... | collective-permute-start | bytes 1572872 | tf_op jit(solution)/shard_map/ppermute | solution.py:27
  61.1 8.5 %collective-permute-start.22 = (bf16[1024,256]{1,0:T(8,128)(2,1)}, bf16[1024,256]{1,0:T(8,128)(2,1)S(1)}, u32[]{:S(2)}, u32[]{:S(2)}) collective-permute-start(bf16[1024,256]{1,0:T(8,128)(2,1)} %collective-permute-done.14.refs_13_), channel_id=1, source_target_pairs={{32,0},{33,1},{34,2},{35,3},{36,4},{37,5},{38,6},{39,7},{40,8},{41... | collective-permute-start | bytes 1572872 | tf_op jit(solution)/shard_map/ppermute | solution.py:27
  92.4 16.5 %copy-start.2 = (bf16[640,256]{1,0:T(8,128)(2,1)S(1)}, bf16[640,256]{1,0:T(8,128)(2,1)}, u32[]{:S(2)}) copy-start(bf16[640,256]{1,0:T(8,128)(2,1)} %param.10) | copy-start | bytes 983044
  92.4 16.5 %copy-start.3 = (f32[640]{0:T(1024)S(1)}, f32[640]{0:T(1024)}, u32[]{:S(2)}) copy-start(f32[640]{0:T(1024)} %param.14) | copy-start | bytes 7684
  94.2 14.7 %all-to-all-start.1 = ((bf16[32,20,256]{2,1,0:T(8,128)(2,1)}), bf16[32,20,256]{2,1,0:T(8,128)(2,1)S(1)}, u32[]{:S(2)}, u32[]{:S(2)}) async-start(bf16[32,20,256]{2,1,0:T(8,128)(2,1)} %reorder.1), calls=%async_computation.1 | async-start | bytes 786432 | tf_op jit(solution)/shard_map/all_to_all | solution.py:215
